TPU v7x, 32 devices: a whole 2x2x4 slice. The times are simulated.
32 devices in a mesh: rep: 8 (over z, x), shard: 4 (over y, core).
Axes of the slice: x: 2, y: 2, z: 4, core: 2. Of those that a mesh axis runs over, the one named last changes fastest.
Arguments:
- tokens: bfloat16 [32768, 1024], P(('rep', 'shard')), may hold values from -6 to 6
- segment_ids: int32 [32, 1024], P(('rep', 'shard')), may hold values from 0 to 3, never falling along the last dimension, each value on 1 to 800 neighbouring positions
- norm_gain_one: bfloat16 [1024], P('shard'), may hold values from 0.5 to 1.5
- w_query: bfloat16 [1024, 256], P('shard'), may hold values from -0.1875 to 0.1875
- w_key: bfloat16 [1024, 256], P('shard'), may hold values from -0.1875 to 0.1875
- w_value: bfloat16 [1024, 1024], P('shard'), may hold values from -0.1875 to 0.1875
- w_convgate: bfloat16 [1024, 1024], P('shard'), may hold values from -0.1875 to 0.1875
- w_output: bfloat16 [1024, 1024], P('shard'), may hold values from -0.375 to 0.375
- conv_filter: bfloat16 [3, 1024], P(None, 'shard'), may hold values from -2.390625 to 2.390625
- norm_gain_two: bfloat16 [1024], P('shard'), may hold values from 0.5 to 1.5
- w_gate: bfloat16 [1024, 4096], P('shard'), may hold values from -0.1875 to 0.1875
- w_up: bfloat16 [1024, 4096], P('shard'), may hold values from -0.1875 to 0.1875
- w_down: bfloat16 [4096, 1024], P('shard'), may hold values from -0.1875 to 0.1875
- cotangent: bfloat16 [32768, 1024], P(('rep', 'shard')), may hold values from -6 to 6
Outputs:
- out: bfloat16 [32768, 1024], P(('rep', 'shard'))
- grad_tokens: float32 [32768, 1024], P(('rep', 'shard'))
- grad_gain_one: float32 [1024], P('shard')
- grad_query: float32 [1024, 256], P('shard')
- grad_key: float32 [1024, 256], P('shard')
- grad_value: float32 [1024, 1024], P('shard')
- grad_convgate: float32 [1024, 1024], P('shard')
- grad_output: float32 [1024, 1024], P('shard')
- grad_filter: float32 [3, 1024], P(None, 'shard')
- grad_gain_two: float32 [1024], P('shard')
- grad_gate: float32 [1024, 4096], P('shard')
- grad_up: float32 [1024, 4096], P('shard')
- grad_down: float32 [4096, 1024], P('shard')
Inputs may be any that keep to these rules, and one draw needn't show every extreme that they name: `segment_ids`: along each sequence the document numbers never fall; a document holds at most 800 tokens.
All inputs are finite; a program needn't handle non-finite values.
Results may differ from a plain program's by a relative error of at most 0.02.
Values may be sent and summed in bfloat16 or wider, within the bound.
No kernel may reach another device: no remote copies, remote signals or barrier semaphores. Data moves between devices by JAX's collectives and lax.ppermute only.
A program may use at most 256 MiB of HBM per device.

v0:
```python
import jax
import jax.numpy as jnp
from jax import lax
from jax.sharding import PartitionSpec as P

HEADS = 16
FEAT = 16
KW = 3


eps_norm = 1e-06


def shift_down(values, segments, offset):
    moved_rows = jnp.concatenate(
        [jnp.zeros((offset, values.shape[1]), values.dtype), values[:-offset]], axis=0
    )
    moved_segments = jnp.concatenate([jnp.full((offset,), -1, jnp.int32), segments[:-offset]])
    return jnp.where((moved_segments == segments)[:, None], moved_rows, 0.0)


def shift_up(values, segments, offset):
    moved_rows = jnp.concatenate(
        [values[offset:], jnp.zeros((offset, values.shape[1]), values.dtype)], axis=0
    )
    moved_segments = jnp.concatenate([segments[offset:], jnp.full((offset,), -1, jnp.int32)])
    return jnp.where((moved_segments == segments)[:, None], moved_rows, 0.0)


def contract_rows(first_arr, second_arr):
    return lax.dot_general(
        first_arr, second_arr, (((0,), (0,)), ((), ())), preferred_element_type=jnp.float32
    )


def contract_cols(first_arr, second_arr):
    return lax.dot_general(
        first_arr, second_arr, (((1,), (1,)), ((), ())), preferred_element_type=jnp.float32
    )


def per_device(
    tokens,
    segment_ids,
    norm_gain_one,
    w_query,
    w_key,
    w_value,
    w_convgate,
    w_output,
    conv_filter,
    norm_gain_two,
    w_gate,
    w_up,
    w_down,
    cotangent,
):
    length = tokens.shape[0]
    model_width = tokens.shape[1]
    value_width = model_width // HEADS
    score_scale = FEAT ** (-0.5)
    segments = segment_ids[0]
    places = jnp.arange(length)
    visible = (places[:, None] >= places[None, :]) & (segments[:, None] == segments[None, :])
    gain_one, query_full, key_full, value_full, convgate_full, output_full, filter_full = (
        lax.all_gather(norm_gain_one, "shard", axis=0, tiled=True),
        lax.all_gather(w_query, "shard", axis=0, tiled=True),
        lax.all_gather(w_key, "shard", axis=0, tiled=True),
        lax.all_gather(w_value, "shard", axis=0, tiled=True),
        lax.all_gather(w_convgate, "shard", axis=0, tiled=True),
        lax.all_gather(w_output, "shard", axis=0, tiled=True),
        lax.all_gather(conv_filter, "shard", axis=1, tiled=True),
    )
    gain_two, gate_full, up_full, down_full = (
        lax.all_gather(norm_gain_two, "shard", axis=0, tiled=True),
        lax.all_gather(w_gate, "shard", axis=0, tiled=True),
        lax.all_gather(w_up, "shard", axis=0, tiled=True),
        lax.all_gather(w_down, "shard", axis=0, tiled=True),
    )
    gain_one_wide = gain_one.astype(jnp.float32)
    gain_two_wide = gain_two.astype(jnp.float32)
    filter_wide = filter_full.astype(jnp.float32)
    inputs = tokens.astype(jnp.float32)
    inverse_one = lax.rsqrt(jnp.mean(inputs * inputs, axis=-1, keepdims=True) + eps_norm)
    normed_one = inputs * inverse_one
    hidden_one = (normed_one * gain_one_wide).astype(jnp.bfloat16)
    queries = jnp.dot(hidden_one, query_full, preferred_element_type=jnp.float32).astype(
        jnp.bfloat16
    )
    key_rows = jnp.dot(hidden_one, key_full, preferred_element_type=jnp.float32).astype(
        jnp.bfloat16
    )
    values = jnp.dot(hidden_one, value_full, preferred_element_type=jnp.float32).astype(
        jnp.bfloat16
    )
    conv_gate = jnp.dot(hidden_one, convgate_full, preferred_element_type=jnp.float32)
    head_query = queries.reshape(length, HEADS, FEAT).transpose(1, 0, 2)
    head_key = key_rows.reshape(length, HEADS, FEAT).transpose(1, 0, 2)
    head_value = values.reshape(length, HEADS, value_width).transpose(1, 0, 2)

    def kernel_of(query_block, key_block):
        scores = contract_cols(query_block, key_block) * score_scale
        kernel = jnp.where(visible, 1.0 + scores + 0.5 * scores * scores, 0.0)
        return (scores, kernel)

    def attend(blocks):
        query_block, key_block, value_block = blocks
        unused_scores, kernel = kernel_of(query_block, key_block)
        totals = jnp.sum(kernel, axis=-1)
        numerators = jnp.dot(
            kernel.astype(jnp.bfloat16), value_block, preferred_element_type=jnp.float32
        )
        return (numerators / totals[:, None], totals)

    head_out, head_totals = lax.map(attend, (head_query, head_key, head_value))
    attention = head_out.transpose(1, 0, 2).reshape(length, model_width)
    values_wide = values.astype(jnp.float32)
    conv_value = filter_wide[0] * values_wide
    for offset in range(1, KW):
        conv_value = conv_value + filter_wide[offset] * shift_down(values_wide, segments, offset)
    mixed_low = (attention + conv_gate * conv_value).astype(jnp.bfloat16)
    middle = inputs + jnp.dot(mixed_low, output_full, preferred_element_type=jnp.float32)
    inverse_two = lax.rsqrt(jnp.mean(middle * middle, axis=-1, keepdims=True) + eps_norm)
    normed_two = middle * inverse_two
    hidden_two = (normed_two * gain_two_wide).astype(jnp.bfloat16)
    gate_pre = jnp.dot(hidden_two, gate_full, preferred_element_type=jnp.float32)
    up_pre = jnp.dot(hidden_two, up_full, preferred_element_type=jnp.float32)
    activation = (jax.nn.silu(gate_pre) * up_pre).astype(jnp.bfloat16)
    result = (middle + jnp.dot(activation, down_full, preferred_element_type=jnp.float32)).astype(
        jnp.bfloat16
    )
    grad_out = cotangent.astype(jnp.float32)
    grad_wdown = contract_rows(activation, cotangent)
    grad_act = contract_cols(cotangent, down_full)
    sigmoid_gate = jax.nn.sigmoid(gate_pre)
    grad_gate_pre = (
        grad_act * up_pre * sigmoid_gate * (1.0 + gate_pre * (1.0 - sigmoid_gate))
    ).astype(jnp.bfloat16)
    grad_up_pre = (grad_act * gate_pre * sigmoid_gate).astype(jnp.bfloat16)
    grad_wgate = contract_rows(hidden_two, grad_gate_pre)
    grad_wup = contract_rows(hidden_two, grad_up_pre)
    grad_hidden_two = contract_cols(grad_gate_pre, gate_full) + contract_cols(grad_up_pre, up_full)
    grad_gain_two = jnp.sum(grad_hidden_two * normed_two, axis=0)
    scaled_two = grad_hidden_two * gain_two_wide
    grad_middle = grad_out + inverse_two * (
        scaled_two - normed_two * jnp.mean(scaled_two * normed_two, axis=-1, keepdims=True)
    )
    mlp_done = (grad_gain_two, grad_wgate, grad_wup, grad_wdown)
    grad_branch = grad_middle.astype(jnp.bfloat16)
    grad_woutput = contract_rows(mixed_low, grad_branch)
    grad_mixed = contract_cols(grad_branch, output_full).astype(jnp.bfloat16).astype(jnp.float32)
    grad_conv_gate = (grad_mixed * conv_value).astype(jnp.bfloat16)
    grad_conv_value = grad_mixed * conv_gate
    filter_rows = [jnp.sum(grad_conv_value * values_wide, axis=0)]
    grad_values_conv = filter_wide[0] * grad_conv_value
    for offset in range(1, KW):
        filter_rows.append(
            jnp.sum(grad_conv_value * shift_down(values_wide, segments, offset), axis=0)
        )
        grad_values_conv = grad_values_conv + filter_wide[offset] * shift_up(
            grad_conv_value, segments, offset
        )
    grad_filter = jnp.stack(filter_rows, axis=0)
    grad_heads = grad_mixed.reshape(length, HEADS, value_width).transpose(1, 0, 2)

    def attend_back(blocks):
        query_block, key_block, value_block, grad_block, out_block, totals = blocks
        scores, kernel = kernel_of(query_block, key_block)
        grad_numerators = (grad_block / totals[:, None]).astype(jnp.bfloat16)
        grad_totals = -jnp.sum(grad_block * out_block, axis=-1) / totals
        grad_kernel = contract_cols(grad_numerators, value_block) + grad_totals[:, None]
        grad_scores = jnp.where(visible, grad_kernel * (1.0 + scores), 0.0).astype(jnp.bfloat16)
        grad_value_block = contract_rows(kernel.astype(jnp.bfloat16), grad_numerators)
        grad_query_block = (
            jnp.dot(grad_scores, key_block, preferred_element_type=jnp.float32) * score_scale
        )
        grad_key_block = contract_rows(grad_scores, query_block) * score_scale
        return (grad_query_block, grad_key_block, grad_value_block)

    head_gq, head_gk, head_gv = lax.map(
        attend_back, (head_query, head_key, head_value, grad_heads, head_out, head_totals)
    )
    grad_queries = head_gq.transpose(1, 0, 2).reshape(length, HEADS * FEAT).astype(jnp.bfloat16)
    grad_keys = head_gk.transpose(1, 0, 2).reshape(length, HEADS * FEAT).astype(jnp.bfloat16)
    grad_values = (
        head_gv.transpose(1, 0, 2).reshape(length, model_width) + grad_values_conv
    ).astype(jnp.bfloat16)
    grad_wquery = contract_rows(hidden_one, grad_queries)
    grad_wkey = contract_rows(hidden_one, grad_keys)
    grad_wvalue = contract_rows(hidden_one, grad_values)
    grad_wconvgate = contract_rows(hidden_one, grad_conv_gate)
    grad_hidden_one = contract_cols(grad_queries, query_full) + contract_cols(grad_keys, key_full)
    grad_hidden_one = (
        grad_hidden_one
        + contract_cols(grad_values, value_full)
        + contract_cols(grad_conv_gate, convgate_full)
    )
    grad_gain_one = jnp.sum(grad_hidden_one * normed_one, axis=0)
    scaled_one = grad_hidden_one * gain_one_wide
    grad_inputs = grad_middle + inverse_one * (
        scaled_one - normed_one * jnp.mean(scaled_one * normed_one, axis=-1, keepdims=True)
    )
    owned_every = (
        lax.psum_scatter(
            grad_gain_one.astype(jnp.bfloat16), "shard", scatter_dimension=0, tiled=True
        ).astype(jnp.float32),
        lax.psum_scatter(
            grad_wquery.astype(jnp.bfloat16), "shard", scatter_dimension=0, tiled=True
        ).astype(jnp.float32),
        lax.psum_scatter(
            grad_wkey.astype(jnp.bfloat16), "shard", scatter_dimension=0, tiled=True
        ).astype(jnp.float32),
        lax.psum_scatter(
            grad_wvalue.astype(jnp.bfloat16), "shard", scatter_dimension=0, tiled=True
        ).astype(jnp.float32),
        lax.psum_scatter(
            grad_wconvgate.astype(jnp.bfloat16), "shard", scatter_dimension=0, tiled=True
        ).astype(jnp.float32),
        lax.psum_scatter(
            grad_woutput.astype(jnp.bfloat16), "shard", scatter_dimension=0, tiled=True
        ).astype(jnp.float32),
        lax.psum_scatter(
            grad_filter.astype(jnp.bfloat16), "shard", scatter_dimension=1, tiled=True
        ).astype(jnp.float32),
        lax.psum_scatter(
            mlp_done[0].astype(jnp.bfloat16), "shard", scatter_dimension=0, tiled=True
        ).astype(jnp.float32),
        lax.psum_scatter(
            mlp_done[1].astype(jnp.bfloat16), "shard", scatter_dimension=0, tiled=True
        ).astype(jnp.float32),
        lax.psum_scatter(
            mlp_done[2].astype(jnp.bfloat16), "shard", scatter_dimension=0, tiled=True
        ).astype(jnp.float32),
        lax.psum_scatter(
            mlp_done[3].astype(jnp.bfloat16), "shard", scatter_dimension=0, tiled=True
        ).astype(jnp.float32),
    )
    everything = (
        lax.psum(owned_every[0].astype(jnp.bfloat16), "rep").astype(jnp.float32),
        lax.psum(owned_every[1].astype(jnp.bfloat16), "rep").astype(jnp.float32),
        lax.psum(owned_every[2].astype(jnp.bfloat16), "rep").astype(jnp.float32),
        lax.psum(owned_every[3].astype(jnp.bfloat16), "rep").astype(jnp.float32),
        lax.psum(owned_every[4].astype(jnp.bfloat16), "rep").astype(jnp.float32),
        lax.psum(owned_every[5].astype(jnp.bfloat16), "rep").astype(jnp.float32),
        lax.psum(owned_every[6].astype(jnp.bfloat16), "rep").astype(jnp.float32),
        lax.psum(owned_every[7].astype(jnp.bfloat16), "rep").astype(jnp.float32),
        lax.psum(owned_every[8].astype(jnp.bfloat16), "rep").astype(jnp.float32),
        lax.psum(owned_every[9].astype(jnp.bfloat16), "rep").astype(jnp.float32),
        lax.psum(owned_every[10].astype(jnp.bfloat16), "rep").astype(jnp.float32),
    )
    attn_done = everything[:7]
    mlp_done = everything[7:]
    return (
        result,
        grad_inputs,
        attn_done[0],
        attn_done[1],
        attn_done[2],
        attn_done[3],
        attn_done[4],
        attn_done[5],
        attn_done[6],
        mlp_done[0],
        mlp_done[1],
        mlp_done[2],
        mlp_done[3],
    )


def solution(mesh):
    return jax.shard_map(
        per_device,
        mesh=mesh,
        in_specs=(
            P(("rep", "shard"), None),
            P(("rep", "shard"), None),
            P("shard"),
            P("shard", None),
            P("shard", None),
            P("shard", None),
            P("shard", None),
            P("shard", None),
            P(None, "shard"),
            P("shard"),
            P("shard", None),
            P("shard", None),
            P("shard", None),
            P(("rep", "shard"), None),
        ),
        out_specs=(
            P(("rep", "shard"), None),
            P(("rep", "shard"), None),
            P("shard"),
            P("shard", None),
            P("shard", None),
            P("shard", None),
            P("shard", None),
            P("shard", None),
            P(None, "shard"),
            P("shard"),
            P("shard", None),
            P("shard", None),
            P("shard", None),
        ),
        check_vma=False,
    )
```

profile of v0, /device:TPU:0, one launch (start us, length us, event | category | flops | bytes accessed | tf_op | source)
XLA Modules:
  0.0 1270.6 jit_solution(83148800643041977)
XLA Ops:
  14.8 6.0 all-gather
  20.8 10.8 all_gather.34
  31.6 8.2 all_gather.35
  41.7 5.2 all_gather.38
  46.9 5.1 all-gather.1
  52.0 3.9 copy.47
  56.6 4.8 convolution_convert_fusion.7
  72.0 92.2 %while.32 = (s32[]{:T(128)}, f32[16,1024,64]{1,2,0:T(8,128)}, f32[16,1024]{1,0:T(8,128)}, bf16[16,1024,16]{1,2,0:T(8,128)(2,1)S(1)}, bf16[16,1024,16]{1,2,0:T(8,...) while((s32[]{:T(128)}, f32[16,1024,64]{1,2,0:T(8,128)}, ...), condition=%wide.region_3.4_spmd.clone, body=%wide.region_1.3_spmd.clone.sunk | while | flops 179371008 | bytes 4810849 | solution.py:115
  164.3 14.4 %fusion.69 = (bf16[1024,1024]{0,1:T(8,128)(2,1)}, f32[1024,1024]{0,1:T(8,128)}, f32[1024,1024]{0,1:T(8,128)}) fusion(f32[16,1024,64]{1,2,0:T(8,128)} %get-tuple-element.568, f32[1022,1024]{0,1:T(8,128)} %slice.65, pred[1024]{0:T(1024)(128)(4,1)S(1)} %get-tuple-element.406, f32[1024]{0:T(1024)S(1)} %bitcast.213, f32[1023,1024]{0,1:T(8,128)} %slice.63, ...), kind=kOutput, calls=%fused_computation.85 | convolution fusion | flops 2163212288 | bytes 29370368 | tf_op jit(solution)/shard_map/dot_general | solution.py:96
  178.8 5.4 multiply_reduce_fusion.5
  188.0 16.5 %fusion.86 = f32[1024,4096]{1,0:T(8,128)} fusion(bf16[1024,1024]{0,1:T(8,128)(2,1)} %multiply_convert_fusion.4, bf16[1024,4096]{1,0:T(8,128)(2,1)} %all-gather.15.cloned.1.call-done), kind=kOutput, calls=%fused_computation.128 | convolution fusion | flops 8589934592 | bytes 27262976 | tf_op jit(solution)/shard_map/dot_general | solution.py:126
  206.1 16.2 %fusion.87 = f32[1024,4096]{1,0:T(8,128)} fusion(bf16[1024,1024]{0,1:T(8,128)(2,1)} %multiply_convert_fusion.4, bf16[1024,4096]{1,0:T(8,128)(2,1)} %all-gather.17.cloned.1.call-done), kind=kOutput, calls=%fused_computation.129 | convolution fusion | flops 8589934592 | bytes 27262976 | tf_op jit(solution)/shard_map/dot_general | solution.py:127
  222.3 43.6 %all-gather.19.cloned.1.call-done = bf16[4096,1024]{1,0:T(8,128)(2,1)} async-done(((bf16[1024,1024]{1,0:T(8,128)(2,1)}), bf16[4096,1024]{1,0:T(8,128)(2,1)}) %all-gather.19.cloned.1.call-update) | async-done | bytes 8388624 | tf_op jit(solution)/shard_map/all_gather | solution.py:78
  265.8 31.2 %multiply_convert_fusion = (bf16[1024,4096]{1,0:T(8,128)(2,1)}, bf16[1024,4096]{1,0:T(8,128)(2,1)}, bf16[1024,4096]{1,0:T(8,128)(2,1)}) fusion(f32[1024,4096]{1,0:T(8,128)} %fusion.86, f32[1024,4096]{1,0:T(8,128)} %fusion.87, bf16[1024,1024]{1,0:T(8,128)(2,1)} %param.31, bf16[4096,1024]{1,0:T(8,128)(2,1)} %all-gather.19.cloned.1.call-done), kind=kOutput, calls=%fused_computation.61 | convolution fusion | flops 8657043456 | bytes 69206016 | tf_op jit(solution)/shard_map/dot_general | solution.py:37
  297.0 15.2 %fusion.88 = f32[1024,1024]{0,1:T(8,128)} fusion(bf16[1024,4096]{1,0:T(8,128)(2,1)} %get-tuple-element.399, bf16[1024,4096]{1,0:T(8,128)(2,1)} %all-gather.15.cloned.1.call-done), kind=kOutput, calls=%fused_computation.130 | convolution fusion | flops 8589934592 | bytes 20971520 | tf_op jit(solution)/shard_map/dot_general | solution.py:37
  312.3 14.9 %multiply_reduce_fusion = (bf16[1024]{0:T(1024)(128)(2,1)}, f32[1024]{0:T(1024)S(1)}, f32[1024,1024]{0,1:T(8,128)}) fusion(f32[1024,1024]{0,1:T(8,128)S(1)} %copy-done.10, f32[1024]{0:T(1024)S(1)} %add_rsqrt_fusion, f32[1024]{0:T(1024)S(1)} %bitcast.216, f32[1024,1024]{0,1:T(8,128)} %fusion.88, bf16[1024,4096]{1,0:T(8,128)(2,1)} %get-tuple-element.398, ...), kind=kOutput, calls=%fused_computation.86 | convolution fusion | flops 8597272576 | bytes 29374464 | tf_op jit(solution)/shard_map/dot_general | solution.py:37
  327.2 4.7 multiply_add_fusion
  335.8 8.0 multiply_reduce_fusion.3
  343.8 5.8 copy.50
  352.2 225.1 %while.33 = (s32[]{:T(128)}, bf16[16,1024,16]{1,2,0:T(8,128)(2,1)S(1)}, bf16[16,1024,16]{1,2,0:T(8,128)(2,1)}, f32[16,1024,64]{1,2,0:T(8,128)}, f32[16,1024,64]{...) while((s32[]{:T(128)}, ...), condition=%wide.region_8.9_spmd.clone, body=%wide.region_6.8_spmd.clone.sunk | while | flops 389448704 | bytes 43312340 | solution.py:180
  374.5 3.5 select_convert_fusion.10
  402.6 3.5 select_convert_fusion.10
  430.7 3.5 select_convert_fusion.10
  458.8 3.5 select_convert_fusion.10
  486.8 3.5 select_convert_fusion.10
  500.9 3.5 select_convert_fusion.10
  514.9 3.5 select_convert_fusion.10
  543.0 3.5 select_convert_fusion.10
  571.1 3.5 select_convert_fusion.10
  580.7 6.6 convolution_convert_fusion.5
  596.3 3.7 convolution_convert_fusion.6
  600.1 6.5 convolution_convert_fusion.4
  606.7 15.3 %convolution_convert_fusion.2 = bf16[1024,4096]{1,0:T(8,128)(2,1)} fusion(bf16[1024,1024]{0,1:T(8,128)(2,1)} %multiply_convert_fusion.4, bf16[1024,4096]{1,0:T(8,128)(2,1)} %get-tuple-element.399), kind=kOutput, calls=%fused_computation.67 | convolution fusion | flops 8594128896 | bytes 18874368 | tf_op jit(solution)/shard_map/dot_general | solution.py:31
  622.1 14.8 %convolution_convert_fusion.1 = bf16[1024,4096]{1,0:T(8,128)(2,1)} fusion(bf16[1024,1024]{0,1:T(8,128)(2,1)} %multiply_convert_fusion.4, bf16[1024,4096]{1,0:T(8,128)(2,1)} %get-tuple-element.398), kind=kOutput, calls=%fused_computation.66 | convolution fusion | flops 8594128896 | bytes 18874368 | tf_op jit(solution)/shard_map/dot_general | solution.py:31
  636.9 15.2 %convolution_convert_fusion = bf16[4096,1024]{1,0:T(8,128)(2,1)} fusion(bf16[1024,4096]{1,0:T(8,128)(2,1)} %get-tuple-element.400, bf16[1024,1024]{1,0:T(8,128)(2,1)} %param.31), kind=kOutput, calls=%fused_computation.65 | convolution fusion | flops 8594128896 | bytes 18874368 | tf_op jit(solution)/shard_map/dot_general | solution.py:31
  654.0 6.3 reduce-scatter.18.cloned.1.call-done
  660.2 34.6 %reduce-scatter.16.cloned.1.call-done = bf16[256,1024]{1,0:T(8,128)(2,1)} async-done(((bf16[1024,1024]{1,0:T(8,128)(2,1)}), bf16[256,1024]{1,0:T(8,128)(2,1)}) %reduce-scatter.16.cloned.1.call-update) | async-done | bytes 524304 | tf_op jit(solution)/shard_map/reduce_scatter | solution.py:213
  694.8 34.6 %reduce-scatter.20.cloned.1.call-done = bf16[256,1024]{1,0:T(8,128)(2,1)} async-done(((bf16[1024,1024]{1,0:T(8,128)(2,1)}), bf16[256,1024]{1,0:T(8,128)(2,1)}) %reduce-scatter.20.cloned.1.call-update) | async-done | bytes 524304 | tf_op jit(solution)/shard_map/reduce_scatter | solution.py:219
  729.4 74.4 %reduce-scatter.22.cloned.1.call-done = bf16[256,4096]{1,0:T(8,128)(2,1)} async-done(((bf16[1024,4096]{1,0:T(8,128)(2,1)}), bf16[256,4096]{1,0:T(8,128)(2,1)}) %reduce-scatter.22.cloned.1.call-update) | async-done | bytes 2097168 | tf_op jit(solution)/shard_map/reduce_scatter | solution.py:228
  803.8 74.3 %reduce-scatter.24.cloned.1.call-done = bf16[256,4096]{1,0:T(8,128)(2,1)} async-done(((bf16[1024,4096]{1,0:T(8,128)(2,1)}), bf16[256,4096]{1,0:T(8,128)(2,1)}) %reduce-scatter.24.cloned.1.call-update) | async-done | bytes 2097168 | tf_op jit(solution)/shard_map/reduce_scatter | solution.py:231
  878.1 74.4 %reduce-scatter.26.cloned.1.call-done = bf16[1024,1024]{1,0:T(8,128)(2,1)} async-done(((bf16[4096,1024]{1,0:T(8,128)(2,1)}), bf16[1024,1024]{1,0:T(8,128)(2,1)}) %reduce-scatter.26.cloned.1.call-update) | async-done | bytes 2097168 | tf_op jit(solution)/shard_map/reduce_scatter | solution.py:234
  965.2 5.7 all-reduce.10
  971.1 6.5 fusion.65
  977.6 5.3 copy.58
  982.9 15.2 %add_convert_fusion = bf16[1024,1024]{0,1:T(8,128)(2,1)S(1)} fusion(f32[1024,1024]{0,1:T(8,128)} %copy-done.9, bf16[1024,4096]{1,0:T(8,128)(2,1)} %get-tuple-element.400, bf16[4096,1024]{1,0:T(8,128)(2,1)} %all-gather.19.cloned.1.call-done), kind=kOutput, calls=%fused_computation.94 | convolution fusion | flops 8592031744 | bytes 23068672 | tf_op jit(solution)/shard_map/dot_general | solution.py:129
  1001.5 22.8 %all-reduce.8 = (bf16[256]{0:T(256)(128)(2,1)S(1)}, bf16[3,256]{1,0:T(4,128)(2,1)S(1)}, bf16[256]{0:T(256)(128)(2,1)S(1)}) all-reduce(bf16[256]{0:T(256)(128)(2,1)S(1)} %dynamic-slice.1, bf16[3,256]{1,0:T(4,128)(2,1)S(1)} %copy.68, bf16[256]{0:T(256)(128)(2,1)S(1)} %dynamic-slice.3), channel_id=1, replica_groups=mesh['rep'=8,'shard'=4] {'rep'}, use_global_device_ids=true, to_apply=%region_12.13 | all-reduce | flops 1280 | bytes 5120 | tf_op jit(solution)/shard_map/psum | solution.py:239
  1026.0 223.9 %all-reduce.13.cloned.1.call-done = (bf16[256,256]{1,0:T(8,128)(2,1)}, bf16[256,256]{1,0:T(8,128)(2,1)}, bf16[256,1024]{1,0:T(8,128)(2,1)}, bf16[256,1024]{1,0:T...) async-done(((bf16[256,256]{1,0:T(8,128)(2,1)}, bf16[256,256]{1,0:T(8,128)(2,1)}, ...) | async-done | bytes 8126480 | tf_op jit(solution)/shard_map/psum | solution.py:240
  1250.0 4.2 convert_element_type.242
  (503 shorter events, 357.7 us)
Async XLA Ops:
  7.2 49.4 %all-gather.9.cloned.1.call-start = ((), (), s32[]{:S(2)}) async-start(), calls=%async_computation.9 | async-start | bytes 2621440 | tf_op jit(solution)/shard_map/all_gather | solution.py:69
  7.9 156.3 %all-gather.11.cloned.1.call-start = ((), (), s32[]{:S(2)}) async-start(), calls=%async_computation.10 | async-start | bytes 2621440 | tf_op jit(solution)/shard_map/all_gather | solution.py:70
  8.7 170.1 %all-gather.13.cloned.1.call-start = ((), (), s32[]{:S(2)}) async-start(), calls=%async_computation.11 | async-start | bytes 2621440 | tf_op jit(solution)/shard_map/all_gather | solution.py:71
  9.4 178.6 %all-gather.15.cloned.1.call-start = ((), (), s32[]{:S(2)}) async-start(), calls=%async_computation.12 | async-start | bytes 10485760 | tf_op jit(solution)/shard_map/all_gather | solution.py:76
  10.0 196.1 %all-gather.17.cloned.1.call-start = ((), (), s32[]{:S(2)}) async-start(), calls=%async_computation.13 | async-start | bytes 10485760 | tf_op jit(solution)/shard_map/all_gather | solution.py:77
  10.6 10.2 copy-start.32
  10.6 21.1 %copy-start.33 = (bf16[256,256]{1,0:T(8,128)(2,1)S(1)}, bf16[256,256]{1,0:T(8,128)(2,1)}, u32[]{:S(2)}) copy-start(bf16[256,256]{1,0:T(8,128)(2,1)} %param.22) | copy-start | bytes 393220
  10.6 255.2 %all-gather.19.cloned.1.call-start = ((), (), s32[]{:S(2)}) async-start(), calls=%async_computation.14 | async-start | bytes 10485760 | tf_op jit(solution)/shard_map/all_gather | solution.py:78
  11.2 642.8 %reduce-scatter.12.cloned.1.call-start = ((), (), s32[]{:S(2)}) async-start(), calls=%async_computation.15 | async-start | bytes 655360 | tf_op jit(solution)/shard_map/reduce_scatter | solution.py:207
  14.3 26.5 %copy-start.2 = (bf16[1024,1024]{0,1:T(8,128)(2,1)}, bf16[1024,1024]{0,1:T(8,128)(2,1)S(1)}, u32[]{:S(2)}) copy-start(bf16[1024,1024]{0,1:T(8,128)(2,1)S(1)} %copy.43) | copy-start | bytes 6291460
  14.8 149.5 %copy-start.38 = (f32[1024]{0:T(1024)}, f32[1024]{0:T(1024)S(1)}, u32[]{:S(2)}) copy-start(f32[1024]{0:T(1024)S(1)} %add_rsqrt_fusion.1) | copy-start | bytes 12292
  20.8 143.4 %copy-start.40 = (f32[4,1,256]{2,1,0:T(1,128)}, f32[4,1,256]{2,1,0:T(1,128)S(1)}, u32[]{:S(2)}) copy-start(f32[4,1,256]{2,1,0:T(1,128)S(1)} %convert_element_type.247) | copy-start | bytes 12292
  31.6 9.1 copy-start.14
  40.8 6.1 copy-start.58
  46.9 117.4 %copy-start.42 = (f32[1,1024]{1,0:T(1,128)}, f32[1,1024]{1,0:T(1,128)S(1)}, u32[]{:S(2)}) copy-start(f32[1,1024]{1,0:T(1,128)S(1)} %get-tuple-element.401) | copy-start | bytes 12292
  46.9 117.4 %copy-start.44 = (f32[1,1024]{1,0:T(1,128)}, f32[1,1024]{1,0:T(1,128)S(1)}, u32[]{:S(2)}) copy-start(f32[1,1024]{1,0:T(1,128)S(1)} %get-tuple-element.402) | copy-start | bytes 12292
  46.9 117.4 %copy-start.46 = (f32[1,1024]{1,0:T(1,128)}, f32[1,1024]{1,0:T(1,128)S(1)}, u32[]{:S(2)}) copy-start(f32[1,1024]{1,0:T(1,128)S(1)} %get-tuple-element.403) | copy-start | bytes 12292
  164.2 14.5 %copy-start.31 = (bf16[16,1024,16]{1,2,0:T(8,128)(2,1)}, bf16[16,1024,16]{1,2,0:T(8,128)(2,1)S(1)}, u32[]{:S(2)}) copy-start(bf16[16,1024,16]{1,2,0:T(8,128)(2,1)S(1)} %get-tuple-element.682) | copy-start | bytes 1572868
  297.0 15.2 %copy-start.10 = (f32[1024,1024]{0,1:T(8,128)S(1)}, f32[1024,1024]{0,1:T(8,128)}, u32[]{:S(2)}) copy-start(f32[1024,1024]{0,1:T(8,128)} %copy-done.9) | copy-start | bytes 12582916
  297.0 15.2 %copy-start.55 = (bf16[1024,4096]{1,0:T(8,128)(2,1)S(1)}, bf16[1024,4096]{1,0:T(8,128)(2,1)}, u32[]{:S(2)}) copy-start(bf16[1024,4096]{1,0:T(8,128)(2,1)} %all-gather.17.cloned.1.call-done) | copy-start | bytes 25165828
  312.3 14.9 %copy-start.12 = (bf16[1024,1024]{0,1:T(8,128)(2,1)S(1)}, bf16[1024,1024]{0,1:T(8,128)(2,1)}, u32[]{:S(2)}) copy-start(bf16[1024,1024]{0,1:T(8,128)(2,1)} %copy.47) | copy-start | bytes 6291460
  327.2 6.4 copy-start.5
  327.2 8.6 copy-start.7
  331.9 12.0 copy-start.6
  352.1 225.2 %copy-start.3 = (bf16[1024,1024]{0,1:T(8,128)(2,1)S(1)}, bf16[1024,1024]{0,1:T(8,128)(2,1)}, u32[]{:S(2)}) copy-start(bf16[1024,1024]{0,1:T(8,128)(2,1)} %copy-done.2) | copy-start | bytes 6291460
  352.1 225.2 %copy-start.39 = (f32[1024]{0:T(1024)S(1)}, f32[1024]{0:T(1024)}, u32[]{:S(2)}) copy-start(f32[1024]{0:T(1024)} %copy-done.38) | copy-start | bytes 12292
  352.1 225.2 %copy-start.41 = (f32[4,1,256]{2,1,0:T(1,128)S(1)}, f32[4,1,256]{2,1,0:T(1,128)}, u32[]{:S(2)}) copy-start(f32[4,1,256]{2,1,0:T(1,128)} %copy-done.40) | copy-start | bytes 12292
  352.2 5.8 copy-start.29
  366.4 5.6 copy-start.29
  394.5 5.6 copy-start.29
  422.6 5.6 copy-start.29
  450.7 5.6 copy-start.29
  478.8 5.6 copy-start.29
  506.9 5.6 copy-start.29
  535.0 5.6 copy-start.29
  579.0 75.0 %reduce-scatter.14.cloned.1.call-start = ((), (), s32[]{:S(2)}) async-start(), calls=%async_computation.16 | async-start | bytes 655360 | tf_op jit(solution)/shard_map/reduce_scatter | solution.py:210
  580.6 79.6 %reduce-scatter.18.cloned.1.call-start = ((), (), s32[]{:S(2)}) async-start(), calls=%async_computation.18 | async-start | bytes 2621440 | tf_op jit(solution)/shard_map/reduce_scatter | solution.py:216
  587.3 107.6 %reduce-scatter.16.cloned.1.call-start = ((), (), s32[]{:S(2)}) async-start(), calls=%async_computation.17 | async-start | bytes 2621440 | tf_op jit(solution)/shard_map/reduce_scatter | solution.py:213
  600.1 129.3 %reduce-scatter.20.cloned.1.call-start = ((), (), s32[]{:S(2)}) async-start(), calls=%async_computation.19 | async-start | bytes 2621440 | tf_op jit(solution)/shard_map/reduce_scatter | solution.py:219
  606.7 197.1 %reduce-scatter.22.cloned.1.call-start = ((), (), s32[]{:S(2)}) async-start(), calls=%async_computation.20 | async-start | bytes 10485760 | tf_op jit(solution)/shard_map/reduce_scatter | solution.py:228
  622.0 256.1 %reduce-scatter.24.cloned.1.call-start = ((), (), s32[]{:S(2)}) async-start(), calls=%async_computation.21 | async-start | bytes 10485760 | tf_op jit(solution)/shard_map/reduce_scatter | solution.py:231
  636.9 315.6 %reduce-scatter.26.cloned.1.call-start = ((), (), s32[]{:S(2)}) async-start(), calls=%async_computation.22 | async-start | bytes 10485760 | tf_op jit(solution)/shard_map/reduce_scatter | solution.py:234
  652.1 348.5 %reduce-scatter.28.cloned.1.call-start = ((), (), s32[]{:S(2)}) async-start(), calls=%async_computation.23 | async-start | bytes 327680
  653.7 298.8 %copy-start.59 = (u32[32]{0:T(128)S(1)}, u32[32]{0:T(128)}, u32[]{:S(2)}) copy-start(u32[32]{0:T(128)} %constant.136) | copy-start | bytes 388
  653.7 300.0 %copy-start.15 = (bf16[1024,256]{1,0:T(8,128)(2,1)S(1)}, bf16[1024,256]{1,0:T(8,128)(2,1)}, u32[]{:S(2)}) copy-start(bf16[1024,256]{1,0:T(8,128)(2,1)} %copy-done.14) | copy-start | bytes 1572868
  653.7 596.2 %all-reduce.13.cloned.1.call-start = ((), (), s32[]{:S(2)}) async-start(), calls=%async_computation.24 | async-start | bytes 16252928 | tf_op jit(solution)/shard_map/psum | solution.py:240
  1256.7 5.7 copy-start.35
  1256.7 6.5 copy-start.34
  (73 other events, 249.1 us)
Sparse Core Ops, SparseCore 0:
  9.6 29.0 all-gather.8
  40.2 22.1 all-gather.10
  64.0 22.5 all-gather.12
  88.0 58.2 all-gather.14
  147.8 58.2 all-gather.16
  207.5 58.2 all-gather.18
  579.1 21.6 reduce-scatter.11
  604.0 21.6 reduce-scatter.13
  628.8 31.4 reduce-scatter.17
  663.3 31.4 reduce-scatter.15
  697.9 31.4 reduce-scatter.19
  732.0 71.7 reduce-scatter.21
  806.4 71.6 reduce-scatter.23
  880.7 71.6 reduce-scatter.25
  955.3 20.0 reduce-scatter.27
  981.7 268.2 all-reduce.12
where the time goes:
time: 1290 us; the launch traced here: 1270 us
  waiting for transfers between devices  571 us (44%)
  matrix products  459 us (36%)
  local copies, waits for them, and re-layouts  106 us (8%)
  blocking collectives  63.8 us (5%)
  other arithmetic  51.9 us (4%)
  between operations  15.5 us (1%)
    psum x1, waiting for transfers between devices, per_device(): lax.psum(owned_every[1].astype(jnp.bfloat16), 'rep').astype(jnp.float32)  224 us
    dot_general x56, matrix products, contract_cols(): lax.dot_general(first_arr, second_arr, (((1,), (1,)), ((), ())), preferre...  193 us
    dot_general x40, matrix products, contract_rows(): lax.dot_general(first_arr, second_arr, (((0,), (0,)), ((), ())), preferre...  134 us
    reduce_scatter x1, waiting for transfers between devices, per_device(): lax.psum_scatter(mlp_done[1].astype(jnp.bfloat16), 'shard', scatter_dimen...  74.4 us
    reduce_scatter x1, waiting for transfers between devices, per_device(): lax.psum_scatter(mlp_done[3].astype(jnp.bfloat16), 'shard', scatter_dimen...  74.4 us
    reduce_scatter x1, waiting for transfers between devices, per_device(): lax.psum_scatter(mlp_done[2].astype(jnp.bfloat16), 'shard', scatter_dimen...  74.3 us
    all_gather x1, waiting for transfers between devices, per_device(): lax.all_gather(w_down, 'shard', axis=0, tiled=True)  43.6 us
    dot_general x16, matrix products, attend(): jnp.dot(kernel.astype(jnp.bfloat16), value_block, preferred_element_type=...  35.3 us
  transfers between devices with their start and end apart: 16, of which 9 were waited for; matrix products, arithmetic and copies ran while one was open for 22% of the time, Pallas kernels for 0%

commit v1 on v0

v1 whole, which is shorter than its diff:
```python
import functools

import jax
import jax.numpy as jnp
import numpy as np
from jax import lax
from jax.experimental import pallas as pl
from jax.experimental.pallas import tpu as pltpu
from jax.sharding import Mesh
from jax.sharding import PartitionSpec as P

HEADS = 16
FEAT = 16
KW = 3
EPS = 1e-06
TILE = 256
SHARD_ROWS = 256
LANES = 128
COST = 0.6
X_AT, MIXER_AT, FEED_AT, DOWN_AT, PACK_AT, COLS_AT, GRAD_AT, OWNER_AT, ACT_AT = 0, 2, 8, 12, 16, 24, 32, 36, 40

low = jnp.bfloat16
wide = jnp.float32


def dot(a, b):
    return jnp.dot(a, b, preferred_element_type=wide)


def dot_nt(a, b):
    return lax.dot_general(a, b, (((1,), (1,)), ((), ())), preferred_element_type=wide)


def dot_tn(a, b):
    return lax.dot_general(a, b, (((0,), (0,)), ((), ())), preferred_element_type=wide)


class Order:
    last = None


def launch(kernel, deps=(), onto=(), *, scalars=0, grid, in_specs, out_specs, out_shape, scratch_shapes=(), **rest):
    taken = scalars + len(in_specs)
    deps = list(onto) + [d for d in deps if d is not None] + ([] if Order.last is None else [Order.last])

    def body(*refs):
        kernel(*refs[:taken], *refs[taken + len(deps) :])

    spec = pltpu.PrefetchScalarGridSpec(
        num_scalar_prefetch=scalars,
        grid=grid,
        in_specs=list(in_specs) + [pl.BlockSpec(memory_space=pl.ANY)] * len(deps),
        out_specs=out_specs,
        scratch_shapes=list(scratch_shapes),
    )
    aliases = {taken + n: n for n in range(len(onto))}
    run = pl.pallas_call(body, grid_spec=spec, out_shape=out_shape, input_output_aliases=aliases, **rest)

    def call(*operands):
        result = run(*operands, *deps)
        Order.last = result[0] if isinstance(result, (list, tuple)) else result
        return result

    return call


def params(mib):
    return pltpu.CompilerParams(vmem_limit_bytes=max(mib, 60) << 20)


def cost(gigaflops, mebibytes):
    return pl.CostEstimate(
        flops=int(gigaflops * COST * 1e9), bytes_accessed=int(mebibytes * COST * (1 << 20)), transcendentals=0
    )


def fixed(shape):
    return pl.BlockSpec(shape, lambda *_: (0,) * len(shape), pipeline_mode=pl.Buffered(1))


def rows(height, width):
    return pl.BlockSpec((height, width), lambda i, *_: (i, 0))


def place(offs_ref, base, pieces, full_ref):
    for n, piece in enumerate(pieces):
        at = pl.multiple_of(offs_ref[base + n], 128)
        full_ref[pl.ds(at, piece.shape[0]), :] = piece[...]


def project_kernel(offs_ref, x_ref, *refs):
    pieces, (hidden_ref, q_ref, k_ref, v_ref, gate_ref, full_ref, vec_ref) = refs[:6], refs[6:]
    heads = HEADS * FEAT
    width = x_ref.shape[1]

    @pl.when(pl.program_id(0) == 0)
    def _():
        place(offs_ref, MIXER_AT, pieces, full_ref)
        small = full_ref[:, 2 * heads + 2 * width :].astype(wide)
        vec_ref[...] = small.T[:8, :]

    x = x_ref[...].astype(wide)
    inverse = lax.rsqrt(jnp.mean(x * x, axis=-1, keepdims=True) + EPS)
    hidden = (x * inverse * vec_ref[0:1, :]).astype(low)
    hidden_ref[...] = hidden
    q_ref[...] = (dot(hidden, full_ref[:, :heads]) * FEAT ** (-0.5)).astype(low)
    k_ref[...] = dot(hidden, full_ref[:, heads : 2 * heads]).astype(low)
    v_ref[...] = dot(hidden, full_ref[:, 2 * heads : 2 * heads + width]).astype(low)
    gate_ref[...] = dot(hidden, full_ref[:, 2 * heads + width : 2 * heads + 2 * width]).astype(low)


def project(offs, x, pieces, deps=()):
    length, width = x.shape
    heads = HEADS * FEAT
    columns = pieces[0].shape[1]
    shapes = [
        jax.ShapeDtypeStruct((length, width), low),
        jax.ShapeDtypeStruct((length, heads), low),
        jax.ShapeDtypeStruct((length, heads), low),
        jax.ShapeDtypeStruct((length, width), low),
        jax.ShapeDtypeStruct((length, width), low),
        jax.ShapeDtypeStruct((width, columns), low),
        jax.ShapeDtypeStruct((8, width), wide),
    ]
    return launch(
        project_kernel,
        deps,
        scalars=1,
        grid=(length // TILE,),
        in_specs=[rows(TILE, width)] + [fixed(p.shape) for p in pieces],
        out_specs=[
            rows(TILE, width),
            rows(TILE, heads),
            rows(TILE, heads),
            rows(TILE, width),
            rows(TILE, width),
            fixed((width, columns)),
            fixed((8, width)),
        ],
        out_shape=shapes,
        compiler_params=params(40),
        cost_estimate=cost(7, 22),
        name="project",
    )(offs, x, *pieces)


def shift_rows(v, seg, by, up):
    zeros = jnp.zeros((by, v.shape[1]), v.dtype)
    none = jnp.full((by, 1), -1, seg.dtype)
    if up:
        moved, moved_seg = jnp.concatenate([v[by:], zeros], 0), jnp.concatenate([seg[by:], none], 0)
    else:
        moved = jnp.concatenate([zeros, v[:-by]], 0)
        moved_seg = jnp.concatenate([none, seg[:-by]], 0)
    return jnp.where(moved_seg == seg, moved, 0.0)


def lane_pick(width, start, stop):
    i = lax.broadcasted_iota(jnp.int32, (1, width), 1)
    return (i >= start) & (i < stop)


def attend_kernel(
    first, q_ref, k_ref, v_ref, gate_ref, vec_ref, segr_ref, segc_ref, mixed_ref, att_ref, recip_ref, mask_ref
):
    length = q_ref.shape[0]
    pair = pl.program_id(0) + first
    zero = jnp.zeros((), low)

    @pl.when(pair == first)
    def _():
        for tb in range(0, length, TILE):
            t = lax.broadcasted_iota(jnp.int32, (TILE, length), 0) + tb
            s = lax.broadcasted_iota(jnp.int32, (TILE, length), 1)
            seen = (s <= t) & (segc_ref[tb : tb + TILE, :] == segr_ref[...])
            mask_ref[tb : tb + TILE, :] = jnp.where(seen, 1.0, 0.0).astype(low)

    v = v_ref[...]
    keys, sides = [], []
    for i in range(2):
        head = 2 * pair + i
        keys.append(jnp.where(lane_pick(HEADS * FEAT, head * FEAT, (head + 1) * FEAT), k_ref[...], zero))
        lanes = lane_pick(128, 64 * i, 64 * i + 64)
        ones = jnp.broadcast_to(jnp.where(lanes, 1.0, 0.0).astype(low), (length, 128))
        sides.append(jnp.concatenate([jnp.where(lanes, v, zero), ones], 1))
    for tb in range(0, length, TILE):
        n = tb + TILE
        total = None
        for i in range(2):
            one_plus = dot_nt(q_ref[tb:n, :], keys[i][:n]) + 1.0
            kernel = (one_plus * one_plus + 1.0).astype(low) * mask_ref[tb:n, :n]
            part = dot(kernel, sides[i][:n])
            total = part if total is None else total + part
        recip = 1.0 / total[:, 128:]
        att_ref[tb:n, :] = (total[:, :128] * recip).astype(low)
        recip_ref[tb:n, :] = (2.0 * recip).astype(low)
    v_wide = v.astype(wide)
    seg = segc_ref[...]
    conv = vec_ref[2:3, :] * v_wide
    for j in range(1, KW):
        conv = conv + vec_ref[2 + j : 3 + j, :] * shift_rows(v_wide, seg, j, False)
    mixed_ref[...] = (att_ref[...].astype(wide) + gate_ref[...].astype(wide) * conv).astype(low)


def whole(a):
    return pl.BlockSpec(a.shape, lambda p: (0, 0))


def attend(q, k, v, gate, vec, seg, first, count, onto=(), deps=()):
    length, width = v.shape
    column = pl.BlockSpec((length, 128), lambda p: (0, p + first))
    seg_row, seg_col = seg.reshape(1, length), seg.reshape(length, 1)
    return launch(
        functools.partial(attend_kernel, first),
        deps,
        onto,
        grid=(count,),
        in_specs=[
            whole(q), whole(k), column, column, pl.BlockSpec((8, 128), lambda p: (0, p + first)), whole(seg_row), whole(seg_col)
        ],
        out_specs=[column] * 3,
        out_shape=[jax.ShapeDtypeStruct((length, width), low)] * 3,
        scratch_shapes=[pltpu.VMEM((length, length), low)],
        compiler_params=params(40),
        cost_estimate=cost(18 * count * 128 / width, 14),
        name="attention_forward",
    )(q, k, v, gate, vec, seg_row, seg_col)


def attend_back_kernel(
    first, q_ref, k_ref, v_ref, gm_ref, att_ref, recip_ref, gconv_ref, segr_ref, segc_ref,
    gqk_ref, gv_ref, mask_ref, gq_acc, gk_acc,
):
    length, heads = q_ref.shape
    pair = pl.program_id(0) + first
    zero = jnp.zeros((), low)

    @pl.when(pair == first)
    def _():
        for sb in range(0, length, TILE):
            s = lax.broadcasted_iota(jnp.int32, (TILE, length), 0) + sb
            t = lax.broadcasted_iota(jnp.int32, (TILE, length), 1)
            seen = (s <= t) & (segc_ref[sb : sb + TILE, :] == segr_ref[...])
            mask_ref[sb : sb + TILE, :] = jnp.where(seen, 1.0, 0.0).astype(low)
        gk_acc[...] = jnp.zeros_like(gk_acc)
        gq_acc[...] = jnp.zeros_like(gq_acc)

    v = v_ref[...]
    gm = gm_ref[...].astype(wide)
    gnum_wide = gm * recip_ref[...].astype(wide)
    gnum = gnum_wide.astype(low)
    product = gnum_wide * att_ref[...].astype(wide)
    high = product.astype(low)
    rest = (product - high.astype(wide)).astype(low)
    r = lax.broadcasted_iota(jnp.int32, (256, 128), 0)
    c = lax.broadcasted_iota(jnp.int32, (256, 128), 1)
    same_head = jnp.where(((r % 128) // 64) == (c // 64), 1.0, 0.0).astype(low)
    gtot = -dot(jnp.concatenate([high, rest], 1), same_head)
    gtot_high = gtot.astype(low)
    gtot_rest = (gtot - gtot_high.astype(wide)).astype(low)
    lane = lax.broadcasted_iota(jnp.int32, (1, 128), 1)
    left = jnp.concatenate([gnum, jnp.where(lane % 64 == 0, gtot_high, gtot_rest)], 1)
    gnum_half = gnum * jnp.asarray(0.5, low)
    queries, sides, gnums, keys = [], [], [], []
    for i in range(2):
        head = 2 * pair + i
        mine = lane_pick(heads, head * FEAT, (head + 1) * FEAT)
        queries.append(jnp.where(mine, q_ref[...], zero))
        keys.append(jnp.where(mine, k_ref[...], zero))
        lanes = lane_pick(128, 64 * i, 64 * i + 64)
        ones = jnp.where(lane_pick(128, 64 * i, 64 * i + 2), 1.0, 0.0).astype(low)
        sides.append(jnp.concatenate([jnp.where(lanes, v, zero), jnp.broadcast_to(ones, (length, 128))], 1))
        gnums.append(jnp.where(lanes, gnum_half, zero))
    for sb in range(0, length, TILE):
        n = sb + TILE
        gv = gconv_ref[sb:n, :].astype(wide)
        gk = None
        for i in range(2):
            one_plus = dot_nt(k_ref[sb:n, :], queries[i][sb:]) + 1.0
            mask = mask_ref[sb:n, sb:]
            kernel = (one_plus * one_plus + 1.0).astype(low) * mask
            gv = gv + dot(kernel, gnums[i][sb:])
            gkernel = dot_nt(sides[i][sb:n], left[sb:])
            gscores = (gkernel * one_plus).astype(low) * mask
            part = dot(gscores, queries[i][sb:])
            gk = part if gk is None else gk + part
            gq_acc[sb:, :] += dot_tn(gscores, keys[i][sb:n])
        gv_ref[sb:n, :] = gv.astype(low)
        gk_acc[sb:n, :] += gk

    @pl.when(pl.program_id(0) == pl.num_programs(0) - 1)
    def _():
        mine = slice(2 * FEAT * first, 2 * FEAT * first + gqk_ref.shape[1] // 2)
        gqk_ref[:, : gqk_ref.shape[1] // 2] = (gq_acc[:, mine] * FEAT ** (-0.5)).astype(low)
        gqk_ref[:, gqk_ref.shape[1] // 2 :] = gk_acc[:, mine].astype(low)


def attend_back(q, k, v, gm, att, recip, gconv, seg, first, count, onto=(), deps=()):
    length, width = v.shape
    heads = q.shape[1]
    column = pl.BlockSpec((length, 128), lambda p: (0, p + first))
    seg_row, seg_col = seg.reshape(1, length), seg.reshape(length, 1)
    return launch(
        functools.partial(attend_back_kernel, first),
        deps,
        onto,
        grid=(count,),
        in_specs=[whole(q), whole(k)] + [column] * 5 + [whole(seg_row), whole(seg_col)],
        out_specs=[pl.BlockSpec((length, 4 * FEAT * count), lambda p: (0, first // count)), column],
        out_shape=[jax.ShapeDtypeStruct((length, 2 * heads), low), jax.ShapeDtypeStruct((length, width), low)],
        scratch_shapes=[
            pltpu.VMEM((length, length), low),
            pltpu.VMEM((length, heads), wide),
            pltpu.VMEM((length, heads), wide),
        ],
        compiler_params=params(48),
        cost_estimate=cost(40 * count * 128 / width, 18),
        name="attention_backward",
    )(q, k, v, gm, att, recip, gconv, seg_row, seg_col)


def conv_back_kernel(v_ref, gm_ref, gate_ref, vec_ref, segc_ref, ggate_ref, gconv_ref, gfilt_ref):
    v_wide = v_ref[...].astype(wide)
    gm = gm_ref[...].astype(wide)
    seg = segc_ref[...]
    taps = [vec_ref[2 + j : 3 + j, :] for j in range(KW)]
    grad = gm * gate_ref[...].astype(wide)
    conv = taps[0] * v_wide
    gv_conv = taps[0] * grad
    lines = [jnp.sum(grad * v_wide, 0, keepdims=True)]
    for j in range(1, KW):
        moved = shift_rows(v_wide, seg, j, False)
        conv = conv + taps[j] * moved
        lines.append(jnp.sum(grad * moved, 0, keepdims=True))
        gv_conv = gv_conv + taps[j] * shift_rows(grad, seg, j, True)
    lines.append(jnp.zeros((LANES - KW, 128), wide))
    gfilt_ref[...] = jnp.concatenate(lines, 0).T.astype(low)
    ggate_ref[...] = (gm * conv).astype(low)
    gconv_ref[...] = gv_conv.astype(low)


def conv_back(v, gm, gate, vec, seg, deps=()):
    length, width = v.shape
    column = pl.BlockSpec((length, 128), lambda p: (0, p))
    small = pl.BlockSpec((8, 128), lambda p: (0, p))
    seg_col = seg.reshape(length, 1)
    return launch(
        conv_back_kernel,
        deps,
        grid=(width // 128,),
        in_specs=[column, column, column, small, whole(seg_col)],
        out_specs=[column, column, pl.BlockSpec((128, LANES), lambda p: (p, 0))],
        out_shape=[jax.ShapeDtypeStruct((length, width), low)] * 2 + [jax.ShapeDtypeStruct((width, LANES), low)],
        compiler_params=params(48),
        cost_estimate=cost(1, 10),
        name="convolution_backward",
    )(v, gm, gate, vec, seg_col)


def mix_kernel(offs_ref, x_ref, mixed_ref, vec_ref, *refs):
    pieces, (middle_ref, hidden_ref, full_ref) = refs[:6], refs[6:]

    @pl.when(pl.program_id(0) == 0)
    def _():
        place(offs_ref, MIXER_AT, pieces, full_ref)

    middle = x_ref[...].astype(wide) + dot(mixed_ref[...], full_ref[...])
    inverse = lax.rsqrt(jnp.mean(middle * middle, axis=-1, keepdims=True) + EPS)
    middle_ref[...] = middle
    hidden_ref[...] = (middle * inverse * vec_ref[1:2, :]).astype(low)


def mix(offs, x, mixed, vec, pieces, deps=()):
    length, width = x.shape
    return launch(
        mix_kernel,
        deps,
        scalars=1,
        grid=(length // TILE,),
        in_specs=[rows(TILE, width), rows(TILE, width), fixed(vec.shape)] + [fixed(p.shape) for p in pieces],
        out_specs=[rows(TILE, width), rows(TILE, width), fixed((width, width))],
        out_shape=[
            jax.ShapeDtypeStruct((length, width), wide),
            jax.ShapeDtypeStruct((length, width), low),
            jax.ShapeDtypeStruct((width, width), low),
        ],
        compiler_params=params(32),
        cost_estimate=cost(3, 16),
        name="mix",
    )(offs, x, mixed, vec, *pieces)


def first_half(n):
    return lambda i, *_: (jnp.minimum(i, n - 1), 0)


def second_half(n):
    return lambda i, *_: (jnp.maximum(i - n, 0), 0)


def feed_kernel(n, offs_ref, ha_ref, hb_ref, ca_ref, cb_ref, *refs):
    pieces, downs, (act_ref, both_ref, full_ref, down_ref) = refs[:4], refs[4:7], refs[7:]
    step = pl.program_id(0)
    half = full_ref.shape[1] // 2

    @pl.when(step == 0)
    def _():
        place(offs_ref, FEED_AT, pieces, full_ref)
        place(offs_ref, DOWN_AT, downs, down_ref)

    def work(hidden, cotangent):
        for at in range(0, half, 256):
            gate = dot(hidden, full_ref[:, at : at + 256])
            up = dot(hidden, full_ref[:, half + at : half + at + 256])
            gact = dot_nt(cotangent, down_ref[at : at + 256, :])
            sig = jax.nn.sigmoid(gate)
            silu = gate * sig
            act_ref[:, at : at + 256] = (silu * up).astype(low)
            both_ref[:, at : at + 256] = (gact * up * (sig + silu * (1.0 - sig))).astype(low)
            both_ref[:, half + at : half + at + 256] = (gact * silu).astype(low)

    @pl.when(step < n)
    def _():
        work(ha_ref[...], ca_ref[...])

    @pl.when(step >= n)
    def _():
        work(hb_ref[...], cb_ref[...])


def feed(offs, hidden, cotangent, j, w_down, pieces, down_pieces, deps=()):
    length, width = hidden[0].shape
    n = length // TILE
    half = w_down.shape[0]
    first = pl.BlockSpec((TILE, width), first_half(n))
    second = pl.BlockSpec((TILE, width), second_half(n))
    own_down = pl.BlockSpec((half // 2, width), lambda *_: (j, 0), pipeline_mode=pl.Buffered(1))
    given_rows = pl.BlockSpec(pieces[0].shape, lambda *_: (j, 0), pipeline_mode=pl.Buffered(1))
    return launch(
        functools.partial(feed_kernel, n),
        deps,
        scalars=1,
        grid=(2 * n,),
        in_specs=[first, second, first, second]
        + [fixed(pieces[0].shape), given_rows]
        + [fixed(p.shape) for p in pieces[2:]]
        + [own_down]
        + [fixed(p.shape) for p in down_pieces],
        out_specs=[rows(TILE, half), rows(TILE, 2 * half), fixed((width, 2 * half)), fixed((half, width))],
        out_shape=[
            jax.ShapeDtypeStruct((2 * length, half), low),
            jax.ShapeDtypeStruct((2 * length, 2 * half), low),
            jax.ShapeDtypeStruct((width, 2 * half), low),
            jax.ShapeDtypeStruct((half, width), low),
        ],
        compiler_params=params(48),
        cost_estimate=cost(16, 34),
        name="feed_in",
    )(offs, *hidden, *cotangent, *pieces, w_down, *down_pieces)


def weight_grad_kernel(parts, counts, outs, length, offs_ref, *refs):
    blocks = sum(outs)
    lefts = [refs[b * parts : (b + 1) * parts] for b in range(blocks)]
    rights = refs[blocks * parts : -len(outs)]
    targets = [(ref, row * TILE) for ref, height in zip(refs[-len(outs) :], outs) for row in range(height)]
    terms = max(parts, len(rights) // len(counts))
    step = pl.program_id(0)

    def part_of(group, t):
        return group[t][...] if len(group) == terms else group[0][t * length : (t + 1) * length, :]

    def work(group):
        for b in range(blocks):
            value = None
            for t in range(terms):
                product = dot_tn(part_of(lefts[b], t), part_of(group, t))
                value = product if value is None else value + product
            ref, row = targets[b]
            ref[row : row + TILE, :] = value.astype(low)

    each = len(rights) // len(counts)
    start = 0
    for n, count in enumerate(counts):
        group = rights[n * each : (n + 1) * each]
        if len(counts) == 1:
            work(group)
        else:
            pl.when((step >= start) & (step < start + count))(functools.partial(work, group))
        start += count


def weight_grad(offs, base, lefts, rights, outs, name, tile=512, deps=()):
    blocks = sum(outs)
    counts = [group[0].shape[1] // tile for group in rights]
    columns = sum(counts) * tile
    in_specs, operands = [], []
    for b in range(blocks):
        for a in lefts:
            in_specs.append(pl.BlockSpec((a.shape[0], TILE), lambda j, offs, b=b: (0, offs[base + b])))
            operands.append(a)
    start = 0
    for group, count in zip(rights, counts):
        for a in group:
            def where_to(j, offs, start=start, count=count):
                return (0, jnp.clip(j - start, 0, count - 1))
            in_specs.append(pl.BlockSpec((a.shape[0], tile), where_to))
            operands.append(a)
        start += count
    tokens = sum(a.shape[0] for a in lefts)
    terms = max(len(lefts), len(rights[0]))
    result = launch(
        functools.partial(weight_grad_kernel, len(lefts), counts, outs, tokens // terms),
        deps,
        scalars=1,
        grid=(sum(counts),),
        in_specs=in_specs,
        out_specs=[pl.BlockSpec((height * TILE, tile), lambda j, offs: (0, j)) for height in outs],
        out_shape=[jax.ShapeDtypeStruct((height * TILE, columns), low) for height in outs],
        compiler_params=params(48),
        cost_estimate=cost(2.5e-9 * tokens * 1024 * columns, (tokens * (1024 + columns) * 2 + 2048 * columns) / 2**20),
        name=name,
    )(offs, *operands)
    return result


def feed_back_kernel(a_ref, b_ref, wa_ref, wb_ref, out_ref):
    out_ref[...] = (dot_nt(a_ref[...], wa_ref[...]) + dot_nt(b_ref[...], wb_ref[...])).astype(low)


def feed_back(first, second, full_first, full_second, deps=()):
    length = first.shape[0] // 2
    width = full_first.shape[0]
    n = length // TILE
    tile = pl.BlockSpec((TILE, first.shape[1]), lambda i: (i + n, 0))
    return launch(
        feed_back_kernel,
        deps,
        grid=(n,),
        in_specs=[tile, tile, fixed(full_first.shape), fixed(full_second.shape)],
        out_specs=rows(TILE, width),
        out_shape=jax.ShapeDtypeStruct((length, width), low),
        compiler_params=params(32),
        cost_estimate=cost(10, 18),
        name="feed_back_partner",
    )(first, second, full_first, full_second)


def middle_back_kernel(
    a_ref, b_ref, other_ref, middle_ref, cot_ref, vec_ref, wa_ref, wb_ref, wo_ref,
    gmiddle_ref, gbranch_ref, gmixed_ref, ggain_ref,
):
    ghidden = dot_nt(a_ref[...], wa_ref[...]) + dot_nt(b_ref[...], wb_ref[...]) + other_ref[...].astype(wide)
    middle = middle_ref[...]
    inverse = lax.rsqrt(jnp.mean(middle * middle, axis=-1, keepdims=True) + EPS)
    normed = middle * inverse
    gain = jnp.sum(ghidden * normed, axis=0, keepdims=True)

    @pl.when(pl.program_id(0) == 0)
    def _():
        ggain_ref[...] = jnp.zeros_like(ggain_ref)

    ggain_ref[0:1, :] += gain
    scaled = ghidden * vec_ref[1:2, :]
    gmiddle = cot_ref[...].astype(wide) + inverse * (
        scaled - normed * jnp.mean(scaled * normed, axis=-1, keepdims=True)
    )
    gmiddle_ref[...] = gmiddle
    gbranch = gmiddle.astype(low)
    gbranch_ref[...] = gbranch
    gmixed_ref[...] = dot_nt(gbranch, wo_ref[...]).astype(low)


def middle_back(first, second, other, middle, cotangent, vec, full_first, full_second, w_output, deps=()):
    length, width = middle.shape
    tile = rows(TILE, first.shape[1])
    line = rows(TILE, width)
    return launch(
        middle_back_kernel,
        deps,
        grid=(length // TILE,),
        in_specs=[
            tile, tile, line, line, line, fixed(vec.shape), fixed(full_first.shape), fixed(full_second.shape), fixed(w_output.shape)
        ],
        out_specs=[line, line, line, fixed((8, width))],
        out_shape=[
            jax.ShapeDtypeStruct((length, width), wide),
            jax.ShapeDtypeStruct((length, width), low),
            jax.ShapeDtypeStruct((length, width), low),
            jax.ShapeDtypeStruct((8, width), wide),
        ],
        compiler_params=params(48),
        cost_estimate=cost(13, 40),
        name="middle_back",
    )(first, second, other, middle, cotangent, vec, full_first, full_second, w_output)


def feed_out_kernel(add, *refs):
    out_ref = refs[-1]
    value = dot(refs[0][...], refs[2][...]) + dot(refs[1][...], refs[3][...])
    for ref in refs[4:-1]:
        value = value + ref[...].astype(wide)
    out_ref[...] = value.astype(low)


def feed_out(first, second, down_first, down_second, shift, extras, name, deps=()):
    length = first.shape[0] // 2
    width = down_first.shape[1]
    n = length // TILE
    tile = pl.BlockSpec((TILE, first.shape[1]), lambda i: (i + shift * n, 0))
    return launch(
        functools.partial(feed_out_kernel, len(extras)),
        deps,
        grid=(n,),
        in_specs=[tile, tile, fixed(down_first.shape), fixed(down_second.shape)] + [rows(TILE, width)] * len(extras),
        out_specs=rows(TILE, width),
        out_shape=jax.ShapeDtypeStruct((length, width), low),
        compiler_params=params(32),
        cost_estimate=cost(5, 16),
        name=name,
    )(first, second, down_first, down_second, *extras)


def tokens_back_kernel(gqk_ref, gv_ref, ggate_ref, x_ref, gmiddle_ref, vec_ref, full_ref, gtokens_ref, ggain_ref):
    two = gqk_ref.shape[1]
    width = x_ref.shape[1]
    quarter = two // 4
    ghidden = None
    for n, col in enumerate((0, 2, 1, 3)):
        term = dot_nt(gqk_ref[:, n * quarter : (n + 1) * quarter], full_ref[:, col * quarter : (col + 1) * quarter])
        ghidden = term if ghidden is None else ghidden + term
    ghidden = (
        ghidden
        + dot_nt(gv_ref[...], full_ref[:, two : two + width])
        + dot_nt(ggate_ref[...], full_ref[:, two + width : two + 2 * width])
    )
    x = x_ref[...].astype(wide)
    inverse = lax.rsqrt(jnp.mean(x * x, axis=-1, keepdims=True) + EPS)
    normed = x * inverse

    @pl.when(pl.program_id(0) == 0)
    def _():
        ggain_ref[...] = jnp.zeros_like(ggain_ref)

    ggain_ref[0:1, :] += jnp.sum(ghidden * normed, axis=0, keepdims=True)
    scaled = ghidden * vec_ref[0:1, :]
    gtokens_ref[...] = gmiddle_ref[...] + inverse * (
        scaled - normed * jnp.mean(scaled * normed, axis=-1, keepdims=True)
    )


def tokens_back(gqk, gv, ggate, x, gmiddle, vec, full, deps=()):
    length, width = x.shape
    line = rows(TILE, width)
    return launch(
        tokens_back_kernel,
        deps,
        grid=(length // TILE,),
        in_specs=[rows(TILE, gqk.shape[1]), line, line, line, line, fixed(vec.shape), fixed(full.shape)],
        out_specs=[line, fixed((8, width))],
        out_shape=[jax.ShapeDtypeStruct((length, width), wide), jax.ShapeDtypeStruct((8, width), wide)],
        compiler_params=params(40),
        cost_estimate=cost(7, 24),
        name="tokens_back",
    )(gqk, gv, ggate, x, gmiddle, vec, full)


def spread_kernel(cols_ref, gain_ref, wg_ref, wu_ref, a_ref, b_ref, c_ref, d_ref, gate_ref, up_ref, ggain_ref):
    total = None
    for n, ref in enumerate((a_ref, b_ref, c_ref, d_ref)):
        quarter = ref.shape[1] // 4
        for part_y in range(2):
            at = pl.ds(pl.multiple_of(cols_ref[COLS_AT + 2 * n + part_y], 512), quarter)
            gate = ref[:, part_y * quarter : (part_y + 1) * quarter].astype(wide)
            up = ref[:, (2 + part_y) * quarter : (3 + part_y) * quarter].astype(wide)
            gate_ref[:, at] = gate
            up_ref[:, at] = up
            term = gate * wg_ref[:, at].astype(wide) + up * wu_ref[:, at].astype(wide)
            line = jnp.sum(term, axis=1, keepdims=True)
            total = line if total is None else total + line
    ggain_ref[...] = total / gain_ref[...]


def spread(cols, gain, w_gate, w_up, blocks, deps=()):
    height, width = blocks[0].shape
    shape = jax.ShapeDtypeStruct((height, 2 * width), wide)
    return launch(
        spread_kernel,
        deps,
        scalars=1,
        grid=(1,),
        in_specs=[fixed(gain.shape), fixed(w_gate.shape), fixed(w_up.shape)] + [fixed(b.shape) for b in blocks],
        out_specs=[fixed(shape.shape)] * 2 + [fixed(gain.shape)],
        out_shape=[shape, shape, jax.ShapeDtypeStruct(gain.shape, wide)],
        compiler_params=params(24),
        cost_estimate=cost(0.001, 16),
        name="spread",
    )(cols, gain, w_gate, w_up, *blocks)


def pack_kernel(at_ref, g1_ref, g2_ref, taps_ref, q_ref, k_ref, v_ref, c_ref, o_ref, pack_ref, half_ref, ohalf_ref):
    height = q_ref.shape[0]
    col = 0
    for ref in (q_ref, k_ref, v_ref, c_ref):
        pack_ref[:, col : col + ref.shape[1]] = ref[...]
        col += ref.shape[1]
    small = jnp.concatenate([g1_ref[...].astype(wide), g2_ref[...].astype(wide), taps_ref[...].astype(wide)], 0)
    small = jnp.concatenate([small, jnp.zeros((LANES - small.shape[0], height), wide)], 0)
    pack_ref[:, col : col + LANES] = small.T.astype(low)
    at = pl.multiple_of(at_ref[X_AT] * (height // 2), 128)
    half_ref[...] = pack_ref[pl.ds(at, height // 2), :]
    ohalf_ref[...] = o_ref[pl.ds(at, height // 2), :]


def pack_mixer(at, gain_one, gain_two, taps, w_query, w_key, w_value, w_convgate, w_output):
    operands = (gain_one, gain_two, taps, w_query, w_key, w_value, w_convgate, w_output)
    height = w_query.shape[0]
    columns = w_query.shape[1] + w_key.shape[1] + w_value.shape[1] + w_convgate.shape[1] + LANES
    shapes = [(height, columns), (height // 2, columns), (height // 2, w_output.shape[1])]
    return launch(
        pack_kernel,
        scalars=1,
        grid=(1,),
        in_specs=[fixed(a.shape) for a in operands],
        out_specs=[fixed(a) for a in shapes],
        out_shape=[jax.ShapeDtypeStruct(a, low) for a in shapes],
        compiler_params=params(24),
        cost_estimate=cost(0.001, 4),
        name="pack_mixer",
    )(at, *operands)


def pack_feed_kernel(offs_ref, gate_ref, up_ref, down_ref, first_ref, second_ref, give_ref, low_ref, high_ref):
    height = gate_ref.shape[0]
    targets = ((first_ref, 0), (second_ref, 0), (give_ref, 0), (give_ref, height))
    for n, (ref, row) in enumerate(targets):
        quarter = ref.shape[1] // 4
        for part_y in range(2):
            at = pl.ds(pl.multiple_of(offs_ref[PACK_AT + 2 * n + part_y], 512), quarter)
            ref[row : row + height, part_y * quarter : (part_y + 1) * quarter] = gate_ref[:, at]
            ref[row : row + height, (2 + part_y) * quarter : (3 + part_y) * quarter] = up_ref[:, at]
    size = low_ref.shape[0]
    for turn, ref in enumerate((low_ref, high_ref)):
        at = pl.multiple_of(offs_ref[X_AT] * size + turn * 2 * size, 128)
        ref[...] = down_ref[pl.ds(at, size), :]


def pack_feed(offs, w_gate, w_up, w_down, deps=()):
    height, columns = w_gate.shape
    shapes = [(height, columns // 2)] * 2 + [(2 * height, columns // 2)] + [(w_down.shape[0] // 4, w_down.shape[1])] * 2
    return launch(
        pack_feed_kernel,
        deps,
        scalars=1,
        grid=(1,),
        in_specs=[fixed(w_gate.shape), fixed(w_up.shape), fixed(w_down.shape)],
        out_specs=[fixed(a) for a in shapes],
        out_shape=[jax.ShapeDtypeStruct(a, low) for a in shapes],
        compiler_params=params(24),
        cost_estimate=cost(0.001, 8),
        name="pack_feed",
    )(offs, w_gate, w_up, w_down)


def step(kernel, offs, operands, shapes, name, deps=()):
    return launch(
        kernel,
        deps,
        scalars=1,
        grid=(1,),
        in_specs=[fixed(a.shape) for a in operands],
        out_specs=[fixed(a) for a in shapes],
        out_shape=[jax.ShapeDtypeStruct(a, low) for a in shapes],
        compiler_params=params(24),
        cost_estimate=cost(0.001, 8),
        name=name,
    )(offs, *operands)


def pick_kernel(offs_ref, first_ref, second_ref, given_ref, a_ref, b_ref):
    height = first_ref.shape[0]

    @pl.when(offs_ref[X_AT] == 0)
    def _():
        a_ref[...] = first_ref[...]
        b_ref[...] = second_ref[...]

    @pl.when(offs_ref[X_AT] != 0)
    def _():
        a_ref[...] = given_ref[:height, :]
        b_ref[...] = given_ref[height:, :]


def add(*refs):
    total = refs[0].astype(wide)
    for other in refs[1:]:
        total = total + other.astype(wide)
    return total.astype(low)


def top_kernel(offs_ref, keep_ref, came_ref, give_ref):
    size = give_ref.shape[0]
    give_ref[...] = add(keep_ref[:size, :], came_ref[:size, :])


def top_sum(offs, keep, came, deps=()):
    return step(top_kernel, offs, [keep, came], [(keep.shape[0] // 2, keep.shape[1])], "top_sum", deps)[0]


def rest_kernel(offs_ref, *refs):
    out_ref = refs[-1]
    col = 0
    for n in range(0, len(refs) - 1, 3):
        keep_ref, came_ref, passed_ref = refs[n : n + 3]
        size, width = passed_ref.shape
        skip = came_ref.shape[0] - size
        out_ref[:, col : col + width] = add(keep_ref[size:, :], came_ref[skip:, :], passed_ref[...])
        col += width


def rest_sum(offs, triples, deps=()):
    operands = [a for triple in triples for a in triple]
    shape = (triples[0][2].shape[0], sum(t[2].shape[1] for t in triples))
    return step(rest_kernel, offs, operands, [shape], "rest_sum", deps)[0]


def halves_kernel(filters, offs_ref, *refs):
    top_ref, rest_ref = refs[-2:]
    size = top_ref.shape[0]
    col = 0
    for n in range(0, len(refs) - 2, 2):
        keep_ref, came_ref = refs[n : n + 2]
        at = slice(col, col + keep_ref.shape[1])
        col += keep_ref.shape[1]
        if filters and n == len(refs) - 4:
            for ref, line in ((top_ref, offs_ref[OWNER_AT + 2]), (rest_ref, offs_ref[OWNER_AT + 3])):
                rows_at = pl.ds(pl.multiple_of(line * size, 128), size)
                ref[:, at] = add(keep_ref[rows_at, :], came_ref[rows_at, :])
        else:
            top_ref[:, at] = add(keep_ref[:size, :], came_ref[:size, :])
            rest_ref[:, at] = add(keep_ref[size:, :], came_ref[size:, :])


def halves_sum(offs, pairs, filters=False, deps=()):
    operands = [a for pair in pairs for a in pair]
    shape = (pairs[0][0].shape[0] // 2, sum(pair[0].shape[1] for pair in pairs))
    return step(functools.partial(halves_kernel, filters), offs, operands, [shape] * 2, "halves_sum", deps)


def near_kernel(offs_ref, keep_ref, came_ref, own_ref, other_ref):
    size = own_ref.shape[0]
    for ref, side in ((own_ref, offs_ref[X_AT]), (other_ref, 1 - offs_ref[X_AT])):
        at = pl.ds(pl.multiple_of(side * size, 128), size)
        ref[...] = add(keep_ref[at, :], came_ref[at, :])


def near_split(offs, keep, came, deps=()):
    return step(near_kernel, offs, [keep, came], [(keep.shape[0] // 2, keep.shape[1])] * 2, "near_split", deps)


def pair_kernel(offs_ref, a_ref, b_ref, out_ref):
    out_ref[...] = add(a_ref[...], b_ref[...])


def pair_sum(offs, a, b, deps=()):
    return step(pair_kernel, offs, [a, b], [a.shape], "pair_sum", deps)[0]


def sort_kernel(offs_ref, total_ref, other_ref, own_ref, give_ref):
    @pl.when(offs_ref[X_AT + 1] == 0)
    def _():
        own_ref[...] = total_ref[...]
        give_ref[...] = other_ref[...]

    @pl.when(offs_ref[X_AT + 1] != 0)
    def _():
        own_ref[...] = other_ref[...]
        give_ref[...] = total_ref[...]


def sort_rows(offs, total, other, deps=()):
    return step(sort_kernel, offs, [total, other], [total.shape] * 2, "sort_rows", deps)


def swap(value, axis):
    return lax.ppermute(value, axis, [(0, 1), (1, 0)])


def part(value, index, count, axis=0):
    size = value.shape[axis] // count
    return lax.dynamic_slice_in_dim(value, index * size, size, axis)


def in_order(index, mine, other):
    return jnp.where(
        index == 0, jnp.concatenate([mine, other], 0), jnp.concatenate([other, mine], 0)
    )


def per_device(
    tokens, segment_ids, gain_one, w_query, w_key, w_value, w_convgate, w_output, conv_filter,
    gain_two, w_gate, w_up, w_down, cotangent,
):
    Order.last = None
    x = lax.axis_index("near")
    y = lax.axis_index("row")
    c = lax.axis_index("core")
    s = 2 * y + c
    width = tokens.shape[1]
    seg = segment_ids[0]
    block = w_down.shape[0]

    def flip(bits):
        return jnp.bitwise_xor(s, bits)

    small_block = block // 2
    half = SHARD_ROWS // 2

    def feed_cols(core, j):
        return [((2 * row + core) * 2 + j) * small_block for row in range(2)]

    feed_rows = [s, flip(1), jnp.bitwise_xor(flip(2), x), jnp.bitwise_xor(flip(3), x)]
    offs = [
        x,
        jnp.bitwise_xor(x, c),
        s * SHARD_ROWS,
        flip(1) * SHARD_ROWS,
        flip(2) * SHARD_ROWS + x * half,
        flip(2) * SHARD_ROWS + (1 - x) * half,
        flip(3) * SHARD_ROWS + x * half,
        flip(3) * SHARD_ROWS + (1 - x) * half,
        *(a * SHARD_ROWS for a in feed_rows),
        y * small_block,
        (1 - y) * small_block + x * (small_block // 2),
        (1 - y) * small_block + (1 - x) * (small_block // 2),
        0,
        *feed_cols(c, 0), *feed_cols(c, 1), *feed_cols(1 - c, 0), *feed_cols(1 - c, 1),
        *feed_cols(c, 0), *feed_cols(1 - c, 0), *feed_cols(c, 1), *feed_cols(1 - c, 1),
        2 * (1 - y) + 1 - x, 2 * (1 - y) + x, 2 * y + 1 - x, 2 * y + x,
        flip(3), flip(1), flip(2), s,
        2 * (1 - y) + 1 - x, 2 * y + 1 - x, 2 * (1 - y) + x, 2 * y + x,
    ]
    offs = jnp.stack([jnp.asarray(a, jnp.int32) for a in offs])

    pack, pack_half, output_half = pack_mixer(
        offs, gain_one[None], gain_two[None], conv_filter, w_query, w_key, w_value, w_convgate, w_output
    )

    def fetch(own, own_half):
        near_core = swap(own, "core")
        direct = swap(own_half, "row")
        relayed = swap(direct, "near")
        return [own, near_core, direct, relayed, swap(direct, "core"), swap(relayed, "core")]

    pack_pieces = fetch(pack, pack_half)
    output_pieces = fetch(w_output, output_half)
    cot_other = swap(cotangent, "core")

    mine_first, mine_second, give, *down_halves = pack_feed(offs, w_gate, w_up, w_down)
    given = swap(give, "core")
    sends = step(pick_kernel, offs, [mine_first, mine_second, given], [mine_first.shape] * 2, "pick")
    feed_pieces, down_pieces = [], []
    for j, own in enumerate((mine_first, mine_second)):
        direct = swap(sends[j], "row")
        feed_pieces.append([own, given, direct, swap(direct, "near")])
        direct = swap(down_halves[j], "row")
        down_pieces.append([direct, swap(direct, "near")])

    hidden_one, queries, keys, values, gates, full_one, vec = project(
        offs, tokens, pack_pieces, deps=[cot_other, output_pieces[1], output_pieces[2]]
    )
    pairs = width // 256
    attended = attend(
        queries, keys, values, gates, vec, seg, 0, pairs, deps=[output_pieces[3], output_pieces[4]]
    )
    mixed, attention, recips = attend(
        queries, keys, values, gates, vec, seg, pairs, pairs, onto=attended, deps=[feed_pieces[0][2], output_pieces[5]]
    )
    middle, hidden_two, full_output = mix(offs, tokens, mixed, vec, output_pieces, deps=[down_pieces[0][0]])
    hiddens = [hidden_two, swap(hidden_two, "core")]
    cots = [cotangent, cot_other]

    def after(value, other):
        return value if other is None else lax.optimization_barrier((value, other))[0]

    def far_sum(part, previous):
        return lax.psum(after(part, previous), "far")

    def far_swap(value, bit):
        count = lax.axis_size("far")
        if bit >= count:
            return None
        return lax.ppermute(value, "far", [(i, i ^ bit) for i in range(count)])

    def far_rest(value, came):
        value = pair_sum(offs, value, came)
        bit = 4
        while bit < lax.axis_size("far"):
            value = pair_sum(offs, value, far_swap(value, bit))
            bit *= 2
        return value

    first_feed = feed(offs, hiddens, cots, 0, w_down, feed_pieces[0], down_pieces[0], deps=[feed_pieces[1][2]])
    down_send, down_keep = weight_grad(
        offs, ACT_AT, [first_feed[0]], [cots], (2, 2), "grad_down", deps=[down_pieces[1][0]]
    )
    down_came = swap(down_send, "near")
    gate_send, gate_send_own, gate_keep = weight_grad(
        offs, GRAD_AT, hiddens, [[first_feed[1]]], (1, 1, 2), "grad_gate_up"
    )
    gate_came, gate_came_own = swap(gate_send, "row"), swap(gate_send_own, "row")
    second_feed = feed(offs, hiddens, cots, 1, w_down, feed_pieces[1], down_pieces[1])
    gate_passed = swap(top_sum(offs, gate_keep, gate_came), "near")
    down_passed = swap(top_sum(offs, down_keep, down_came), "row")
    down_send_2, down_keep_2 = weight_grad(offs, ACT_AT, [second_feed[0]], [cots], (2, 2), "grad_down")
    down_came_2 = swap(down_send_2, "near")
    gate_send_2, gate_send_own_2, gate_keep_2 = weight_grad(
        offs, GRAD_AT, hiddens, [[second_feed[1]]], (1, 1, 2), "grad_gate_up"
    )
    gate_came_2, gate_came_own_2 = swap(gate_send_2, "row"), swap(gate_send_own_2, "row")
    acts, boths, fulls, downs = zip(first_feed, second_feed)
    gate_total = far_sum(rest_sum(offs, [(gate_keep, gate_came_own, gate_passed)]), None)
    ghidden_part = feed_back(boths[0], boths[1], fulls[0], fulls[1])
    ghidden_other = swap(ghidden_part, "core")
    down_sum = rest_sum(offs, [(down_keep, down_came, down_passed)])
    down_far = far_swap(down_sum, 1)
    gmiddle, gbranch, gmixed, _ = middle_back(
        boths[0], boths[1], ghidden_other, middle, cotangent, vec, fulls[0], fulls[1], full_output
    )
    gate_passed_2 = swap(top_sum(offs, gate_keep_2, gate_came_2), "near")
    down_passed_2 = swap(top_sum(offs, down_keep_2, down_came_2), "row")
    down_sum = pair_sum(offs, down_sum, down_far)
    down_far = far_swap(down_sum, 2)

    output_send, output_keep = weight_grad(offs, OWNER_AT, [mixed], [[gbranch]], (2, 2), "grad_output")
    output_came = swap(output_send, "core")
    ggate, gconv, gfilter = conv_back(values, gmixed, gates, vec, seg)
    filter_came = swap(gfilter, "core")
    convgate_send, convgate_keep = weight_grad(
        offs, OWNER_AT, [hidden_one], [[ggate]], (2, 2), "grad_convgate", deps=[output_came]
    )
    convgate_came = swap(convgate_send, "core")
    gate_total_2 = far_sum(rest_sum(offs, [(gate_keep_2, gate_came_own_2, gate_passed_2)]), gate_total)
    attended = attend_back(
        queries, keys, values, gmixed, attention, recips, gconv, seg, 0, pairs, deps=[filter_came]
    )
    early_give, early_held = halves_sum(
        offs, [(output_keep, output_came), (convgate_keep, convgate_came), (gfilter, filter_came)], True
    )
    early_came = swap(early_give, "row")
    down_sum_2 = rest_sum(offs, [(down_keep_2, down_came_2, down_passed_2)])
    down_far_2 = far_swap(down_sum_2, 1)
    down_sum = far_rest(down_sum, down_far)
    down_other = swap(down_sum, "near")
    gqk, gv = attend_back(
        queries, keys, values, gmixed, attention, recips, gconv, seg, pairs, pairs, onto=attended
    )
    down_sum_2 = pair_sum(offs, down_sum_2, down_far_2)
    down_far_2 = far_swap(down_sum_2, 2)
    early_own, early_other = near_split(offs, early_held, early_came)
    early_passed = swap(early_other, "near")
    late_send, late_keep = weight_grad(offs, OWNER_AT, [hidden_one], [[gqk], [gv]], (2, 2), "grad_query_key_value")
    late_came = swap(late_send, "core")
    grad_tokens, _ = tokens_back(gqk, gv, ggate, tokens, gmiddle, vec, full_one)
    late_give, late_held = halves_sum(offs, [(late_keep, late_came)])
    late_came = swap(late_give, "row")
    early = pair_sum(offs, early_own, early_passed)
    early_far = far_swap(early, 1)
    out_part = feed_out(acts[0], acts[1], downs[0], downs[1], 1, [], "feed_out_partner")
    out_came = swap(out_part, "core")
    down_sum_2 = far_rest(down_sum_2, down_far_2)
    down_other_2 = swap(down_sum_2, "near")
    gate_other = swap(gate_total, "near")
    early = pair_sum(offs, early, early_far)
    early_far = far_swap(early, 2)
    late_own, late_other = near_split(offs, late_held, late_came)
    late_passed = swap(late_other, "near")
    result = feed_out(acts[0], acts[1], downs[0], downs[1], 0, [middle, out_came], "feed_out")
    own_rows, theirs = sort_rows(offs, gate_total, gate_other)
    spreads = [own_rows, swap(theirs, "core")]
    late = pair_sum(offs, late_own, late_passed)
    late_far = far_swap(late, 1)
    gate_other = swap(gate_total_2, "near")
    early = far_rest(early, early_far)
    early_other = swap(early, "near")
    late = pair_sum(offs, late, late_far)
    late_far = far_swap(late, 2)
    own_rows, theirs = sort_rows(offs, gate_total_2, gate_other)
    spreads += [own_rows, swap(theirs, "core")]
    late = far_rest(late, late_far)
    late_other = swap(late, "near")
    grad_gate, grad_up, ggain_two = spread(offs, gain_two[:, None].astype(wide), w_gate, w_up, spreads)

    grad_down = jnp.concatenate(
        [in_order(x, down_sum, down_other), in_order(x, down_sum_2, down_other_2)], 0
    ).astype(wide)
    early = in_order(x, early, early_other).astype(wide)
    late = in_order(x, late, late_other).astype(wide)
    heads = HEADS * FEAT
    quarters = [late[:, n * heads // 2 : (n + 1) * heads // 2] for n in range(4)]
    grads = (
        jnp.concatenate([quarters[0], quarters[2]], 1),
        jnp.concatenate([quarters[1], quarters[3]], 1),
        late[:, 2 * heads :],
        early[:, width : 2 * width],
    )
    ggain_one = sum(
        jnp.sum(g * w.astype(wide), axis=1) for g, w in zip(grads, (w_query, w_key, w_value, w_convgate))
    ) / gain_one.astype(wide)
    return (
        result,
        grad_tokens,
        ggain_one,
        *grads,
        early[:, :width],
        early[:, 2 * width : 2 * width + KW].T,
        ggain_two[:, 0],
        grad_gate,
        grad_up,
        grad_down,
    )


def solution(mesh):
    replicas, shards = mesh.shape["rep"], mesh.shape["shard"]
    devices = np.asarray(mesh.devices).reshape(replicas // 2, 2, shards // 2, 2)
    fine = Mesh(devices, ("far", "near", "row", "core"))
    token = P(("far", "near", "row", "core"), None)
    line = P(("row", "core"))
    weight = P(("row", "core"), None)
    taps = P(None, ("row", "core"))
    return jax.shard_map(
        per_device,
        mesh=fine,
        in_specs=(
            token, token, line, weight, weight, weight, weight, weight, taps, line, weight, weight, weight, token
        ),
        out_specs=(
            token, token, line, weight, weight, weight, weight, weight, taps, line, weight, weight, weight
        ),
        check_vma=False,
    )
```

time: 1290 us -> 716 us (0.56); the launches traced: 1270 us -> 712 us
  matrix products: 459 us -> 0 us
  Pallas kernels: 0 us -> 382 us
  waiting for transfers between devices: 571 us -> 230 us
  local copies, waits for them, and re-layouts: 106 us -> 26.1 us
  blocking collectives: 63.8 us -> 0 us
  starting transfers between devices: 0.82 us -> 48.9 us
  other arithmetic: 51.9 us -> 10.6 us
    dot_general x136 -> x0, matrix products: 459 us -> none  [the longest x56 193 us: contract_cols(): lax.dot_general(first_arr, second_arr, (((1,), (1,)), ((), ())), preferre...]
    pallas_call x0 -> x49, Pallas kernels: none -> 382 us  [call(): result = run(*operands, *deps)]
    reduce_scatter x8 -> x0, waiting for transfers between devices: 298 us -> none  [the longest x1 74.4 us: per_device(): lax.psum_scatter(mlp_done[1].astype(jnp.bfloat16), 'shard', scatter_dimen...]
    ppermute x0 -> x57, waiting for transfers between devices: none -> 171 us  [the longest x49 117 us: swap(): return lax.ppermute(value, axis, [(0, 1), (1, 0)])]
    psum x1 -> x2, waiting for transfers between devices: 224 us -> 58.6 us  [far_sum(): return lax.psum(after(part, previous), 'far')]
    ppermute x0 -> x57, starting transfers between devices: none -> 48.8 us  [the longest x49 37.6 us: swap(): return lax.ppermute(value, axis, [(0, 1), (1, 0)])]
    all_gather x6 -> x0, waiting for transfers between devices: 45.2 us -> none  [the longest x1 43.6 us: per_device(): lax.all_gather(w_down, 'shard', axis=0, tiled=True)]
    all_gather x5 -> x0, blocking collectives: 35.3 us -> none  [the longest x1 10.8 us: per_device(): lax.all_gather(w_query, 'shard', axis=0, tiled=True)]
  transfers between devices with their start and end apart: 16 -> 59, of which waited for: 9 -> 17; matrix products, arithmetic and copies ran while one was open for 22% -> 2% of each run, Pallas kernels for 0% -> 44%
where the time goes in v1:
time: 716 us; the launch traced here: 712 us
  Pallas kernels  382 us (53%)
  waiting for transfers between devices  230 us (32%)
  starting transfers between devices  48.9 us (7%)
  local copies, waits for them, and re-layouts  26.1 us (4%)
  between operations  15 us (2%)
  other arithmetic  10.6 us (1%)
    pallas_call x49, Pallas kernels, call(): result = run(*operands, *deps)  382 us
    ppermute x49, waiting for transfers between devices, swap(): return lax.ppermute(value, axis, [(0, 1), (1, 0)])  117 us
    psum x2, waiting for transfers between devices, far_sum(): return lax.psum(after(part, previous), 'far')  58.6 us
    ppermute x8, waiting for transfers between devices, far_swap(): return lax.ppermute(value, 'far', [(i, i ^ bit) for i in range(count)])  54 us
    ppermute x49, starting transfers between devices, swap(): return lax.ppermute(value, axis, [(0, 1), (1, 0)])  37.6 us
    unnamed x106, local copies, waits for them, and re-layouts  21.1 us
  transfers between devices with their start and end apart: 59, of which 17 were waited for; matrix products, arithmetic and copies ran while one was open for 2% of the time, Pallas kernels for 44%

profile of v1, /device:TPU:0, one launch (start us, length us, event | category | flops | bytes accessed | tf_op | source)
XLA Modules:
  0.0 712.3 jit_solution(4388858884234139045)
XLA Ops:
  10.4 3.7 pack_mixer.1
  14.1 6.5 pack_feed.1
  24.1 16.5 %collective-permute-done.1.refs_4_ = bf16[128,2688]{1,0:T(8,128)(2,1)} collective-permute-done((bf16[128,2688]{1,0:T(8,128)(2,1)}, bf16[128,2688]{1,0:T(8,128)(2,1)}, u32[]{:S(2)}, u32[]{:S(2)}) %collective-permute-start.1) | collective-permute-done | bytes 688160 | tf_op jit(solution)/shard_map/ppermute | solution.py:886
  47.6 9.6 %collective-permute-done.2.refs_5_ = bf16[128,2688]{1,0:T(8,128)(2,1)} collective-permute-done((bf16[128,2688]{1,0:T(8,128)(2,1)}, bf16[128,2688]{1,0:T(8,128)(2,1)}, u32[]{:S(2)}, u32[]{:S(2)}) %collective-permute-start.2) | collective-permute-done | bytes 688160 | tf_op jit(solution)/shard_map/ppermute | solution.py:886
  58.6 4.5 pick.1
  69.6 13.0 %project.1 = (bf16[1024,1024]{1,0:T(8,128)(2,1)}, bf16[1024,256]{1,0:T(8,128)(2,1)}, bf16[1024,256]{1,0:T(8,128)(2,1)}, bf16[1024,1024]{1,0:T(8,128)(2,1)}, bf16...) custom-call(s32[44]{0:T(128)} %stack.133.refs_0_, bf16[1024,1024]{1,0:T(8,128)(2,1)} %refs_3_.10, ...), custom_call_target="tpu_custom_call" | custom-call | flops 4200000000 | bytes 13841203 | tf_op jit(solution)/shard_map/project/pallas_call | solution.py:60
  83.3 11.6 %attention_forward.2 = (bf16[1024,1024]{1,0:T(8,128)(2,1)}, bf16[1024,1024]{1,0:T(8,128)(2,1)}, bf16[1024,1024]{1,0:T(8,128)(2,1)}) custom-call(bf16[1024,256]{1,0:T(8,128)(2,1)} %get-tuple-element.97.refs_0_, bf16[1024,256]{1,0:T(8,128)(2,1)} %get-tuple-element.98.refs_1_, bf16[1024,1024]{1,0:T(8,128)(2,1)} %get-tuple-element.99.refs_2_.refs_0_, ...), custom_call_target="tpu_custom_call" | custom-call | flops 5400000000 | bytes 8808038 | tf_op jit(solution)/shard_map/attention_forward/pallas_call | solution.py:60
  98.7 11.7 %attention_forward.3 = (bf16[1024,1024]{1,0:T(8,128)(2,1)}, bf16[1024,1024]{1,0:T(8,128)(2,1)}, bf16[1024,1024]{1,0:T(8,128)(2,1)}) custom-call(bf16[1024,256]{1,0:T(8,128)(2,1)} %get-tuple-element.97.refs_0_, bf16[1024,256]{1,0:T(8,128)(2,1)} %get-tuple-element.98.refs_1_, ...), custom_call_target="tpu_custom_call", output_to_operand_aliasing={{0}: (7, {}), {1}: (8, {}), {2}: (9, {})} | custom-call | flops 5400000000 | bytes 8808038 | tf_op jit(solution)/shard_map/attention_forward/pallas_call | solution.py:60
  111.2 8.7 %mix.1 = (f32[1024,1024]{1,0:T(8,128)}, bf16[1024,1024]{1,0:T(8,128)(2,1)}, bf16[1024,1024]{1,0:T(8,128)(2,1)}) custom-call(s32[44]{0:T(128)} %stack.133.refs_0_, bf16[1024,1024]{1,0:T(8,128)(2,1)} %refs_3_.10, bf16[1024,1024]{1,0:T(8,128)(2,1)} %get-tuple-element.106.refs_2_.refs_11_.refs_1_.refs_3_.refs_4_, ...), custom_call_target="tpu_custom_call" | custom-call | flops 1800000000 | bytes 10066329 | tf_op jit(solution)/shard_map/mix/pallas_call | solution.py:60
  124.0 32.9 %collective-permute-done.19.refs_7_.refs_10_ = bf16[256,1024]{1,0:T(8,128)(2,1)S(1)} collective-permute-done((bf16[256,1024]{1,0:T(8,128)(2,1)}, bf16[256,1024]{1,0:T(8,128)(2,1)S(1)}, u32[]{:S(2)}, u32[]{:S(2)}) %collective-permute-start.19) | collective-permute-done | bytes 524320 | tf_op jit(solution)/shard_map/ppermute | solution.py:886
  161.0 23.5 %feed_in.2 = (bf16[2048,1024]{1,0:T(8,128)(2,1)}, bf16[2048,2048]{1,0:T(8,128)(2,1)}, bf16[1024,2048]{1,0:T(8,128)(2,1)}, bf16[1024,1024]{1,0:T(8,128)(2,1)}) custom-call(s32[44]{0:T(128)} %stack.133.refs_0_, bf16[1024,1024]{1,0:T(8,128)(2,1)} %get-tuple-element.108.refs_1_.refs_3_.refs_5_.refs_7_, bf16[1024,1024]{1,0:T(8,128)(2,1)} %copy-done, ...), custom_call_target="tpu_custom_call" | custom-call | flops 9600000000 | bytes 21390950 | tf_op jit(solution)/shard_map/feed_in/pallas_call | solution.py:60
  184.5 9.5 %grad_down.2 = (bf16[512,1024]{1,0:T(8,128)(2,1)}, bf16[512,1024]{1,0:T(8,128)(2,1)}) custom-call(s32[44]{0:T(128)} %stack.133.refs_0_, bf16[2048,1024]{1,0:T(8,128)(2,1)} %get-tuple-element.111.refs_1_.refs_2_.refs_3_.refs_4_.refs_8_.refs_0_, bf16[2048,1024]{1,0:T(8,128)(2,1)} %get-tuple-element.111.refs_1_.refs_2_.refs_3_.refs_4_.refs_8_.refs_0_, ...), custom_call_target="tpu_custom_call" | custom-call | flops 3221225472 | bytes 6291456 | tf_op jit(solution)/shard_map/grad_down/pallas_call | solution.py:60
  194.0 14.2 %grad_gate_up.2 = (bf16[256,2048]{1,0:T(8,128)(2,1)}, bf16[256,2048]{1,0:T(8,128)(2,1)}, bf16[512,2048]{1,0:T(8,128)(2,1)}) custom-call(s32[44]{0:T(128)} %stack.133.refs_0_, bf16[1024,1024]{1,0:T(8,128)(2,1)} %get-tuple-element.108.refs_1_.refs_3_.refs_5_.refs_7_, bf16[1024,1024]{1,0:T(8,128)(2,1)} %copy-done, ...), custom_call_target="tpu_custom_call" | custom-call | flops 6442450944 | bytes 10066329 | tf_op jit(solution)/shard_map/grad_gate_up/pallas_call | solution.py:60
  211.6 23.5 %feed_in.3 = (bf16[2048,1024]{1,0:T(8,128)(2,1)}, bf16[2048,2048]{1,0:T(8,128)(2,1)}, bf16[1024,2048]{1,0:T(8,128)(2,1)}, bf16[1024,1024]{1,0:T(8,128)(2,1)}) custom-call(s32[44]{0:T(128)} %stack.133.refs_0_, bf16[1024,1024]{1,0:T(8,128)(2,1)} %get-tuple-element.108.refs_1_.refs_3_.refs_5_.refs_7_, bf16[1024,1024]{1,0:T(8,128)(2,1)} %copy-done, ...), custom_call_target="tpu_custom_call" | custom-call | flops 9600000000 | bytes 21390950 | tf_op jit(solution)/shard_map/feed_in/pallas_call | solution.py:60
  235.2 3.7 top_sum.4.refs_3_
  243.8 9.1 %grad_down.3 = (bf16[512,1024]{1,0:T(8,128)(2,1)}, bf16[512,1024]{1,0:T(8,128)(2,1)}) custom-call(s32[44]{0:T(128)} %stack.133.refs_0_, bf16[2048,1024]{1,0:T(8,128)(2,1)} %get-tuple-element.116.refs_3_.refs_1_.refs_2_.refs_4_, bf16[2048,1024]{1,0:T(8,128)(2,1)} %get-tuple-element.116.refs_3_.refs_1_.refs_2_.refs_4_, ...), custom_call_target="tpu_custom_call" | custom-call | flops 3221225472 | bytes 6291456 | tf_op jit(solution)/shard_map/grad_down/pallas_call | solution.py:60
  253.0 14.0 %grad_gate_up.3 = (bf16[256,2048]{1,0:T(8,128)(2,1)}, bf16[256,2048]{1,0:T(8,128)(2,1)}, bf16[512,2048]{1,0:T(8,128)(2,1)}) custom-call(s32[44]{0:T(128)} %stack.133.refs_0_, bf16[1024,1024]{1,0:T(8,128)(2,1)} %get-tuple-element.108.refs_1_.refs_3_.refs_5_.refs_7_, bf16[1024,1024]{1,0:T(8,128)(2,1)} %copy-done, ...), custom_call_target="tpu_custom_call" | custom-call | flops 6442450944 | bytes 10066329 | tf_op jit(solution)/shard_map/grad_gate_up/pallas_call | solution.py:60
  268.0 4.2 rest_sum.4.refs_4_
  272.2 14.6 %feed_back_partner.1.refs_4_ = bf16[1024,1024]{1,0:T(8,128)(2,1)} custom-call(bf16[2048,2048]{1,0:T(8,128)(2,1)} %get-tuple-element.113.refs_9_.refs_0_, bf16[2048,2048]{1,0:T(8,128)(2,1)} %get-tuple-element.119.refs_9_.refs_1_, bf16[1024,2048]{1,0:T(8,128)(2,1)} %get-tuple-element.120.refs_2_.refs_6_, ...), custom_call_target="tpu_custom_call" | custom-call | flops 6000000000 | bytes 11324620 | tf_op jit(solution)/shard_map/feed_back_partner/pallas_call | solution.py:60
  290.1 11.5 %collective-permute-done.26.refs_3_ = bf16[256,1024]{1,0:T(8,128)(2,1)S(1)} collective-permute-done((bf16[256,1024]{1,0:T(8,128)(2,1)S(1)}, bf16[256,1024]{1,0:T(8,128)(2,1)S(1)}, u32[]{:S(2)}, u32[]{:S(2)}) %collective-permute-start.26) | collective-permute-done | bytes 524320 | tf_op jit(solution)/shard_map/ppermute | solution.py:886
  302.4 3.3 rest_sum.5.refs_9_.refs_1_
  307.3 20.3 %middle_back.1 = (f32[1024,1024]{1,0:T(8,128)}, bf16[1024,1024]{1,0:T(8,128)(2,1)}, bf16[1024,1024]{1,0:T(8,128)(2,1)}, f32[8,1024]{1,0:T(8,128)}) custom-call(bf16[2048,2048]{1,0:T(8,128)(2,1)} %get-tuple-element.113.refs_9_.refs_0_, bf16[2048,2048]{1,0:T(8,128)(2,1)} %get-tuple-element.119.refs_9_.refs_1_, ...), custom_call_target="tpu_custom_call" | custom-call | flops 7800000000 | bytes 25165824 | tf_op jit(solution)/shard_map/middle_back/pallas_call | solution.py:60
  327.7 3.7 top_sum.6.refs_3_
  339.1 6.1 grad_output.1
  347.9 10.9 %convolution_backward.1 = (bf16[1024,1024]{1,0:T(8,128)(2,1)}, bf16[1024,1024]{1,0:T(8,128)(2,1)}, bf16[1024,128]{1,0:T(8,128)(2,1)}) custom-call(bf16[1024,1024]{1,0:T(8,128)(2,1)} %get-tuple-element.99.refs_2_.refs_0_, bf16[1024,1024]{1,0:T(8,128)(2,1)} %get-tuple-element.134.refs_1_.refs_3_, bf16[1024,1024]{1,0:T(8,128)(2,1)} %get-tuple-element.100.refs_3_.refs_2_, ...), custom_call_target="tpu_custom_call" | custom-call | flops 600000000 | bytes 6291456 | tf_op jit(solution)/shard_map/convolution_backward/pallas_call | solution.py:60
  362.1 6.0 grad_convgate.1
  368.1 3.4 collective-permute-done.33.refs_2_
  372.2 4.1 rest_sum.6.refs_10_
  377.0 21.0 %attention_backward.2 = (bf16[1024,512]{1,0:T(8,128)(2,1)}, bf16[1024,1024]{1,0:T(8,128)(2,1)}) custom-call(bf16[1024,256]{1,0:T(8,128)(2,1)} %get-tuple-element.97.refs_0_, bf16[1024,256]{1,0:T(8,128)(2,1)} %get-tuple-element.98.refs_1_, bf16[1024,1024]{1,0:T(8,128)(2,1)} %get-tuple-element.99.refs_2_.refs_0_, ...), custom_call_target="tpu_custom_call" | custom-call | flops 12000000000 | bytes 11324620 | tf_op jit(solution)/shard_map/attention_backward/pallas_call | solution.py:60
  399.0 4.8 halves_sum.2
  404.7 3.3 rest_sum.7.refs_3_.refs_1_
  411.3 20.8 %attention_backward.3 = (bf16[1024,512]{1,0:T(8,128)(2,1)}, bf16[1024,1024]{1,0:T(8,128)(2,1)}) custom-call(bf16[1024,256]{1,0:T(8,128)(2,1)} %get-tuple-element.97.refs_0_, bf16[1024,256]{1,0:T(8,128)(2,1)} %get-tuple-element.98.refs_1_, bf16[1024,1024]{1,0:T(8,128)(2,1)} %get-tuple-element.99.refs_2_.refs_0_, ...), custom_call_target="tpu_custom_call", output_to_operand_aliasing={{0}: (9, {}), {1}: (10, {})} | custom-call | flops 12000000000 | bytes 11324620 | tf_op jit(solution)/shard_map/attention_backward/pallas_call | solution.py:60
  436.7 3.4 near_split.2
  440.1 8.5 %grad_query_key_value.1 = (bf16[512,1536]{1,0:T(8,128)(2,1)}, bf16[512,1536]{1,0:T(8,128)(2,1)}) custom-call(s32[44]{0:T(128)} %stack.133.refs_0_, bf16[1024,1024]{1,0:T(8,128)(2,1)} %get-tuple-element.102.refs_9_.refs_1_.refs_2_.refs_3_.refs_4_, bf16[1024,1024]{1,0:T(8,128)(2,1)} %get-tuple-element.102.refs_9_.refs_1_.refs_2_.refs_3_.refs_4_, ...), custom_call_target="tpu_custom_call" | custom-call | flops 2415919104 | bytes 5033164 | tf_op jit(solution)/shard_map/grad_query_key_value/pallas_call | solution.py:60
  449.8 13.9 %tokens_back.1 = (f32[1024,1024]{1,0:T(8,128)}, f32[8,1024]{1,0:T(8,128)}) custom-call(bf16[1024,512]{1,0:T(8,128)(2,1)} %get-tuple-element.147.refs_3_.refs_5_.refs_0_, bf16[1024,1024]{1,0:T(8,128)(2,1)} %get-tuple-element.150.refs_6_.refs_1_, bf16[1024,1024]{1,0:T(8,128)(2,1)} %get-tuple-element.135.refs_5_.refs_7_.refs_2_, bf16[1024,1024]{1,0:T(8,128)(2,1)} %refs_3_.10, ...), custom_call_target="tpu_custom_call" | custom-call | flops 4200000000 | bytes 15099494 | tf_op jit(solution)/shard_map/tokens_back/pallas_call | solution.py:60
  464.8 3.9 halves_sum.3
  472.3 8.7 %feed_out_partner.1.refs_3_ = bf16[1024,1024]{1,0:T(8,128)(2,1)} custom-call(bf16[2048,1024]{1,0:T(8,128)(2,1)} %get-tuple-element.111.refs_1_.refs_2_.refs_3_.refs_4_.refs_8_.refs_0_, bf16[2048,1024]{1,0:T(8,128)(2,1)} %get-tuple-element.116.refs_3_.refs_1_.refs_2_.refs_4_, bf16[1024,1024]{1,0:T(8,128)(2,1)} %get-tuple-element.117.refs_2_, ...), custom_call_target="tpu_custom_call" | custom-call | flops 3000000000 | bytes 10066329 | tf_op jit(solution)/shard_map/feed_out_partner/pallas_call | solution.py:60
  481.2 20.8 %all-reduce.3.cloned.1.call-done.refs_1_ = bf16[256,2048]{1,0:T(8,128)(2,1)} async-done(((bf16[256,2048]{1,0:T(8,128)(2,1)}), bf16[256,2048]{1,0:T(8,128)(2,1)}) %all-reduce.3.cloned.1.call-update) | async-done | bytes 1048592 | tf_op jit(solution)/shard_map/psum | solution.py:987
  507.4 38.2 %collective-permute-done.44.refs_2_ = bf16[256,1024]{1,0:T(8,128)(2,1)} collective-permute-done((bf16[256,1024]{1,0:T(8,128)(2,1)S(1)}, bf16[256,1024]{1,0:T(8,128)(2,1)}, u32[]{:S(2)}, u32[]{:S(2)}) %collective-permute-start.44) | collective-permute-done | bytes 524320 | tf_op jit(solution)/shard_map/ppermute | solution.py:993
  552.0 3.5 collective-permute-start.48
  555.5 37.8 %all-reduce.5.cloned.1.call-done.refs_1_ = bf16[256,2048]{1,0:T(8,128)(2,1)} async-done(((bf16[256,2048]{1,0:T(8,128)(2,1)}), bf16[256,2048]{1,0:T(8,128)(2,1)}) %all-reduce.5.cloned.1.call-update) | async-done | bytes 1048592 | tf_op jit(solution)/shard_map/psum | solution.py:987
  600.4 10.0 %feed_out.1.refs_3_ = bf16[1024,1024]{1,0:T(8,128)(2,1)} custom-call(bf16[2048,1024]{1,0:T(8,128)(2,1)} %get-tuple-element.111.refs_1_.refs_2_.refs_3_.refs_4_.refs_8_.refs_0_, bf16[2048,1024]{1,0:T(8,128)(2,1)} %get-tuple-element.116.refs_3_.refs_1_.refs_2_.refs_4_, bf16[1024,1024]{1,0:T(8,128)(2,1)} %get-tuple-element.117.refs_2_, ...), custom_call_target="tpu_custom_call" | custom-call | flops 3000000000 | bytes 10066329 | tf_op jit(solution)/shard_map/feed_out/pallas_call | solution.py:60
  610.4 3.7 sort_rows.2
  614.1 25.1 %collective-permute-done.45.refs_2_ = bf16[128,1536]{1,0:T(8,128)(2,1)S(1)} collective-permute-done((bf16[128,1536]{1,0:T(8,128)(2,1)}, bf16[128,1536]{1,0:T(8,128)(2,1)S(1)}, u32[]{:S(2)}, u32[]{:S(2)}) %collective-permute-start.45) | collective-permute-done | bytes 393248 | tf_op jit(solution)/shard_map/ppermute | solution.py:886
  660.0 4.0 sort_rows.3
  664.1 13.2 %collective-permute-done.49.refs_2_ = bf16[128,1536]{1,0:T(8,128)(2,1)S(1)} collective-permute-done((bf16[128,1536]{1,0:T(8,128)(2,1)}, bf16[128,1536]{1,0:T(8,128)(2,1)S(1)}, u32[]{:S(2)}, u32[]{:S(2)}) %collective-permute-start.49) | collective-permute-done | bytes 393248 | tf_op jit(solution)/shard_map/ppermute | solution.py:993
  684.2 7.8 %collective-permute-done.51 = bf16[128,1536]{1,0:T(8,128)(2,1)S(1)} collective-permute-done((bf16[128,1536]{1,0:T(8,128)(2,1)}, bf16[128,1536]{1,0:T(8,128)(2,1)S(1)}, u32[]{:S(2)}, u32[]{:S(2)}) %collective-permute-start.51) | collective-permute-done | bytes 393248 | tf_op jit(solution)/shard_map/ppermute | solution.py:886
  694.8 8.5 %spread.1 = (f32[256,4096]{1,0:T(8,128)}, f32[256,4096]{1,0:T(8,128)}, f32[256,1]{1,0:T(8,128)}) custom-call(s32[44]{0:T(128)} %stack.133.refs_0_, f32[256,1]{1,0:T(8,128)} %copy.38.refs_1_, bf16[256,4096]{1,0:T(8,128)(2,1)} %refs_2_.3, bf16[256,4096]{1,0:T(8,128)(2,1)} %refs_3_.11, bf16[256,2048]{1,0:T(8,128)(2,1)} %get-tuple-element.159.refs_3_.refs_4_, ...), custom_call_target="tpu_custom_call" | custom-call | flops 600000 | bytes 10066329 | tf_op jit(solution)/shard_map/spread/pallas_call | solution.py:60
  (245 shorter events, 131.9 us)
Async XLA Ops:
  20.6 36.7 %collective-permute-start.8 = (bf16[512,2048]{1,0:T(8,128)(2,1)}, bf16[512,2048]{1,0:T(8,128)(2,1)}, u32[]{:S(2)}, u32[]{:S(2)}) collective-permute-start(bf16[512,2048]{1,0:T(8,128)(2,1)} %get-tuple-element.95), channel_id=1, source_target_pairs={{0,1},{1,0},{2,3},{3,2},{4,5},{5,4},{6,7},{7,6},{8,9},{9,8},{10,11... | collective-permute-start | bytes 6291464 | tf_op jit(solution)/shard_map/ppermute | solution.py:886
  21.0 48.5 %collective-permute-start.5 = (bf16[1024,1024]{1,0:T(8,128)(2,1)S(1)}, bf16[1024,1024]{1,0:T(8,128)(2,1)}, u32[]{:S(2)}, u32[]{:S(2)}) collective-permute-start(bf16[1024,1024]{1,0:T(8,128)(2,1)S(1)} %copy-done.1), channel_id=1, source_target_pairs={{0,1},{1,0},{2,3},{3,2},{4,5},{5,4},{6,7},{7,6},{8,9},{9,8},{10,11... | collective-permute-start | bytes 6291464 | tf_op jit(solution)/shard_map/ppermute | solution.py:886
  21.1 19.5 %collective-permute-start.1 = (bf16[128,2688]{1,0:T(8,128)(2,1)}, bf16[128,2688]{1,0:T(8,128)(2,1)}, u32[]{:S(2)}, u32[]{:S(2)}) collective-permute-start(bf16[128,2688]{1,0:T(8,128)(2,1)} %get-tuple-element.91), channel_id=1, source_target_pairs={{0,2},{2,0},{1,3},{3,1},{4,6},{6,4},{5,7},{7,5},{8,10},{10,8},{9,1... | collective-permute-start | bytes 2064392 | tf_op jit(solution)/shard_map/ppermute | solution.py:886
  24.1 21.5 %collective-permute-start.7 = (bf16[128,1024]{1,0:T(8,128)(2,1)S(1)}, bf16[128,1024]{1,0:T(8,128)(2,1)S(1)}, u32[]{:S(2)}, u32[]{:S(2)}) collective-permute-start(bf16[128,1024]{1,0:T(8,128)(2,1)S(1)} %copy-done.50), channel_id=1, source_target_pairs={{0,2},{2,0},{1,3},{3,1},{4,6},{6,4},{5,7},{7,5},{8,10},{10,8},{9,1... | collective-permute-start | bytes 786440 | tf_op jit(solution)/shard_map/ppermute | solution.py:886
  24.1 44.9 %collective-permute-start = (bf16[256,2688]{1,0:T(8,128)(2,1)}, bf16[256,2688]{1,0:T(8,128)(2,1)}, u32[]{:S(2)}, u32[]{:S(2)}) collective-permute-start(bf16[256,2688]{1,0:T(8,128)(2,1)} %get-tuple-element.90.refs_4_.refs_2_), channel_id=1, source_target_pairs={{0,1},{1,0},{2,3},{3,2},{4,5},{5,4},{6,7},{7,6},{8,9},{9,8},{10,11... | collective-permute-start | bytes 4128776 | tf_op jit(solution)/shard_map/ppermute | solution.py:886
  47.5 21.0 %collective-permute-start.3 = (bf16[128,2688]{1,0:T(8,128)(2,1)}, bf16[128,2688]{1,0:T(8,128)(2,1)}, u32[]{:S(2)}, u32[]{:S(2)}) collective-permute-start(bf16[128,2688]{1,0:T(8,128)(2,1)} %collective-permute-done.1.refs_4_), channel_id=1, source_target_pairs={{0,1},{1,0},{2,3},{3,2},{4,5},{5,4},{6,7},{7,6},{8,9},{9,8},{10,11... | collective-permute-start | bytes 2064392 | tf_op jit(solution)/shard_map/ppermute | solution.py:886
  66.0 32.0 %collective-permute-start.11 = (bf16[256,2048]{1,0:T(8,128)(2,1)}, bf16[256,2048]{1,0:T(8,128)(2,1)}, u32[]{:S(2)}, u32[]{:S(2)}) collective-permute-start(bf16[256,2048]{1,0:T(8,128)(2,1)} %get-tuple-element.96.refs_11_), channel_id=1, source_target_pairs={{0,2},{2,0},{1,3},{3,1},{4,6},{6,4},{5,7},{7,5},{8,10},{10,8},{9,1... | collective-permute-start | bytes 3145736 | tf_op jit(solution)/shard_map/ppermute | solution.py:886
  68.4 42.0 %collective-permute-start.13 = (bf16[256,1024]{1,0:T(8,128)(2,1)}, bf16[256,1024]{1,0:T(8,128)(2,1)S(1)}, u32[]{:S(2)}, u32[]{:S(2)}) collective-permute-start(bf16[256,1024]{1,0:T(8,128)(2,1)} %get-tuple-element.107), channel_id=1, source_target_pairs={{0,2},{2,0},{1,3},{3,1},{4,6},{6,4},{5,7},{7,5},{8,10},{10,8},{9,1... | collective-permute-start | bytes 1572872 | tf_op jit(solution)/shard_map/ppermute | solution.py:886
  69.1 28.9 %collective-permute-start.12 = (bf16[128,1024]{1,0:T(8,128)(2,1)}, bf16[128,1024]{1,0:T(8,128)(2,1)S(1)}, u32[]{:S(2)}, u32[]{:S(2)}) collective-permute-start(bf16[128,1024]{1,0:T(8,128)(2,1)} %copy-done.41), channel_id=1, source_target_pairs={{0,1},{1,0},{2,3},{3,2},{4,5},{5,4},{6,7},{7,6},{8,9},{9,8},{10,11... | collective-permute-start | bytes 786440 | tf_op jit(solution)/shard_map/ppermute | solution.py:886
  119.8 39.1 %collective-permute-start.14 = (bf16[1024,1024]{1,0:T(8,128)(2,1)}, bf16[1024,1024]{1,0:T(8,128)(2,1)S(1)}, u32[]{:S(2)}, u32[]{:S(2)}) collective-permute-start(bf16[1024,1024]{1,0:T(8,128)(2,1)} %get-tuple-element.108.refs_1_.refs_3_.refs_5_.refs_7_), channel_id=1, source_target_pairs={{0,1},{1,0},{2,3},{3,2},{4,5},{5,4},{6,7},{7,6},{8,9},{9,8},{10,11... | collective-permute-start | bytes 6291464 | tf_op jit(solution)/shard_map/ppermute | solution.py:886
  119.9 38.4 %collective-permute-start.17 = (bf16[256,2048]{1,0:T(8,128)(2,1)}, bf16[256,2048]{1,0:T(8,128)(2,1)}, u32[]{:S(2)}, u32[]{:S(2)}) collective-permute-start(bf16[256,2048]{1,0:T(8,128)(2,1)} %get-tuple-element.109), channel_id=1, source_target_pairs={{0,2},{2,0},{1,3},{3,1},{4,6},{6,4},{5,7},{7,5},{8,10},{10,8},{9,1... | collective-permute-start | bytes 3145736 | tf_op jit(solution)/shard_map/ppermute | solution.py:886
  121.3 37.6 %collective-permute-start.15 = (bf16[256,2048]{1,0:T(8,128)(2,1)}, bf16[256,2048]{1,0:T(8,128)(2,1)S(1)}, u32[]{:S(2)}, u32[]{:S(2)}) collective-permute-start(bf16[256,2048]{1,0:T(8,128)(2,1)} %collective-permute-done.11.refs_10_.refs_7_), channel_id=1, source_target_pairs={{0,4},{4,0},{1,5},{5,1},{2,6},{6,2},{3,7},{7,3},{8,12},{12,8},{9,1... | collective-permute-start | bytes 3145736 | tf_op jit(solution)/shard_map/ppermute | solution.py:886
  122.8 34.0 %collective-permute-start.19 = (bf16[256,1024]{1,0:T(8,128)(2,1)}, bf16[256,1024]{1,0:T(8,128)(2,1)S(1)}, u32[]{:S(2)}, u32[]{:S(2)}) collective-permute-start(bf16[256,1024]{1,0:T(8,128)(2,1)} %get-tuple-element.112), channel_id=1, source_target_pairs={{0,2},{2,0},{1,3},{3,1},{4,6},{6,4},{5,7},{7,5},{8,10},{10,8},{9,1... | collective-permute-start | bytes 1572872 | tf_op jit(solution)/shard_map/ppermute | solution.py:886
  123.3 35.6 %collective-permute-start.16 = (bf16[256,1024]{1,0:T(8,128)(2,1)}, bf16[256,1024]{1,0:T(8,128)(2,1)S(1)}, u32[]{:S(2)}, u32[]{:S(2)}) collective-permute-start(bf16[256,1024]{1,0:T(8,128)(2,1)} %copy-done.29), channel_id=1, source_target_pairs={{0,4},{4,0},{1,5},{5,1},{2,6},{6,2},{3,7},{7,3},{8,12},{12,8},{9,1... | collective-permute-start | bytes 1572872 | tf_op jit(solution)/shard_map/ppermute | solution.py:886
  156.9 54.8 %collective-permute-start.20 = (bf16[256,1024]{1,0:T(8,128)(2,1)S(1)}, bf16[256,1024]{1,0:T(8,128)(2,1)}, u32[]{:S(2)}, u32[]{:S(2)}) collective-permute-start(bf16[256,1024]{1,0:T(8,128)(2,1)S(1)} %collective-permute-done.19.refs_7_.refs_10_), channel_id=1, source_target_pairs={{0,4},{4,0},{1,5},{5,1},{2,6},{6,2},{3,7},{7,3},{8,12},{12,8},{9,1... | collective-permute-start | bytes 1572872 | tf_op jit(solution)/shard_map/ppermute | solution.py:886
  158.3 53.4 %collective-permute-start.18 = (bf16[256,2048]{1,0:T(8,128)(2,1)}, bf16[256,2048]{1,0:T(8,128)(2,1)}, u32[]{:S(2)}, u32[]{:S(2)}) collective-permute-start(bf16[256,2048]{1,0:T(8,128)(2,1)} %collective-permute-done.17.refs_12_.refs_7_), channel_id=1, source_target_pairs={{0,4},{4,0},{1,5},{5,1},{2,6},{6,2},{3,7},{7,3},{8,12},{12,8},{9,1... | collective-permute-start | bytes 3145736 | tf_op jit(solution)/shard_map/ppermute | solution.py:886
  208.2 27.0 %collective-permute-start.22 = (bf16[256,2048]{1,0:T(8,128)(2,1)}, bf16[256,2048]{1,0:T(8,128)(2,1)}, u32[]{:S(2)}, u32[]{:S(2)}) collective-permute-start(bf16[256,2048]{1,0:T(8,128)(2,1)} %get-tuple-element.115.refs_12_), channel_id=1, source_target_pairs={{0,2},{2,0},{1,3},{3,1},{4,6},{6,4},{5,7},{7,5},{8,10},{10,8},{9,1... | collective-permute-start | bytes 3145736 | tf_op jit(solution)/shard_map/ppermute | solution.py:886
  209.6 30.1 %collective-permute-start.24 = (bf16[512,1024]{1,0:T(8,128)(2,1)S(1)}, bf16[512,1024]{1,0:T(8,128)(2,1)S(1)}, u32[]{:S(2)}, u32[]{:S(2)}) collective-permute-start(bf16[512,1024]{1,0:T(8,128)(2,1)S(1)} %copy-done.24), channel_id=1, source_target_pairs={{0,4},{4,0},{1,5},{5,1},{2,6},{6,2},{3,7},{7,3},{8,12},{12,8},{9,1... | collective-permute-start | bytes 3145736 | tf_op jit(solution)/shard_map/ppermute | solution.py:886
  211.1 55.9 %collective-permute-start.21 = (bf16[256,2048]{1,0:T(8,128)(2,1)}, bf16[256,2048]{1,0:T(8,128)(2,1)S(1)}, u32[]{:S(2)}, u32[]{:S(2)}) collective-permute-start(bf16[256,2048]{1,0:T(8,128)(2,1)} %get-tuple-element.123), channel_id=1, source_target_pairs={{0,2},{2,0},{1,3},{3,1},{4,6},{6,4},{5,7},{7,5},{8,10},{10,8},{9,1... | collective-permute-start | bytes 3145736 | tf_op jit(solution)/shard_map/ppermute | solution.py:886
  238.9 28.2 %collective-permute-start.23 = (bf16[256,2048]{1,0:T(8,128)(2,1)}, bf16[256,2048]{1,0:T(8,128)(2,1)}, u32[]{:S(2)}, u32[]{:S(2)}) collective-permute-start(bf16[256,2048]{1,0:T(8,128)(2,1)} %top_sum.4.refs_3_), channel_id=1, source_target_pairs={{0,4},{4,0},{1,5},{5,1},{2,6},{6,2},{3,7},{7,3},{8,12},{12,8},{9,1... | collective-permute-start | bytes 3145736 | tf_op jit(solution)/shard_map/ppermute | solution.py:886
  286.8 215.2 %all-reduce.3.cloned.1.call-start = ((), (), s32[]{:S(2)}) async-start(), calls=%async_computation | async-start | bytes 2097152 | tf_op jit(solution)/shard_map/psum | solution.py:987
  286.8 20.5 %collective-permute-start.25 = (bf16[1024,1024]{1,0:T(8,128)(2,1)}, bf16[1024,1024]{1,0:T(8,128)(2,1)}, u32[]{:S(2)}, u32[]{:S(2)}) collective-permute-start(bf16[1024,1024]{1,0:T(8,128)(2,1)} %feed_back_partner.1.refs_4_), channel_id=1, source_target_pairs={{0,1},{1,0},{2,3},{3,2},{4,5},{5,4},{6,7},{7,6},{8,9},{9,8},{10,11... | collective-permute-start | bytes 6291464 | tf_op jit(solution)/shard_map/ppermute | solution.py:886
  288.4 39.3 %collective-permute-start.29 = (bf16[256,2048]{1,0:T(8,128)(2,1)}, bf16[256,2048]{1,0:T(8,128)(2,1)}, u32[]{:S(2)}, u32[]{:S(2)}) collective-permute-start(bf16[256,2048]{1,0:T(8,128)(2,1)} %get-tuple-element.126.refs_4_), channel_id=1, source_target_pairs={{0,2},{2,0},{1,3},{3,1},{4,6},{6,4},{5,7},{7,5},{8,10},{10,8},{9,1... | collective-permute-start | bytes 3145736 | tf_op jit(solution)/shard_map/ppermute | solution.py:886
  288.9 42.5 %collective-permute-start.28 = (bf16[512,1024]{1,0:T(8,128)(2,1)S(1)}, bf16[512,1024]{1,0:T(8,128)(2,1)S(1)}, u32[]{:S(2)}, u32[]{:S(2)}) collective-permute-start(bf16[512,1024]{1,0:T(8,128)(2,1)S(1)} %copy-done.21), channel_id=1, source_target_pairs={{0,4},{4,0},{1,5},{5,1},{2,6},{6,2},{3,7},{7,3},{8,12},{12,8},{9,1... | collective-permute-start | bytes 3145736 | tf_op jit(solution)/shard_map/ppermute | solution.py:886
  305.8 29.7 %collective-permute-start.27 = (bf16[256,1024]{1,0:T(8,128)(2,1)}, bf16[256,1024]{1,0:T(8,128)(2,1)S(1)}, u32[]{:S(2)}, u32[]{:S(2)}) collective-permute-start(bf16[256,1024]{1,0:T(8,128)(2,1)} %rest_sum.5.refs_9_.refs_1_), channel_id=1, source_target_pairs={{0,8},{8,0},{16,24},{24,16},{1,9},{9,1},{17,25},{25,17},{2,10},{10... | collective-permute-start | bytes 1572872 | tf_op jit(solution)/shard_map/ppermute | solution.py:993
  345.2 26.3 %collective-permute-start.33 = (bf16[256,2048]{1,0:T(8,128)(2,1)}, bf16[256,2048]{1,0:T(8,128)(2,1)}, u32[]{:S(2)}, u32[]{:S(2)}) collective-permute-start(bf16[256,2048]{1,0:T(8,128)(2,1)} %get-tuple-element.142), channel_id=1, source_target_pairs={{0,2},{2,0},{1,3},{3,1},{4,6},{6,4},{5,7},{7,5},{8,10},{10,8},{9,1... | collective-permute-start | bytes 3145736 | tf_op jit(solution)/shard_map/ppermute | solution.py:886
  346.8 25.4 %collective-permute-start.34 = (bf16[256,2048]{1,0:T(8,128)(2,1)S(1)}, bf16[256,2048]{1,0:T(8,128)(2,1)}, u32[]{:S(2)}, u32[]{:S(2)}) collective-permute-start(bf16[256,2048]{1,0:T(8,128)(2,1)S(1)} %copy-done.8), channel_id=1, source_target_pairs={{0,4},{4,0},{1,5},{5,1},{2,6},{6,2},{3,7},{7,3},{8,12},{12,8},{9,1... | collective-permute-start | bytes 3145736 | tf_op jit(solution)/shard_map/ppermute | solution.py:886
  358.9 45.8 %collective-permute-start.36 = (bf16[256,1024]{1,0:T(8,128)(2,1)S(1)}, bf16[256,1024]{1,0:T(8,128)(2,1)}, u32[]{:S(2)}, u32[]{:S(2)}) collective-permute-start(bf16[256,1024]{1,0:T(8,128)(2,1)S(1)} %copy-done.17), channel_id=1, source_target_pairs={{0,2},{2,0},{1,3},{3,1},{4,6},{6,4},{5,7},{7,5},{8,10},{10,8},{9,1... | collective-permute-start | bytes 1572872 | tf_op jit(solution)/shard_map/ppermute | solution.py:886
  359.4 49.1 %collective-permute-start.38 = (bf16[256,1024]{1,0:T(8,128)(2,1)S(1)}, bf16[256,1024]{1,0:T(8,128)(2,1)}, u32[]{:S(2)}, u32[]{:S(2)}) collective-permute-start(bf16[256,1024]{1,0:T(8,128)(2,1)S(1)} %copy-done.4), channel_id=1, source_target_pairs={{0,16},{8,24},{16,0},{24,8},{1,17},{9,25},{17,1},{25,9},{2,18},{10... | collective-permute-start | bytes 1572872 | tf_op jit(solution)/shard_map/ppermute | solution.py:993
  371.5 26.5 %collective-permute-start.31 = (bf16[512,1024]{1,0:T(8,128)(2,1)}, bf16[512,1024]{1,0:T(8,128)(2,1)S(1)}, u32[]{:S(2)}, u32[]{:S(2)}) collective-permute-start(bf16[512,1024]{1,0:T(8,128)(2,1)} %get-tuple-element.137.refs_4_), channel_id=1, source_target_pairs={{0,1},{1,0},{2,3},{3,2},{4,5},{5,4},{6,7},{7,6},{8,9},{9,8},{10,11... | collective-permute-start | bytes 3145736 | tf_op jit(solution)/shard_map/ppermute | solution.py:886
  403.9 31.8 %collective-permute-start.35 = (bf16[256,2176]{1,0:T(8,128)(2,1)}, bf16[256,2176]{1,0:T(8,128)(2,1)S(1)}, u32[]{:S(2)}, u32[]{:S(2)}) collective-permute-start(bf16[256,2176]{1,0:T(8,128)(2,1)} %get-tuple-element.145.refs_4_), channel_id=1, source_target_pairs={{0,2},{2,0},{1,3},{3,1},{4,6},{6,4},{5,7},{7,5},{8,10},{10,8},{9,1... | collective-permute-start | bytes 3342344 | tf_op jit(solution)/shard_map/ppermute | solution.py:886
  408.1 24.0 %collective-permute-start.37 = (bf16[256,1024]{1,0:T(8,128)(2,1)}, bf16[256,1024]{1,0:T(8,128)(2,1)S(1)}, u32[]{:S(2)}, u32[]{:S(2)}) collective-permute-start(bf16[256,1024]{1,0:T(8,128)(2,1)} %rest_sum.7.refs_3_.refs_1_), channel_id=1, source_target_pairs={{0,8},{8,0},{16,24},{24,16},{1,9},{9,1},{17,25},{25,17},{2,10},{10... | collective-permute-start | bytes 1572872 | tf_op jit(solution)/shard_map/ppermute | solution.py:993
  448.5 20.2 %collective-permute-start.39 = (bf16[128,2176]{1,0:T(8,128)(2,1)S(1)}, bf16[128,2176]{1,0:T(8,128)(2,1)S(1)}, u32[]{:S(2)}, u32[]{:S(2)}) collective-permute-start(bf16[128,2176]{1,0:T(8,128)(2,1)S(1)} %copy-done.48), channel_id=1, source_target_pairs={{0,4},{4,0},{1,5},{5,1},{2,6},{6,2},{3,7},{7,3},{8,12},{12,8},{9,1... | collective-permute-start | bytes 1671176 | tf_op jit(solution)/shard_map/ppermute | solution.py:886
  449.8 143.5 %all-reduce.5.cloned.1.call-start = ((), (), s32[]{:S(2)}) async-start(), calls=%async_computation.1 | async-start | bytes 2097152 | tf_op jit(solution)/shard_map/psum | solution.py:987
  481.0 118.2 %collective-permute-start.41 = (bf16[1024,1024]{1,0:T(8,128)(2,1)}, bf16[1024,1024]{1,0:T(8,128)(2,1)}, u32[]{:S(2)}, u32[]{:S(2)}) collective-permute-start(bf16[1024,1024]{1,0:T(8,128)(2,1)} %feed_out_partner.1.refs_3_), channel_id=1, source_target_pairs={{0,1},{1,0},{2,3},{3,2},{4,5},{5,4},{6,7},{7,6},{8,9},{9,8},{10,11... | collective-permute-start | bytes 6291464 | tf_op jit(solution)/shard_map/ppermute | solution.py:886
  502.0 96.3 %collective-permute-start.46 = (bf16[256,2048]{1,0:T(8,128)(2,1)}, bf16[256,2048]{1,0:T(8,128)(2,1)S(1)}, u32[]{:S(2)}, u32[]{:S(2)}) collective-permute-start(bf16[256,2048]{1,0:T(8,128)(2,1)} %all-reduce.3.cloned.1.call-done.refs_1_), channel_id=1, source_target_pairs={{0,4},{4,0},{1,5},{5,1},{2,6},{6,2},{3,7},{7,3},{8,12},{12,8},{9,1... | collective-permute-start | bytes 3145736 | tf_op jit(solution)/shard_map/ppermute | solution.py:886
  503.6 90.1 %collective-permute-start.42 = (bf16[256,1536]{1,0:T(8,128)(2,1)}, bf16[256,1536]{1,0:T(8,128)(2,1)S(1)}, u32[]{:S(2)}, u32[]{:S(2)}) collective-permute-start(bf16[256,1536]{1,0:T(8,128)(2,1)} %get-tuple-element.155.refs_3_), channel_id=1, source_target_pairs={{0,2},{2,0},{1,3},{3,1},{4,6},{6,4},{5,7},{7,5},{8,10},{10,8},{9,1... | collective-permute-start | bytes 2359304 | tf_op jit(solution)/shard_map/ppermute | solution.py:886
  505.1 43.3 %collective-permute-start.43 = (bf16[128,2176]{1,0:T(8,128)(2,1)S(1)}, bf16[128,2176]{1,0:T(8,128)(2,1)S(1)}, u32[]{:S(2)}, u32[]{:S(2)}) collective-permute-start(bf16[128,2176]{1,0:T(8,128)(2,1)S(1)} %copy-done.3), channel_id=1, source_target_pairs={{0,8},{8,0},{16,24},{24,16},{1,9},{9,1},{17,25},{25,17},{2,10},{10... | collective-permute-start | bytes 1671176 | tf_op jit(solution)/shard_map/ppermute | solution.py:993
  506.4 39.2 %collective-permute-start.44 = (bf16[256,1024]{1,0:T(8,128)(2,1)S(1)}, bf16[256,1024]{1,0:T(8,128)(2,1)}, u32[]{:S(2)}, u32[]{:S(2)}) collective-permute-start(bf16[256,1024]{1,0:T(8,128)(2,1)S(1)} %copy-done.6), channel_id=1, source_target_pairs={{0,16},{8,24},{16,0},{24,8},{1,17},{9,25},{17,1},{25,9},{2,18},{10... | collective-permute-start | bytes 1572872 | tf_op jit(solution)/shard_map/ppermute | solution.py:993
  552.0 90.6 %collective-permute-start.48 = (bf16[128,2176]{1,0:T(8,128)(2,1)}, bf16[128,2176]{1,0:T(8,128)(2,1)}, u32[]{:S(2)}, u32[]{:S(2)}) collective-permute-start(bf16[128,2176]{1,0:T(8,128)(2,1)} %pair_sum.15.refs_3_.refs_1_), channel_id=1, source_target_pairs={{0,16},{8,24},{16,0},{24,8},{1,17},{9,25},{17,1},{25,9},{2,18},{10... | collective-permute-start | bytes 1671176 | tf_op jit(solution)/shard_map/ppermute | solution.py:993
  593.3 66.7 %collective-permute-start.50 = (bf16[256,2048]{1,0:T(8,128)(2,1)}, bf16[256,2048]{1,0:T(8,128)(2,1)}, u32[]{:S(2)}, u32[]{:S(2)}) collective-permute-start(bf16[256,2048]{1,0:T(8,128)(2,1)} %all-reduce.5.cloned.1.call-done.refs_1_), channel_id=1, source_target_pairs={{0,4},{4,0},{1,5},{5,1},{2,6},{6,2},{3,7},{7,3},{8,12},{12,8},{9,1... | collective-permute-start | bytes 3145736 | tf_op jit(solution)/shard_map/ppermute | solution.py:886
  593.7 53.2 %collective-permute-start.55 = (bf16[256,1024]{1,0:T(8,128)(2,1)S(1)}, bf16[256,1024]{1,0:T(8,128)(2,1)}, u32[]{:S(2)}, u32[]{:S(2)}) collective-permute-start(bf16[256,1024]{1,0:T(8,128)(2,1)S(1)} %copy-done.13), channel_id=1, source_target_pairs={{0,4},{4,0},{1,5},{5,1},{2,6},{6,2},{3,7},{7,3},{8,12},{12,8},{9,1... | collective-permute-start | bytes 1572872 | tf_op jit(solution)/shard_map/ppermute | solution.py:886
  598.4 40.8 %collective-permute-start.45 = (bf16[128,1536]{1,0:T(8,128)(2,1)}, bf16[128,1536]{1,0:T(8,128)(2,1)S(1)}, u32[]{:S(2)}, u32[]{:S(2)}) collective-permute-start(bf16[128,1536]{1,0:T(8,128)(2,1)} %get-tuple-element.158), channel_id=1, source_target_pairs={{0,4},{4,0},{1,5},{5,1},{2,6},{6,2},{3,7},{7,3},{8,12},{12,8},{9,1... | collective-permute-start | bytes 1179656 | tf_op jit(solution)/shard_map/ppermute | solution.py:886
  599.2 51.2 %collective-permute-start.56 = (bf16[256,1024]{1,0:T(8,128)(2,1)S(1)}, bf16[256,1024]{1,0:T(8,128)(2,1)S(1)}, u32[]{:S(2)}, u32[]{:S(2)}) collective-permute-start(bf16[256,1024]{1,0:T(8,128)(2,1)S(1)} %copy-done.5), channel_id=1, source_target_pairs={{0,4},{4,0},{1,5},{5,1},{2,6},{6,2},{3,7},{7,3},{8,12},{12,8},{9,1... | collective-permute-start | bytes 1572872 | tf_op jit(solution)/shard_map/ppermute | solution.py:886
  645.6 18.4 %collective-permute-start.52 = (bf16[128,2176]{1,0:T(8,128)(2,1)}, bf16[128,2176]{1,0:T(8,128)(2,1)S(1)}, u32[]{:S(2)}, u32[]{:S(2)}) collective-permute-start(bf16[128,2176]{1,0:T(8,128)(2,1)} %pair_sum.17.refs_3_), channel_id=1, source_target_pairs={{0,4},{4,0},{1,5},{5,1},{2,6},{6,2},{3,7},{7,3},{8,12},{12,8},{9,1... | collective-permute-start | bytes 1671176 | tf_op jit(solution)/shard_map/ppermute | solution.py:886
  653.3 41.5 %collective-permute-start.53 = (bf16[256,2048]{1,0:T(8,128)(2,1)}, bf16[256,2048]{1,0:T(8,128)(2,1)}, u32[]{:S(2)}, u32[]{:S(2)}) collective-permute-start(bf16[256,2048]{1,0:T(8,128)(2,1)} %get-tuple-element.162), channel_id=1, source_target_pairs={{0,1},{1,0},{2,3},{3,2},{4,5},{5,4},{6,7},{7,6},{8,9},{9,8},{10,11... | collective-permute-start | bytes 3145736 | tf_op jit(solution)/shard_map/ppermute | solution.py:886
  659.3 18.1 %collective-permute-start.49 = (bf16[128,1536]{1,0:T(8,128)(2,1)}, bf16[128,1536]{1,0:T(8,128)(2,1)S(1)}, u32[]{:S(2)}, u32[]{:S(2)}) collective-permute-start(bf16[128,1536]{1,0:T(8,128)(2,1)} %pair_sum.18.refs_3_.refs_1_), channel_id=1, source_target_pairs={{0,16},{8,24},{16,0},{24,8},{1,17},{9,25},{17,1},{25,9},{2,18},{10... | collective-permute-start | bytes 1179656 | tf_op jit(solution)/shard_map/ppermute | solution.py:993
  664.0 30.8 %collective-permute-start.54 = (bf16[256,2048]{1,0:T(8,128)(2,1)}, bf16[256,2048]{1,0:T(8,128)(2,1)}, u32[]{:S(2)}, u32[]{:S(2)}) collective-permute-start(bf16[256,2048]{1,0:T(8,128)(2,1)} %get-tuple-element.163), channel_id=1, source_target_pairs={{0,1},{1,0},{2,3},{3,2},{4,5},{5,4},{6,7},{7,6},{8,9},{9,8},{10,11... | collective-permute-start | bytes 3145736 | tf_op jit(solution)/shard_map/ppermute | solution.py:886
  (63 other events, 666.5 us)
Sparse Core Ops, SparseCore 0:
  449.9 52.0 all-reduce.2
  504.5 88.7 all-reduce.4

commit v2 on v1

--- a/solution.py
+++ b/solution.py
@@ -16,7 +16,7 @@
 TILE = 256
 SHARD_ROWS = 256
 LANES = 128
-COST = 0.6
+TICK = 1e5
 X_AT, MIXER_AT, FEED_AT, DOWN_AT, PACK_AT, COLS_AT, GRAD_AT, OWNER_AT, ACT_AT = 0, 2, 8, 12, 16, 24, 32, 36, 40
 
 low = jnp.bfloat16
@@ -37,6 +37,7 @@
 
 class Order:
     last = None
+    scale = 1.0
 
 
 def launch(kernel, deps=(), onto=(), *, scalars=0, grid, in_specs, out_specs, out_shape, scratch_shapes=(), **rest):
@@ -70,7 +71,7 @@
 
 def cost(gigaflops, mebibytes):
     return pl.CostEstimate(
-        flops=int(gigaflops * COST * 1e9), bytes_accessed=int(mebibytes * COST * (1 << 20)), transcendentals=0
+        flops=int(gigaflops * Order.scale * 1e9), bytes_accessed=int(mebibytes * Order.scale * (1 << 20)), transcendentals=0
     )
 
 
@@ -96,17 +97,19 @@
     @pl.when(pl.program_id(0) == 0)
     def _():
         place(offs_ref, MIXER_AT, pieces, full_ref)
-        small = full_ref[:, 2 * heads + 2 * width :].astype(wide)
+        small = full_ref[:, 2 * heads + 3 * width :].astype(wide)
         vec_ref[...] = small.T[:8, :]
 
     x = x_ref[...].astype(wide)
     inverse = lax.rsqrt(jnp.mean(x * x, axis=-1, keepdims=True) + EPS)
     hidden = (x * inverse * vec_ref[0:1, :]).astype(low)
     hidden_ref[...] = hidden
-    q_ref[...] = (dot(hidden, full_ref[:, :heads]) * FEAT ** (-0.5)).astype(low)
-    k_ref[...] = dot(hidden, full_ref[:, heads : 2 * heads]).astype(low)
-    v_ref[...] = dot(hidden, full_ref[:, 2 * heads : 2 * heads + width]).astype(low)
-    gate_ref[...] = dot(hidden, full_ref[:, 2 * heads + width : 2 * heads + 2 * width]).astype(low)
+    at = width
+    q_ref[...] = (dot(hidden, full_ref[:, at : at + heads]) * FEAT ** (-0.5)).astype(low)
+    k_ref[...] = dot(hidden, full_ref[:, at + heads : at + 2 * heads]).astype(low)
+    at = at + 2 * heads
+    v_ref[...] = dot(hidden, full_ref[:, at : at + width]).astype(low)
+    gate_ref[...] = dot(hidden, full_ref[:, at + width : at + 2 * width]).astype(low)
 
 
 def project(offs, x, pieces, deps=()):
@@ -357,37 +360,26 @@
     )(v, gm, gate, vec, seg_col)
 
 
-def mix_kernel(offs_ref, x_ref, mixed_ref, vec_ref, *refs):
-    pieces, (middle_ref, hidden_ref, full_ref) = refs[:6], refs[6:]
-
-    @pl.when(pl.program_id(0) == 0)
-    def _():
-        place(offs_ref, MIXER_AT, pieces, full_ref)
-
-    middle = x_ref[...].astype(wide) + dot(mixed_ref[...], full_ref[...])
+def mix_kernel(x_ref, mixed_ref, vec_ref, weight_ref, middle_ref, hidden_ref):
+    middle = x_ref[...].astype(wide) + dot(mixed_ref[...], weight_ref[...])
     inverse = lax.rsqrt(jnp.mean(middle * middle, axis=-1, keepdims=True) + EPS)
     middle_ref[...] = middle
     hidden_ref[...] = (middle * inverse * vec_ref[1:2, :]).astype(low)
 
 
-def mix(offs, x, mixed, vec, pieces, deps=()):
+def mix(x, mixed, vec, full, deps=()):
     length, width = x.shape
     return launch(
         mix_kernel,
         deps,
-        scalars=1,
         grid=(length // TILE,),
-        in_specs=[rows(TILE, width), rows(TILE, width), fixed(vec.shape)] + [fixed(p.shape) for p in pieces],
-        out_specs=[rows(TILE, width), rows(TILE, width), fixed((width, width))],
-        out_shape=[
-            jax.ShapeDtypeStruct((length, width), wide),
-            jax.ShapeDtypeStruct((length, width), low),
-            jax.ShapeDtypeStruct((width, width), low),
-        ],
+        in_specs=[rows(TILE, width), rows(TILE, width), fixed(vec.shape), fixed((width, width))],
+        out_specs=[rows(TILE, width), rows(TILE, width)],
+        out_shape=[jax.ShapeDtypeStruct((length, width), wide), jax.ShapeDtypeStruct((length, width), low)],
         compiler_params=params(32),
         cost_estimate=cost(3, 16),
         name="mix",
-    )(offs, x, mixed, vec, *pieces)
+    )(x, mixed, vec, full)
 
 
 def first_half(n):
@@ -399,7 +391,7 @@
 
 
 def feed_kernel(n, offs_ref, ha_ref, hb_ref, ca_ref, cb_ref, *refs):
-    pieces, downs, (act_ref, both_ref, full_ref, down_ref) = refs[:4], refs[4:7], refs[7:]
+    pieces, downs, (act_ref, both_ref, full_ref, down_ref) = refs[:4], refs[4:6], refs[6:]
     step = pl.program_id(0)
     half = full_ref.shape[1] // 2
 
@@ -459,58 +451,62 @@
     )(offs, *hidden, *cotangent, *pieces, w_down, *down_pieces)
 
 
-def weight_grad_kernel(parts, counts, outs, length, offs_ref, *refs):
-    blocks = sum(outs)
-    lefts = [refs[b * parts : (b + 1) * parts] for b in range(blocks)]
-    rights = refs[blocks * parts : -len(outs)]
+def weight_grad_kernel(shape_of, counts, outs, length, offs_ref, *refs):
     targets = [(ref, row * TILE) for ref, height in zip(refs[-len(outs) :], outs) for row in range(height)]
-    terms = max(parts, len(rights) // len(counts))
     step = pl.program_id(0)
 
-    def part_of(group, t):
-        return group[t][...] if len(group) == terms else group[0][t * length : (t + 1) * length, :]
-
-    def work(group):
-        for b in range(blocks):
+    def work(lefts, rights):
+        terms = max(len(lefts[0]), len(rights))
+
+        def part_of(group, t):
+            return group[t][...] if len(group) == terms else group[0][t * length : (t + 1) * length, :]
+
+        for b, (ref, row) in enumerate(targets):
             value = None
             for t in range(terms):
-                product = dot_tn(part_of(lefts[b], t), part_of(group, t))
+                product = dot_tn(part_of(lefts[b], t), part_of(rights, t))
                 value = product if value is None else value + product
-            ref, row = targets[b]
             ref[row : row + TILE, :] = value.astype(low)
 
-    each = len(rights) // len(counts)
     start = 0
-    for n, count in enumerate(counts):
-        group = rights[n * each : (n + 1) * each]
+    for (left_at, right_at), count in zip(shape_of, counts):
+        lefts = [[refs[n] for n in block] for block in left_at]
+        rights = [refs[n] for n in right_at]
         if len(counts) == 1:
-            work(group)
+            work(lefts, rights)
         else:
-            pl.when((step >= start) & (step < start + count))(functools.partial(work, group))
+            pl.when((step >= start) & (step < start + count))(functools.partial(work, lefts, rights))
         start += count
 
 
-def weight_grad(offs, base, lefts, rights, outs, name, tile=512, deps=()):
+def weight_grad(offs, base, groups, outs, name, tile=512, deps=()):
     blocks = sum(outs)
-    counts = [group[0].shape[1] // tile for group in rights]
+    counts = [rights[0].shape[1] // tile for _, rights in groups]
     columns = sum(counts) * tile
-    in_specs, operands = [], []
-    for b in range(blocks):
-        for a in lefts:
-            in_specs.append(pl.BlockSpec((a.shape[0], TILE), lambda j, offs, b=b: (0, offs[base + b])))
-            operands.append(a)
+    in_specs, operands, shape_of, known = [], [], [], {}
     start = 0
-    for group, count in zip(rights, counts):
-        for a in group:
+    for (lefts, rights), count in zip(groups, counts):
+        key = tuple(id(a) for a in lefts)
+        if key not in known:
+            known[key] = []
+            for b in range(blocks):
+                known[key].append([len(operands) + n for n in range(len(lefts))])
+                for a in lefts:
+                    in_specs.append(pl.BlockSpec((a.shape[0], TILE), lambda j, offs, b=b: (0, offs[base + b])))
+                    operands.append(a)
+        shape_of.append((known[key], [len(operands) + n for n in range(len(rights))]))
+        for a in rights:
+
             def where_to(j, offs, start=start, count=count):
                 return (0, jnp.clip(j - start, 0, count - 1))
+
             in_specs.append(pl.BlockSpec((a.shape[0], tile), where_to))
             operands.append(a)
         start += count
-    tokens = sum(a.shape[0] for a in lefts)
-    terms = max(len(lefts), len(rights[0]))
-    result = launch(
-        functools.partial(weight_grad_kernel, len(lefts), counts, outs, tokens // terms),
+    tokens = sum(a.shape[0] for a in groups[0][0])
+    terms = max(len(groups[0][0]), len(groups[0][1]))
+    return launch(
+        functools.partial(weight_grad_kernel, shape_of, counts, outs, tokens // terms),
         deps,
         scalars=1,
         grid=(sum(counts),),
@@ -521,7 +517,6 @@
         cost_estimate=cost(2.5e-9 * tokens * 1024 * columns, (tokens * (1024 + columns) * 2 + 2048 * columns) / 2**20),
         name=name,
     )(offs, *operands)
-    return result
 
 
 def feed_back_kernel(a_ref, b_ref, wa_ref, wb_ref, out_ref):
@@ -580,7 +575,7 @@
         deps,
         grid=(length // TILE,),
         in_specs=[
-            tile, tile, line, line, line, fixed(vec.shape), fixed(full_first.shape), fixed(full_second.shape), fixed(w_output.shape)
+            tile, tile, line, line, line, fixed(vec.shape), fixed(full_first.shape), fixed(full_second.shape), fixed((width, width))
         ],
         out_specs=[line, line, line, fixed((8, width))],
         out_shape=[
@@ -627,12 +622,13 @@
     quarter = two // 4
     ghidden = None
     for n, col in enumerate((0, 2, 1, 3)):
-        term = dot_nt(gqk_ref[:, n * quarter : (n + 1) * quarter], full_ref[:, col * quarter : (col + 1) * quarter])
+        at = width + col * quarter
+        term = dot_nt(gqk_ref[:, n * quarter : (n + 1) * quarter], full_ref[:, at : at + quarter])
         ghidden = term if ghidden is None else ghidden + term
     ghidden = (
         ghidden
-        + dot_nt(gv_ref[...], full_ref[:, two : two + width])
-        + dot_nt(ggate_ref[...], full_ref[:, two + width : two + 2 * width])
+        + dot_nt(gv_ref[...], full_ref[:, width + two : 2 * width + two])
+        + dot_nt(ggate_ref[...], full_ref[:, two + 2 * width : two + 3 * width])
     )
     x = x_ref[...].astype(wide)
     inverse = lax.rsqrt(jnp.mean(x * x, axis=-1, keepdims=True) + EPS)
@@ -698,10 +694,10 @@
     )(cols, gain, w_gate, w_up, *blocks)
 
 
-def pack_kernel(at_ref, g1_ref, g2_ref, taps_ref, q_ref, k_ref, v_ref, c_ref, o_ref, pack_ref, half_ref, ohalf_ref):
+def pack_kernel(at_ref, g1_ref, g2_ref, taps_ref, q_ref, k_ref, v_ref, c_ref, o_ref, pack_ref, half_ref):
     height = q_ref.shape[0]
     col = 0
-    for ref in (q_ref, k_ref, v_ref, c_ref):
+    for ref in (o_ref, q_ref, k_ref, v_ref, c_ref):
         pack_ref[:, col : col + ref.shape[1]] = ref[...]
         col += ref.shape[1]
     small = jnp.concatenate([g1_ref[...].astype(wide), g2_ref[...].astype(wide), taps_ref[...].astype(wide)], 0)
@@ -709,14 +705,13 @@
     pack_ref[:, col : col + LANES] = small.T.astype(low)
     at = pl.multiple_of(at_ref[X_AT] * (height // 2), 128)
     half_ref[...] = pack_ref[pl.ds(at, height // 2), :]
-    ohalf_ref[...] = o_ref[pl.ds(at, height // 2), :]
 
 
 def pack_mixer(at, gain_one, gain_two, taps, w_query, w_key, w_value, w_convgate, w_output):
     operands = (gain_one, gain_two, taps, w_query, w_key, w_value, w_convgate, w_output)
     height = w_query.shape[0]
-    columns = w_query.shape[1] + w_key.shape[1] + w_value.shape[1] + w_convgate.shape[1] + LANES
-    shapes = [(height, columns), (height // 2, columns), (height // 2, w_output.shape[1])]
+    columns = sum(a.shape[1] for a in operands[3:]) + LANES
+    shapes = [(height, columns), (height // 2, columns)]
     return launch(
         pack_kernel,
         scalars=1,
@@ -740,14 +735,13 @@
             ref[row : row + height, part_y * quarter : (part_y + 1) * quarter] = gate_ref[:, at]
             ref[row : row + height, (2 + part_y) * quarter : (3 + part_y) * quarter] = up_ref[:, at]
     size = low_ref.shape[0]
-    for turn, ref in enumerate((low_ref, high_ref)):
-        at = pl.multiple_of(offs_ref[X_AT] * size + turn * 2 * size, 128)
-        ref[...] = down_ref[pl.ds(at, size), :]
+    low_ref[...] = down_ref[:size, :]
+    high_ref[...] = down_ref[size:, :]
 
 
 def pack_feed(offs, w_gate, w_up, w_down, deps=()):
     height, columns = w_gate.shape
-    shapes = [(height, columns // 2)] * 2 + [(2 * height, columns // 2)] + [(w_down.shape[0] // 4, w_down.shape[1])] * 2
+    shapes = [(height, columns // 2)] * 2 + [(2 * height, columns // 2)] + [(w_down.shape[0] // 2, w_down.shape[1])] * 2
     return launch(
         pack_feed_kernel,
         deps,
@@ -762,7 +756,7 @@
     )(offs, w_gate, w_up, w_down)
 
 
-def step(kernel, offs, operands, shapes, name, deps=()):
+def step(kernel, offs, operands, shapes, name, deps=(), giga=0.001):
     return launch(
         kernel,
         deps,
@@ -772,7 +766,7 @@
         out_specs=[fixed(a) for a in shapes],
         out_shape=[jax.ShapeDtypeStruct(a, low) for a in shapes],
         compiler_params=params(24),
-        cost_estimate=cost(0.001, 8),
+        cost_estimate=cost(giga, 8),
         name=name,
     )(offs, *operands)
 
@@ -867,23 +861,130 @@
 
 
 def sort_kernel(offs_ref, total_ref, other_ref, own_ref, give_ref):
+    skip = total_ref.shape[1] - own_ref.shape[1]
+
     @pl.when(offs_ref[X_AT + 1] == 0)
     def _():
-        own_ref[...] = total_ref[...]
-        give_ref[...] = other_ref[...]
+        own_ref[...] = total_ref[:, skip:]
+        give_ref[...] = other_ref[:, skip:]
 
     @pl.when(offs_ref[X_AT + 1] != 0)
     def _():
-        own_ref[...] = other_ref[...]
-        give_ref[...] = total_ref[...]
-
-
-def sort_rows(offs, total, other, deps=()):
-    return step(sort_kernel, offs, [total, other], [total.shape] * 2, "sort_rows", deps)
+        own_ref[...] = other_ref[:, skip:]
+        give_ref[...] = total_ref[:, skip:]
+
+
+def sort_rows(offs, total, other, skip, deps=()):
+    shape = (total.shape[0], total.shape[1] - skip)
+    return step(sort_kernel, offs, [total, other], [shape, shape], "sort_rows", deps)
+
+
+def pairs_kernel(offs_ref, *refs):
+    col = 0
+    for n in range(0, len(refs) - 1, 2):
+        width = refs[n].shape[1]
+        refs[-1][:, col : col + width] = add(refs[n][...], refs[n + 1][...])
+        col += width
+
+
+def pairs_sum(offs, pairs, deps=()):
+    shape = (pairs[0][0].shape[0], sum(a.shape[1] for a, _ in pairs))
+    return step(pairs_kernel, offs, [a for pair in pairs for a in pair], [shape], "pairs_sum", deps)[0]
+
+
+def settle_down_kernel(offs_ref, *refs):
+    out_ref = refs[-1]
+    size = out_ref.shape[0] // 4
+    width = out_ref.shape[1]
+    for n in range(4):
+        side = offs_ref[X_AT] if n % 2 == 0 else 1 - offs_ref[X_AT]
+        at = pl.ds(pl.multiple_of((n // 2) * 2 * size + side * size, 128), size)
+        out_ref[at, :] = refs[n][:, :width].astype(wide)
+
+
+def settle_down(offs, pairs, width, deps=()):
+    operands = [a for pair in pairs for a in pair]
+    size = operands[0].shape[0]
+    column = pl.BlockSpec((size, width), lambda *_: (0, 0), pipeline_mode=pl.Buffered(1))
+    return launch(
+        settle_down_kernel,
+        deps,
+        scalars=1,
+        grid=(1,),
+        in_specs=[column] * 4,
+        out_specs=fixed((4 * size, width)),
+        out_shape=jax.ShapeDtypeStruct((4 * size, width), wide),
+        compiler_params=params(24),
+        cost_estimate=cost(0.001, 6),
+        name="settle_down",
+    )(offs, *operands)
+
+
+def settle_mixer_kernel(
+    offs_ref, gain_ref, mine_ref, other_ref, wq_ref, wk_ref, wv_ref, wc_ref,
+    gq_ref, gk_ref, gv_ref, gc_ref, go_ref, gf_ref, ggain_ref, all_ref,
+):
+    size = mine_ref.shape[0]
+    for ref, side in ((mine_ref, offs_ref[X_AT]), (other_ref, 1 - offs_ref[X_AT])):
+        all_ref[pl.ds(pl.multiple_of(side * size, 128), size), :] = ref[...].astype(wide)
+    width = wv_ref.shape[1]
+    half = wq_ref.shape[1] // 2
+    go_ref[...] = all_ref[:, :width]
+    gc = all_ref[:, width : 2 * width]
+    gc_ref[...] = gc
+    gf_ref[...] = all_ref[:, 2 * width : 2 * width + LANES].T
+    at = 2 * width + LANES
+    gv = all_ref[:, at + 4 * half :]
+    gv_ref[...] = gv
+    total = jnp.sum(gc * wc_ref[...].astype(wide), axis=1, keepdims=True)
+    total = total + jnp.sum(gv * wv_ref[...].astype(wide), axis=1, keepdims=True)
+    for n, (ref, weight_ref, cols) in enumerate(
+        (
+            (gq_ref, wq_ref, slice(0, half)),
+            (gk_ref, wk_ref, slice(0, half)),
+            (gq_ref, wq_ref, slice(half, 2 * half)),
+            (gk_ref, wk_ref, slice(half, 2 * half)),
+        )
+    ):
+        value = all_ref[:, at + n * half : at + (n + 1) * half]
+        ref[:, cols] = value
+        total = total + jnp.sum(value * weight_ref[:, cols].astype(wide), axis=1, keepdims=True)
+    ggain_ref[...] = total / gain_ref[...]
+
+
+def settle_mixer(offs, gain, mine, other, w_query, w_key, w_value, w_convgate, deps=()):
+    operands = (gain, mine, other, w_query, w_key, w_value, w_convgate)
+    height, width = w_value.shape
+    shapes = [w_query.shape, w_key.shape, w_value.shape, w_convgate.shape, (height, width), (LANES, height), gain.shape]
+    return launch(
+        settle_mixer_kernel,
+        deps,
+        scalars=1,
+        grid=(1,),
+        in_specs=[fixed(a.shape) for a in operands],
+        out_specs=[fixed(a) for a in shapes],
+        out_shape=[jax.ShapeDtypeStruct(a, wide) for a in shapes],
+        scratch_shapes=[pltpu.VMEM((height, mine.shape[1]), wide)],
+        compiler_params=params(24),
+        cost_estimate=cost(0.001, 8),
+        name="settle_mixer",
+    )(offs, *operands)
+
+
+def tick_kernel(offs_ref, out_ref):
+    out_ref[...] = jnp.zeros_like(out_ref)
+
+
+def tick(offs, deps=()):
+    return step(tick_kernel, offs, [], [(16, 128)], "arrived", deps, TICK)[0]
 
 
 def swap(value, axis):
     return lax.ppermute(value, axis, [(0, 1), (1, 0)])
+
+
+def later(value, other):
+    return lax.optimization_barrier((value, other))[0]
 
 
 def part(value, index, count, axis=0):
@@ -902,6 +1003,7 @@
     gain_two, w_gate, w_up, w_down, cotangent,
 ):
     Order.last = None
+    Order.scale = 0.05
     x = lax.axis_index("near")
     y = lax.axis_index("row")
     c = lax.axis_index("core")
@@ -931,8 +1033,8 @@
         flip(3) * SHARD_ROWS + (1 - x) * half,
         *(a * SHARD_ROWS for a in feed_rows),
         y * small_block,
-        (1 - y) * small_block + x * (small_block // 2),
-        (1 - y) * small_block + (1 - x) * (small_block // 2),
+        (1 - y) * small_block,
+        0,
         0,
         *feed_cols(c, 0), *feed_cols(c, 1), *feed_cols(1 - c, 0), *feed_cols(1 - c, 1),
         *feed_cols(c, 0), *feed_cols(1 - c, 0), *feed_cols(c, 1), *feed_cols(1 - c, 1),
@@ -942,178 +1044,126 @@
     ]
     offs = jnp.stack([jnp.asarray(a, jnp.int32) for a in offs])
 
-    pack, pack_half, output_half = pack_mixer(
+    pack, pack_half = pack_mixer(
         offs, gain_one[None], gain_two[None], conv_filter, w_query, w_key, w_value, w_convgate, w_output
     )
-
-    def fetch(own, own_half):
-        near_core = swap(own, "core")
-        direct = swap(own_half, "row")
-        relayed = swap(direct, "near")
-        return [own, near_core, direct, relayed, swap(direct, "core"), swap(relayed, "core")]
-
-    pack_pieces = fetch(pack, pack_half)
-    output_pieces = fetch(w_output, output_half)
-    cot_other = swap(cotangent, "core")
+    direct = swap(pack_half, "row")
+    near_core = swap(pack, "core")
+    relayed = swap(direct, "near")
+    pack_pieces = [pack, near_core, direct, relayed, swap(direct, "core"), swap(relayed, "core")]
+    cot_other = swap(later(cotangent, direct), "core")
 
     mine_first, mine_second, give, *down_halves = pack_feed(offs, w_gate, w_up, w_down)
-    given = swap(give, "core")
+    given = swap(later(give, direct), "core")
     sends = step(pick_kernel, offs, [mine_first, mine_second, given], [mine_first.shape] * 2, "pick")
-    feed_pieces, down_pieces = [], []
-    for j, own in enumerate((mine_first, mine_second)):
-        direct = swap(sends[j], "row")
-        feed_pieces.append([own, given, direct, swap(direct, "near")])
-        direct = swap(down_halves[j], "row")
-        down_pieces.append([direct, swap(direct, "near")])
-
-    hidden_one, queries, keys, values, gates, full_one, vec = project(
-        offs, tokens, pack_pieces, deps=[cot_other, output_pieces[1], output_pieces[2]]
-    )
+    feed_pieces = [[own, given] for own in (mine_first, mine_second)]
+
+    feed_pieces[0].append(swap(sends[0], "row"))
+    hidden_one, queries, keys, values, gates, full_one, vec = project(offs, tokens, pack_pieces, deps=[cot_other])
+    down_pieces = [[swap(later(down_halves[0], queries), "row")]]
     pairs = width // 256
-    attended = attend(
-        queries, keys, values, gates, vec, seg, 0, pairs, deps=[output_pieces[3], output_pieces[4]]
-    )
+    attended = attend(queries, keys, values, gates, vec, seg, 0, pairs)
+    token = tick(offs)
+    feed_pieces[0].append(swap(later(feed_pieces[0][2], token), "near"))
+    feed_pieces[1].append(swap(later(sends[1], token), "row"))
     mixed, attention, recips = attend(
-        queries, keys, values, gates, vec, seg, pairs, pairs, onto=attended, deps=[feed_pieces[0][2], output_pieces[5]]
-    )
-    middle, hidden_two, full_output = mix(offs, tokens, mixed, vec, output_pieces, deps=[down_pieces[0][0]])
+        queries, keys, values, gates, vec, seg, pairs, pairs, onto=attended, deps=[feed_pieces[0][2]]
+    )
+    middle, hidden_two = mix(tokens, mixed, vec, full_one, deps=[down_pieces[0][0]])
+    down_pieces.append([swap(later(down_halves[1], middle), "row")])
+    tick(offs, [feed_pieces[0][3]])
     hiddens = [hidden_two, swap(hidden_two, "core")]
     cots = [cotangent, cot_other]
 
-    def after(value, other):
-        return value if other is None else lax.optimization_barrier((value, other))[0]
-
-    def far_sum(part, previous):
-        return lax.psum(after(part, previous), "far")
-
-    def far_swap(value, bit):
-        count = lax.axis_size("far")
-        if bit >= count:
-            return None
-        return lax.ppermute(value, "far", [(i, i ^ bit) for i in range(count)])
-
-    def far_rest(value, came):
-        value = pair_sum(offs, value, came)
-        bit = 4
-        while bit < lax.axis_size("far"):
-            value = pair_sum(offs, value, far_swap(value, bit))
-            bit *= 2
-        return value
-
-    first_feed = feed(offs, hiddens, cots, 0, w_down, feed_pieces[0], down_pieces[0], deps=[feed_pieces[1][2]])
-    down_send, down_keep = weight_grad(
-        offs, ACT_AT, [first_feed[0]], [cots], (2, 2), "grad_down", deps=[down_pieces[1][0]]
-    )
+    Order.scale = 20.0
+
+    def down_grad(act, deps=()):
+        return weight_grad(offs, ACT_AT, [([act], cots)], (2, 2), "grad_down", deps=deps)
+
+    def gate_grad(both):
+        return weight_grad(offs, GRAD_AT, [(hiddens, [both])], (1, 1, 2), "grad_gate_up")
+
+    first_feed = feed(offs, hiddens, cots, 0, w_down, feed_pieces[0], down_pieces[0])
+    feed_pieces[1].append(swap(later(feed_pieces[1][2], first_feed[0]), "near"))
+    down_send, down_keep = down_grad(first_feed[0], deps=[feed_pieces[1][2]])
     down_came = swap(down_send, "near")
-    gate_send, gate_send_own, gate_keep = weight_grad(
-        offs, GRAD_AT, hiddens, [[first_feed[1]]], (1, 1, 2), "grad_gate_up"
-    )
+    gate_send, gate_send_own, gate_keep = gate_grad(first_feed[1])
     gate_came, gate_came_own = swap(gate_send, "row"), swap(gate_send_own, "row")
     second_feed = feed(offs, hiddens, cots, 1, w_down, feed_pieces[1], down_pieces[1])
+    acts, boths, fulls, downs = zip(first_feed, second_feed)
+    down_passed = swap(top_sum(offs, down_keep, down_came), "row")
     gate_passed = swap(top_sum(offs, gate_keep, gate_came), "near")
-    down_passed = swap(top_sum(offs, down_keep, down_came), "row")
-    down_send_2, down_keep_2 = weight_grad(offs, ACT_AT, [second_feed[0]], [cots], (2, 2), "grad_down")
-    down_came_2 = swap(down_send_2, "near")
-    gate_send_2, gate_send_own_2, gate_keep_2 = weight_grad(
-        offs, GRAD_AT, hiddens, [[second_feed[1]]], (1, 1, 2), "grad_gate_up"
-    )
-    gate_came_2, gate_came_own_2 = swap(gate_send_2, "row"), swap(gate_send_own_2, "row")
-    acts, boths, fulls, downs = zip(first_feed, second_feed)
-    gate_total = far_sum(rest_sum(offs, [(gate_keep, gate_came_own, gate_passed)]), None)
     ghidden_part = feed_back(boths[0], boths[1], fulls[0], fulls[1])
     ghidden_other = swap(ghidden_part, "core")
-    down_sum = rest_sum(offs, [(down_keep, down_came, down_passed)])
-    down_far = far_swap(down_sum, 1)
+    down_send_2, down_keep_2 = down_grad(second_feed[0])
+    down_came_2 = swap(down_send_2, "near")
+    gate_send_2, gate_send_own_2, gate_keep_2 = gate_grad(second_feed[1])
+    gate_came_2, gate_came_own_2 = swap(gate_send_2, "row"), swap(gate_send_own_2, "row")
+    feed_sum = lax.psum(
+        rest_sum(offs, [(down_keep, down_came, down_passed), (gate_keep, gate_came_own, gate_passed)]), "far"
+    )
+    tick(offs)
     gmiddle, gbranch, gmixed, _ = middle_back(
-        boths[0], boths[1], ghidden_other, middle, cotangent, vec, fulls[0], fulls[1], full_output
-    )
+        boths[0], boths[1], ghidden_other, middle, cotangent, vec, fulls[0], fulls[1], full_one
+    )
+    down_passed_2 = swap(top_sum(offs, down_keep_2, down_came_2), "row")
     gate_passed_2 = swap(top_sum(offs, gate_keep_2, gate_came_2), "near")
-    down_passed_2 = swap(top_sum(offs, down_keep_2, down_came_2), "row")
-    down_sum = pair_sum(offs, down_sum, down_far)
-    down_far = far_swap(down_sum, 2)
-
-    output_send, output_keep = weight_grad(offs, OWNER_AT, [mixed], [[gbranch]], (2, 2), "grad_output")
-    output_came = swap(output_send, "core")
+
     ggate, gconv, gfilter = conv_back(values, gmixed, gates, vec, seg)
     filter_came = swap(gfilter, "core")
-    convgate_send, convgate_keep = weight_grad(
-        offs, OWNER_AT, [hidden_one], [[ggate]], (2, 2), "grad_convgate", deps=[output_came]
-    )
-    convgate_came = swap(convgate_send, "core")
-    gate_total_2 = far_sum(rest_sum(offs, [(gate_keep_2, gate_came_own_2, gate_passed_2)]), gate_total)
-    attended = attend_back(
-        queries, keys, values, gmixed, attention, recips, gconv, seg, 0, pairs, deps=[filter_came]
-    )
-    early_give, early_held = halves_sum(
-        offs, [(output_keep, output_came), (convgate_keep, convgate_came), (gfilter, filter_came)], True
-    )
+    early_send, early_keep = weight_grad(
+        offs, OWNER_AT, [([mixed], [gbranch]), ([hidden_one], [ggate])], (2, 2), "grad_output_convgate"
+    )
+    early_came = swap(early_send, "core")
+    attended = attend_back(queries, keys, values, gmixed, attention, recips, gconv, seg, 0, pairs)
+    early_give, early_held = halves_sum(offs, [(early_keep, early_came), (gfilter, filter_came)], True)
     early_came = swap(early_give, "row")
-    down_sum_2 = rest_sum(offs, [(down_keep_2, down_came_2, down_passed_2)])
-    down_far_2 = far_swap(down_sum_2, 1)
-    down_sum = far_rest(down_sum, down_far)
-    down_other = swap(down_sum, "near")
+    tick(offs, [feed_sum])
+    feed_near = rest_sum(
+        offs, [(down_keep_2, down_came_2, down_passed_2), (gate_keep_2, gate_came_own_2, gate_passed_2)]
+    )
+    feed_other = swap(later(feed_sum, feed_near), "near")
+    feed_sum_2 = lax.psum(feed_near, "far")
+    tick(offs)
     gqk, gv = attend_back(
         queries, keys, values, gmixed, attention, recips, gconv, seg, pairs, pairs, onto=attended
     )
-    down_sum_2 = pair_sum(offs, down_sum_2, down_far_2)
-    down_far_2 = far_swap(down_sum_2, 2)
     early_own, early_other = near_split(offs, early_held, early_came)
     early_passed = swap(early_other, "near")
-    late_send, late_keep = weight_grad(offs, OWNER_AT, [hidden_one], [[gqk], [gv]], (2, 2), "grad_query_key_value")
+    late_send, late_keep = weight_grad(
+        offs, OWNER_AT, [([hidden_one], [gqk]), ([hidden_one], [gv])], (2, 2), "grad_query_key_value"
+    )
     late_came = swap(late_send, "core")
-    grad_tokens, _ = tokens_back(gqk, gv, ggate, tokens, gmiddle, vec, full_one)
+    own_rows, theirs = sort_rows(offs, feed_sum, feed_other, width)
+    spreads = [own_rows, swap(theirs, "core")]
     late_give, late_held = halves_sum(offs, [(late_keep, late_came)])
     late_came = swap(late_give, "row")
-    early = pair_sum(offs, early_own, early_passed)
-    early_far = far_swap(early, 1)
+    grad_tokens, _ = tokens_back(gqk, gv, ggate, tokens, gmiddle, vec, full_one)
+    late_own, late_other = near_split(offs, late_held, late_came)
+    late_passed = swap(late_other, "near")
     out_part = feed_out(acts[0], acts[1], downs[0], downs[1], 1, [], "feed_out_partner")
     out_came = swap(out_part, "core")
-    down_sum_2 = far_rest(down_sum_2, down_far_2)
-    down_other_2 = swap(down_sum_2, "near")
-    gate_other = swap(gate_total, "near")
-    early = pair_sum(offs, early, early_far)
-    early_far = far_swap(early, 2)
-    late_own, late_other = near_split(offs, late_held, late_came)
-    late_passed = swap(late_other, "near")
+    tick(offs, [feed_sum_2])
+    mixer_near = pairs_sum(offs, [(early_own, early_passed), (late_own, late_passed)])
+    feed_other_2 = swap(later(feed_sum_2, mixer_near), "near")
+    mixer_sum = lax.psum(mixer_near, "far")
+    tick(offs)
     result = feed_out(acts[0], acts[1], downs[0], downs[1], 0, [middle, out_came], "feed_out")
-    own_rows, theirs = sort_rows(offs, gate_total, gate_other)
-    spreads = [own_rows, swap(theirs, "core")]
-    late = pair_sum(offs, late_own, late_passed)
-    late_far = far_swap(late, 1)
-    gate_other = swap(gate_total_2, "near")
-    early = far_rest(early, early_far)
-    early_other = swap(early, "near")
-    late = pair_sum(offs, late, late_far)
-    late_far = far_swap(late, 2)
-    own_rows, theirs = sort_rows(offs, gate_total_2, gate_other)
+    own_rows, theirs = sort_rows(offs, feed_sum_2, feed_other_2, width)
     spreads += [own_rows, swap(theirs, "core")]
-    late = far_rest(late, late_far)
-    late_other = swap(late, "near")
+    grad_down = settle_down(offs, [(feed_sum, feed_other), (feed_sum_2, feed_other_2)], width)
     grad_gate, grad_up, ggain_two = spread(offs, gain_two[:, None].astype(wide), w_gate, w_up, spreads)
-
-    grad_down = jnp.concatenate(
-        [in_order(x, down_sum, down_other), in_order(x, down_sum_2, down_other_2)], 0
-    ).astype(wide)
-    early = in_order(x, early, early_other).astype(wide)
-    late = in_order(x, late, late_other).astype(wide)
-    heads = HEADS * FEAT
-    quarters = [late[:, n * heads // 2 : (n + 1) * heads // 2] for n in range(4)]
-    grads = (
-        jnp.concatenate([quarters[0], quarters[2]], 1),
-        jnp.concatenate([quarters[1], quarters[3]], 1),
-        late[:, 2 * heads :],
-        early[:, width : 2 * width],
-    )
-    ggain_one = sum(
-        jnp.sum(g * w.astype(wide), axis=1) for g, w in zip(grads, (w_query, w_key, w_value, w_convgate))
-    ) / gain_one.astype(wide)
+    mixer_other = swap(mixer_sum, "near")
+    *grads, grad_output, grad_filter, ggain_one = settle_mixer(
+        offs, gain_one[:, None].astype(wide), mixer_sum, mixer_other, w_query, w_key, w_value, w_convgate
+    )
     return (
         result,
         grad_tokens,
-        ggain_one,
+        ggain_one[:, 0],
         *grads,
-        early[:, :width],
-        early[:, 2 * width : 2 * width + KW].T,
+        grad_output,
+        grad_filter[:KW],
         ggain_two[:, 0],
         grad_gate,
         grad_up,

time: 716 us -> 567 us (0.79)
  waiting for transfers between devices: 230 us -> 114 us
  starting transfers between devices: 48.9 us -> 32.1 us
  local copies, waits for them, and re-layouts: 26.1 us -> 13.1 us
  other arithmetic: 10.6 us -> 2.26 us
    ppermute x8 -> x0, waiting for transfers between devices: 54 us -> none  [far_swap(): return lax.ppermute(value, 'far', [(i, i ^ bit) for i in range(count)])]
    ppermute x49 -> x38, waiting for transfers between devices: 117 us -> 78.2 us  [swap(): return lax.ppermute(value, axis, [(0, 1), (1, 0)])]
    psum x2 -> x3, waiting for transfers between devices: 58.6 us -> 34.7 us  [the longest x1 24 us: per_device(): feed_sum_2 = lax.psum(feed_near, 'far')]
    unnamed x106 -> x26, local copies, waits for them, and re-layouts: 21.1 us -> 6.08 us
    ppermute x8 -> x0, starting transfers between devices: 11.2 us -> none  [far_swap(): return lax.ppermute(value, 'far', [(i, i ^ bit) for i in range(count)])]
    ppermute x49 -> x38, starting transfers between devices: 37.6 us -> 32 us  [swap(): return lax.ppermute(value, axis, [(0, 1), (1, 0)])]
    pallas_call x49 -> x46, Pallas kernels: 382 us -> 380 us  [call(): result = run(*operands, *deps)]
  transfers between devices with their start and end apart: 59 -> 41, of which waited for: 17 -> 10; matrix products, arithmetic and copies ran while one was open for 2% -> 0% of each run, Pallas kernels for 44% -> 67%
where the time goes in v2:
time: 567 us; the launch traced here: 556 us
  Pallas kernels  380 us (67%)
  waiting for transfers between devices  114 us (20%)
  starting transfers between devices  32.1 us (6%)
  between operations  14.4 us (3%)
  local copies, waits for them, and re-layouts  13.1 us (2%)
    pallas_call x46, Pallas kernels, call(): result = run(*operands, *deps)  380 us
    ppermute x38, waiting for transfers between devices, swap(): return lax.ppermute(value, axis, [(0, 1), (1, 0)])  78.2 us
    ppermute x38, starting transfers between devices, swap(): return lax.ppermute(value, axis, [(0, 1), (1, 0)])  32 us
    psum x1, waiting for transfers between devices, per_device(): feed_sum_2 = lax.psum(feed_near, 'far')  24 us
  transfers between devices with their start and end apart: 41, of which 10 were waited for; matrix products, arithmetic and copies ran while one was open for 0% of the time, Pallas kernels for 67%

profile of v2, /device:TPU:0, one launch (start us, length us, event | category | flops | bytes accessed | tf_op | source)
XLA Modules:
  0.0 556.4 jit_solution(14464664912348812714)
XLA Ops:
  10.4 3.9 pack_mixer.1
  14.2 3.0 collective-permute-start.1
  17.2 6.8 %pack_feed.1 = (bf16[256,2048]{1,0:T(8,128)(2,1)}, bf16[256,2048]{1,0:T(8,128)(2,1)}, bf16[512,2048]{1,0:T(8,128)(2,1)}, bf16[512,1024]{1,0:T(8,128)(2,1)}, bf16[512,1024]{1,0:T(8,128)(2,1)}) custom-call(s32[44]{0:T(128)} %stack.129.refs_0_, bf16[256,4096]{1,0:T(8,128)(2,1)} %refs_2_.3, bf16[256,4096]{1,0:T(8,128)(2,1)} %refs_3_.11, ...), custom_call_target="tpu_custom_call" | custom-call | flops 50000 | bytes 419430 | tf_op jit(solution)/shard_map/pack_feed/pallas_call | solution.py:61
  23.9 14.5 %collective-permute-done.1.refs_4_ = bf16[128,3712]{1,0:T(8,128)(2,1)S(1)} collective-permute-done((bf16[128,3712]{1,0:T(8,128)(2,1)}, bf16[128,3712]{1,0:T(8,128)(2,1)S(1)}, u32[]{:S(2)}, u32[]{:S(2)}) %collective-permute-start.1) | collective-permute-done | bytes 950304 | tf_op jit(solution)/shard_map/ppermute | solution.py:983
  40.9 21.6 %collective-permute-done.2.refs_5_ = bf16[128,3712]{1,0:T(8,128)(2,1)} collective-permute-done((bf16[128,3712]{1,0:T(8,128)(2,1)S(1)}, bf16[128,3712]{1,0:T(8,128)(2,1)}, u32[]{:S(2)}, u32[]{:S(2)}) %collective-permute-start.2) | collective-permute-done | bytes 950304 | tf_op jit(solution)/shard_map/ppermute | solution.py:983
  63.6 4.4 pick.1
  69.7 14.2 %project.1 = (bf16[1024,1024]{1,0:T(8,128)(2,1)}, bf16[1024,256]{1,0:T(8,128)(2,1)}, bf16[1024,256]{1,0:T(8,128)(2,1)}, bf16[1024,1024]{1,0:T(8,128)(2,1)}, bf16...) custom-call(s32[44]{0:T(128)} %stack.129.refs_0_, bf16[1024,1024]{1,0:T(8,128)(2,1)} %refs_3_.10, ...), custom_call_target="tpu_custom_call" | custom-call | flops 350000000 | bytes 1153433 | tf_op jit(solution)/shard_map/project/pallas_call | solution.py:61
  84.3 11.7 %attention_forward.2 = (bf16[1024,1024]{1,0:T(8,128)(2,1)}, bf16[1024,1024]{1,0:T(8,128)(2,1)}, bf16[1024,1024]{1,0:T(8,128)(2,1)}) custom-call(bf16[1024,256]{1,0:T(8,128)(2,1)} %get-tuple-element.109.refs_0_, bf16[1024,256]{1,0:T(8,128)(2,1)} %get-tuple-element.110.refs_1_, bf16[1024,1024]{1,0:T(8,128)(2,1)} %get-tuple-element.111.refs_2_.refs_0_, ...), custom_call_target="tpu_custom_call" | custom-call | flops 450000000 | bytes 734003 | tf_op jit(solution)/shard_map/attention_forward/pallas_call | solution.py:61
  100.4 11.7 %attention_forward.3 = (bf16[1024,1024]{1,0:T(8,128)(2,1)}, bf16[1024,1024]{1,0:T(8,128)(2,1)}, bf16[1024,1024]{1,0:T(8,128)(2,1)}) custom-call(bf16[1024,256]{1,0:T(8,128)(2,1)} %get-tuple-element.109.refs_0_, bf16[1024,256]{1,0:T(8,128)(2,1)} %get-tuple-element.110.refs_1_, ...), custom_call_target="tpu_custom_call", output_to_operand_aliasing={{0}: (7, {}), {1}: (8, {}), {2}: (9, {})} | custom-call | flops 450000000 | bytes 734003 | tf_op jit(solution)/shard_map/attention_forward/pallas_call | solution.py:61
  112.2 4.5 collective-permute-done.8.refs_4_.refs_10_
  116.7 7.2 %mix.1 = (f32[1024,1024]{1,0:T(8,128)}, bf16[1024,1024]{1,0:T(8,128)(2,1)}) custom-call(bf16[1024,1024]{1,0:T(8,128)(2,1)} %refs_3_.10, bf16[1024,1024]{1,0:T(8,128)(2,1)} %get-tuple-element.118.refs_1_.refs_5_.refs_2_.refs_3_.refs_4_, f32[8,1024]{1,0:T(8,128)} %get-tuple-element.113.refs_4_.refs_2_.refs_5_.refs_3_, ...), custom_call_target="tpu_custom_call" | custom-call | flops 150000000 | bytes 838860 | tf_op jit(solution)/shard_map/mix/pallas_call | solution.py:61
  128.4 23.6 %feed_in.2 = (bf16[2048,1024]{1,0:T(8,128)(2,1)}, bf16[2048,2048]{1,0:T(8,128)(2,1)}, bf16[1024,2048]{1,0:T(8,128)(2,1)}, bf16[1024,1024]{1,0:T(8,128)(2,1)}) custom-call(s32[44]{0:T(128)} %stack.129.refs_0_, bf16[1024,1024]{1,0:T(8,128)(2,1)} %get-tuple-element.122.refs_1_.refs_3_.refs_5_.refs_7_, ...), custom_call_target="tpu_custom_call" | custom-call | flops 320000000000 | bytes 713031680 | tf_op jit(solution)/shard_map/feed_in/pallas_call | solution.py:61
  153.8 9.4 %grad_down.2 = (bf16[512,1024]{1,0:T(8,128)(2,1)}, bf16[512,1024]{1,0:T(8,128)(2,1)}) custom-call(s32[44]{0:T(128)} %stack.129.refs_0_, bf16[2048,1024]{1,0:T(8,128)(2,1)} %get-tuple-element.125.refs_1_.refs_2_.refs_3_.refs_4_.refs_8_.refs_0_, bf16[2048,1024]{1,0:T(8,128)(2,1)} %get-tuple-element.125.refs_1_.refs_2_.refs_3_.refs_4_.refs_8_.refs_0_, ...), custom_call_target="tpu_custom_call" | custom-call | flops 107374182400 | bytes 209715200 | tf_op jit(solution)/shard_map/grad_down/pallas_call | solution.py:61
  163.5 14.1 %grad_gate_up.2 = (bf16[256,2048]{1,0:T(8,128)(2,1)}, bf16[256,2048]{1,0:T(8,128)(2,1)}, bf16[512,2048]{1,0:T(8,128)(2,1)}) custom-call(s32[44]{0:T(128)} %stack.129.refs_0_, bf16[1024,1024]{1,0:T(8,128)(2,1)} %get-tuple-element.122.refs_1_.refs_3_.refs_5_.refs_7_, bf16[1024,1024]{1,0:T(8,128)(2,1)} %collective-permute-done.9.refs_2_.refs_4_.refs_6_.refs_8_, ...), custom_call_target="tpu_custom_call" | custom-call | flops 214748364800 | bytes 335544320 | tf_op jit(solution)/shard_map/grad_gate_up/pallas_call | solution.py:61
  179.6 23.5 %feed_in.3 = (bf16[2048,1024]{1,0:T(8,128)(2,1)}, bf16[2048,2048]{1,0:T(8,128)(2,1)}, bf16[1024,2048]{1,0:T(8,128)(2,1)}, bf16[1024,1024]{1,0:T(8,128)(2,1)}) custom-call(s32[44]{0:T(128)} %stack.129.refs_0_, bf16[1024,1024]{1,0:T(8,128)(2,1)} %get-tuple-element.122.refs_1_.refs_3_.refs_5_.refs_7_, ...), custom_call_target="tpu_custom_call" | custom-call | flops 320000000000 | bytes 713031680 | tf_op jit(solution)/shard_map/feed_in/pallas_call | solution.py:61
  203.1 3.1 top_sum.4.refs_3_
  207.9 3.7 top_sum.5.refs_4_
  213.2 14.4 %feed_back_partner.1.refs_7_ = bf16[1024,1024]{1,0:T(8,128)(2,1)} custom-call(bf16[2048,2048]{1,0:T(8,128)(2,1)} %get-tuple-element.131.refs_9_.refs_0_, bf16[2048,2048]{1,0:T(8,128)(2,1)} %get-tuple-element.137.refs_1_.refs_9_, bf16[1024,2048]{1,0:T(8,128)(2,1)} %get-tuple-element.138.refs_2_.refs_6_, ...), custom_call_target="tpu_custom_call" | custom-call | flops 199999995904 | bytes 377487360 | tf_op jit(solution)/shard_map/feed_back_partner/pallas_call | solution.py:61
  227.5 9.2 %grad_down.3 = (bf16[512,1024]{1,0:T(8,128)(2,1)}, bf16[512,1024]{1,0:T(8,128)(2,1)}) custom-call(s32[44]{0:T(128)} %stack.129.refs_0_, bf16[2048,1024]{1,0:T(8,128)(2,1)} %get-tuple-element.134.refs_3_.refs_1_.refs_2_.refs_4_, bf16[2048,1024]{1,0:T(8,128)(2,1)} %get-tuple-element.134.refs_3_.refs_1_.refs_2_.refs_4_, ...), custom_call_target="tpu_custom_call" | custom-call | flops 107374182400 | bytes 209715200 | tf_op jit(solution)/shard_map/grad_down/pallas_call | solution.py:61
  237.2 24.0 %grad_gate_up.3 = (bf16[256,2048]{1,0:T(8,128)(2,1)}, bf16[256,2048]{1,0:T(8,128)(2,1)}, bf16[512,2048]{1,0:T(8,128)(2,1)}) custom-call(s32[44]{0:T(128)} %stack.129.refs_0_, bf16[1024,1024]{1,0:T(8,128)(2,1)} %get-tuple-element.122.refs_1_.refs_3_.refs_5_.refs_7_, bf16[1024,1024]{1,0:T(8,128)(2,1)} %collective-permute-done.9.refs_2_.refs_4_.refs_6_.refs_8_, ...), custom_call_target="tpu_custom_call" | custom-call | flops 214748364800 | bytes 335544320 | tf_op jit(solution)/shard_map/grad_gate_up/pallas_call | solution.py:61
  263.3 5.3 rest_sum.2.refs_1_
  270.6 20.4 %middle_back.1 = (f32[1024,1024]{1,0:T(8,128)}, bf16[1024,1024]{1,0:T(8,128)(2,1)}, bf16[1024,1024]{1,0:T(8,128)(2,1)}, f32[8,1024]{1,0:T(8,128)}) custom-call(bf16[2048,2048]{1,0:T(8,128)(2,1)} %get-tuple-element.131.refs_9_.refs_0_, bf16[2048,2048]{1,0:T(8,128)(2,1)} %get-tuple-element.137.refs_1_.refs_9_, ...), custom_call_target="tpu_custom_call" | custom-call | flops 260000006144 | bytes 838860800 | tf_op jit(solution)/shard_map/middle_back/pallas_call | solution.py:61
  291.0 3.1 top_sum.6.refs_3_
  294.5 3.8 top_sum.7.refs_5_
  299.9 10.9 %convolution_backward.1 = (bf16[1024,1024]{1,0:T(8,128)(2,1)}, bf16[1024,1024]{1,0:T(8,128)(2,1)}, bf16[1024,128]{1,0:T(8,128)(2,1)}) custom-call(bf16[1024,1024]{1,0:T(8,128)(2,1)} %get-tuple-element.111.refs_2_.refs_0_, bf16[1024,1024]{1,0:T(8,128)(2,1)} %get-tuple-element.145.refs_1_.refs_3_, bf16[1024,1024]{1,0:T(8,128)(2,1)} %get-tuple-element.112.refs_3_.refs_2_, ...), custom_call_target="tpu_custom_call" | custom-call | flops 20000000000 | bytes 209715200 | tf_op jit(solution)/shard_map/convolution_backward/pallas_call | solution.py:61
  310.8 10.4 %grad_output_convgate.1 = (bf16[512,2048]{1,0:T(8,128)(2,1)}, bf16[512,2048]{1,0:T(8,128)(2,1)}) custom-call(s32[44]{0:T(128)} %stack.129.refs_0_, bf16[1024,1024]{1,0:T(8,128)(2,1)} %get-tuple-element.118.refs_1_.refs_5_.refs_2_.refs_3_.refs_4_, bf16[1024,1024]{1,0:T(8,128)(2,1)} %get-tuple-element.118.refs_1_.refs_5_.refs_2_.refs_3_.refs_4_, ...), custom_call_target="tpu_custom_call" | custom-call | flops 107374182400 | bytes 209715200 | tf_op jit(solution)/shard_map/grad_output_convgate/pallas_call | solution.py:61
  321.7 20.9 %attention_backward.2 = (bf16[1024,512]{1,0:T(8,128)(2,1)}, bf16[1024,1024]{1,0:T(8,128)(2,1)}) custom-call(bf16[1024,256]{1,0:T(8,128)(2,1)} %get-tuple-element.109.refs_0_, bf16[1024,256]{1,0:T(8,128)(2,1)} %get-tuple-element.110.refs_1_, bf16[1024,1024]{1,0:T(8,128)(2,1)} %get-tuple-element.111.refs_2_.refs_0_, ...), custom_call_target="tpu_custom_call" | custom-call | flops 399999991808 | bytes 377487360 | tf_op jit(solution)/shard_map/attention_backward/pallas_call | solution.py:61
  342.6 4.9 halves_sum.2
  350.2 5.3 rest_sum.3.refs_1_
  357.2 20.7 %attention_backward.3 = (bf16[1024,512]{1,0:T(8,128)(2,1)}, bf16[1024,1024]{1,0:T(8,128)(2,1)}) custom-call(bf16[1024,256]{1,0:T(8,128)(2,1)} %get-tuple-element.109.refs_0_, bf16[1024,256]{1,0:T(8,128)(2,1)} %get-tuple-element.110.refs_1_, bf16[1024,1024]{1,0:T(8,128)(2,1)} %get-tuple-element.111.refs_2_.refs_0_, ...), custom_call_target="tpu_custom_call", output_to_operand_aliasing={{0}: (9, {}), {1}: (10, {})} | custom-call | flops 399999991808 | bytes 377487360 | tf_op jit(solution)/shard_map/attention_backward/pallas_call | solution.py:61
  377.9 3.4 near_split.2
  381.3 8.1 %grad_query_key_value.1 = (bf16[512,1536]{1,0:T(8,128)(2,1)}, bf16[512,1536]{1,0:T(8,128)(2,1)}) custom-call(s32[44]{0:T(128)} %stack.129.refs_0_, bf16[1024,1024]{1,0:T(8,128)(2,1)} %get-tuple-element.114.refs_7_.refs_6_.refs_8_.refs_9_.refs_1_.refs_2_.refs_3_.refs_4_, ...), custom_call_target="tpu_custom_call" | custom-call | flops 80530636800 | bytes 167772160 | tf_op jit(solution)/shard_map/grad_query_key_value/pallas_call | solution.py:61
  393.4 4.2 sort_rows.2
  398.8 3.9 halves_sum.3
  403.1 14.8 %tokens_back.1 = (f32[1024,1024]{1,0:T(8,128)}, f32[8,1024]{1,0:T(8,128)}) custom-call(bf16[1024,512]{1,0:T(8,128)(2,1)} %get-tuple-element.161.refs_3_.refs_5_.refs_0_, bf16[1024,1024]{1,0:T(8,128)(2,1)} %get-tuple-element.162.refs_6_.refs_1_, bf16[1024,1024]{1,0:T(8,128)(2,1)} %get-tuple-element.153.refs_10_.refs_11_.refs_2_, bf16[1024,1024]{1,0:T(8,128)(2,1)} %refs_3_.10, ...), custom_call_target="tpu_custom_call" | custom-call | flops 140000002048 | bytes 503316480 | tf_op jit(solution)/shard_map/tokens_back/pallas_call | solution.py:61
  417.9 4.9 collective-permute-done.30.refs_2_
  423.7 3.0 near_split.3
  426.7 8.6 %feed_out_partner.1.refs_2_ = bf16[1024,1024]{1,0:T(8,128)(2,1)} custom-call(bf16[2048,1024]{1,0:T(8,128)(2,1)} %get-tuple-element.125.refs_1_.refs_2_.refs_3_.refs_4_.refs_8_.refs_0_, bf16[2048,1024]{1,0:T(8,128)(2,1)} %get-tuple-element.134.refs_3_.refs_1_.refs_2_.refs_4_, bf16[1024,1024]{1,0:T(8,128)(2,1)} %get-tuple-element.135.refs_2_, ...), custom_call_target="tpu_custom_call" | custom-call | flops 99999997952 | bytes 335544320 | tf_op jit(solution)/shard_map/feed_out_partner/pallas_call | solution.py:61
  435.4 24.0 %all-reduce.6.cloned.1.call-done.refs_1_.refs_3_ = bf16[256,3072]{1,0:T(8,128)(2,1)} async-done(((bf16[256,3072]{1,0:T(8,128)(2,1)}), bf16[256,3072]{1,0:T(8,128)(2,1)}) %all-reduce.6.cloned.1.call-update) | async-done | bytes 1572880 | tf_op jit(solution)/shard_map/psum | solution.py:1126
  460.6 3.3 pairs_sum.1.refs_1_
  467.5 10.0 %feed_out.1.refs_3_ = bf16[1024,1024]{1,0:T(8,128)(2,1)} custom-call(bf16[2048,1024]{1,0:T(8,128)(2,1)} %get-tuple-element.125.refs_1_.refs_2_.refs_3_.refs_4_.refs_8_.refs_0_, bf16[2048,1024]{1,0:T(8,128)(2,1)} %get-tuple-element.134.refs_3_.refs_1_.refs_2_.refs_4_, bf16[1024,1024]{1,0:T(8,128)(2,1)} %get-tuple-element.135.refs_2_, ...), custom_call_target="tpu_custom_call" | custom-call | flops 99999997952 | bytes 335544320 | tf_op jit(solution)/shard_map/feed_out/pallas_call | solution.py:61
  477.5 23.5 %collective-permute-done.36.refs_2_.refs_4_ = bf16[256,3072]{1,0:T(8,128)(2,1)S(1)} collective-permute-done((bf16[256,3072]{1,0:T(8,128)(2,1)S(1)}, bf16[256,3072]{1,0:T(8,128)(2,1)S(1)}, u32[]{:S(2)}, u32[]{:S(2)}) %collective-permute-start.36) | collective-permute-done | bytes 1572896 | tf_op jit(solution)/shard_map/ppermute | solution.py:983
  502.2 4.0 sort_rows.3
  506.2 10.7 %all-reduce.8.cloned.1.call-done.refs_2_ = bf16[128,3712]{1,0:T(8,128)(2,1)} async-done(((bf16[128,3712]{1,0:T(8,128)(2,1)}), bf16[128,3712]{1,0:T(8,128)(2,1)}) %all-reduce.8.cloned.1.call-update) | async-done | bytes 950288 | tf_op jit(solution)/shard_map/psum | solution.py:1149
  520.0 4.5 settle_down.1.refs_8_
  525.4 8.5 %spread.1 = (f32[256,4096]{1,0:T(8,128)}, f32[256,4096]{1,0:T(8,128)}, f32[256,1]{1,0:T(8,128)}) custom-call(s32[44]{0:T(128)} %stack.129.refs_0_, f32[256,1]{1,0:T(8,128)} %copy.37.refs_1_, bf16[256,4096]{1,0:T(8,128)(2,1)} %refs_2_.3, bf16[256,4096]{1,0:T(8,128)(2,1)} %refs_3_.11, bf16[256,2048]{1,0:T(8,128)(2,1)} %get-tuple-element.168.refs_3_.refs_4_, ...), custom_call_target="tpu_custom_call" | custom-call | flops 20000000 | bytes 335544320 | tf_op jit(solution)/shard_map/spread/pallas_call | solution.py:61
  534.0 6.1 %collective-permute-done.34.refs_3_ = bf16[128,3712]{1,0:T(8,128)(2,1)S(1)} collective-permute-done((bf16[128,3712]{1,0:T(8,128)(2,1)}, bf16[128,3712]{1,0:T(8,128)(2,1)S(1)}, u32[]{:S(2)}, u32[]{:S(2)}) %collective-permute-start.34) | collective-permute-done | bytes 950304 | tf_op jit(solution)/shard_map/ppermute | solution.py:983
  541.1 4.8 settle_mixer.1
  (121 shorter events, 57.7 us)
Async XLA Ops:
  14.2 24.2 %collective-permute-start.1 = (bf16[128,3712]{1,0:T(8,128)(2,1)}, bf16[128,3712]{1,0:T(8,128)(2,1)S(1)}, u32[]{:S(2)}, u32[]{:S(2)}) collective-permute-start(bf16[128,3712]{1,0:T(8,128)(2,1)} %get-tuple-element.102), channel_id=1, source_target_pairs={{0,2},{2,0},{1,3},{3,1},{4,6},{6,4},{5,7},{7,5},{8,10},{10,8},{9,1... | collective-permute-start | bytes 2850824 | tf_op jit(solution)/shard_map/ppermute | solution.py:983
  17.2 21.8 %copy-start = (bf16[256,3712]{1,0:T(8,128)(2,1)S(1)}, bf16[256,3712]{1,0:T(8,128)(2,1)}, u32[]{:S(2)}) copy-start(bf16[256,3712]{1,0:T(8,128)(2,1)} %get-tuple-element.101.refs_4_.refs_2_) | copy-start | bytes 5701636
  17.2 45.4 %copy-start.9 = (s32[1,1024]{1,0:T(1,128)S(1)}, s32[1,1024]{1,0:T(1,128)}, u32[]{:S(2)}) copy-start(s32[1,1024]{1,0:T(1,128)} %refs_7_.6) | copy-start | bytes 12292
  38.4 29.5 %copy-start.5 = (bf16[128,3712]{1,0:T(8,128)(2,1)}, bf16[128,3712]{1,0:T(8,128)(2,1)S(1)}, u32[]{:S(2)}) copy-start(bf16[128,3712]{1,0:T(8,128)(2,1)S(1)} %collective-permute-done.1.refs_4_) | copy-start | bytes 2850820
  38.4 25.2 %collective-permute-start.6 = (bf16[512,2048]{1,0:T(8,128)(2,1)}, bf16[512,2048]{1,0:T(8,128)(2,1)}, u32[]{:S(2)}, u32[]{:S(2)}) collective-permute-start(bf16[512,2048]{1,0:T(8,128)(2,1)} %get-tuple-element.107), channel_id=1, source_target_pairs={{0,1},{1,0},{2,3},{3,2},{4,5},{5,4},{6,7},{7,6},{8,9},{9,8},{10,11... | collective-permute-start | bytes 6291464 | tf_op jit(solution)/shard_map/ppermute | solution.py:983
  38.5 31.3 %collective-permute-start.5 = (bf16[1024,1024]{1,0:T(8,128)(2,1)}, bf16[1024,1024]{1,0:T(8,128)(2,1)}, u32[]{:S(2)}, u32[]{:S(2)}) collective-permute-start(bf16[1024,1024]{1,0:T(8,128)(2,1)} %refs_4_.4), channel_id=1, source_target_pairs={{0,1},{1,0},{2,3},{3,2},{4,5},{5,4},{6,7},{7,6},{8,9},{9,8},{10,11... | collective-permute-start | bytes 6291464 | tf_op jit(solution)/shard_map/ppermute | solution.py:983
  39.0 30.7 %collective-permute-start = (bf16[256,3712]{1,0:T(8,128)(2,1)S(1)}, bf16[256,3712]{1,0:T(8,128)(2,1)}, u32[]{:S(2)}, u32[]{:S(2)}) collective-permute-start(bf16[256,3712]{1,0:T(8,128)(2,1)S(1)} %copy-done), channel_id=1, source_target_pairs={{0,1},{1,0},{2,3},{3,2},{4,5},{5,4},{6,7},{7,6},{8,9},{9,8},{10,11... | collective-permute-start | bytes 5701640 | tf_op jit(solution)/shard_map/ppermute | solution.py:983
  39.0 23.6 %collective-permute-start.2 = (bf16[128,3712]{1,0:T(8,128)(2,1)S(1)}, bf16[128,3712]{1,0:T(8,128)(2,1)}, u32[]{:S(2)}, u32[]{:S(2)}) collective-permute-start(bf16[128,3712]{1,0:T(8,128)(2,1)S(1)} %collective-permute-done.1.refs_4_), channel_id=1, source_target_pairs={{0,4},{4,0},{1,5},{5,1},{2,6},{6,2},{3,7},{7,3},{8,12},{12,8},{9,1... | collective-permute-start | bytes 2850824 | tf_op jit(solution)/shard_map/ppermute | solution.py:983
  40.7 29.0 %collective-permute-start.3 = (bf16[128,3712]{1,0:T(8,128)(2,1)S(1)}, bf16[128,3712]{1,0:T(8,128)(2,1)}, u32[]{:S(2)}, u32[]{:S(2)}) collective-permute-start(bf16[128,3712]{1,0:T(8,128)(2,1)S(1)} %collective-permute-done.1.refs_4_), channel_id=1, source_target_pairs={{0,1},{1,0},{2,3},{3,2},{4,5},{5,4},{6,7},{7,6},{8,9},{9,8},{10,11... | collective-permute-start | bytes 2850824 | tf_op jit(solution)/shard_map/ppermute | solution.py:983
  62.5 7.2 %collective-permute-start.4 = (bf16[128,3712]{1,0:T(8,128)(2,1)}, bf16[128,3712]{1,0:T(8,128)(2,1)}, u32[]{:S(2)}, u32[]{:S(2)}) collective-permute-start(bf16[128,3712]{1,0:T(8,128)(2,1)} %collective-permute-done.2.refs_5_), channel_id=1, source_target_pairs={{0,1},{1,0},{2,3},{3,2},{4,5},{5,4},{6,7},{7,6},{8,9},{9,8},{10,11... | collective-permute-start | bytes 2850824 | tf_op jit(solution)/shard_map/ppermute | solution.py:983
  68.0 29.3 %collective-permute-start.7 = (bf16[256,2048]{1,0:T(8,128)(2,1)}, bf16[256,2048]{1,0:T(8,128)(2,1)}, u32[]{:S(2)}, u32[]{:S(2)}) collective-permute-start(bf16[256,2048]{1,0:T(8,128)(2,1)} %get-tuple-element.108.refs_9_), channel_id=1, source_target_pairs={{0,2},{2,0},{1,3},{3,1},{4,6},{6,4},{5,7},{7,5},{8,10},{10,8},{9,1... | collective-permute-start | bytes 3145736 | tf_op jit(solution)/shard_map/ppermute | solution.py:983
  84.0 32.7 %collective-permute-start.8 = (bf16[512,1024]{1,0:T(8,128)(2,1)}, bf16[512,1024]{1,0:T(8,128)(2,1)}, u32[]{:S(2)}, u32[]{:S(2)}) collective-permute-start(bf16[512,1024]{1,0:T(8,128)(2,1)} %get-tuple-element.121), channel_id=1, source_target_pairs={{0,2},{2,0},{1,3},{3,1},{4,6},{6,4},{5,7},{7,5},{8,10},{10,8},{9,1... | collective-permute-start | bytes 3145736 | tf_op jit(solution)/shard_map/ppermute | solution.py:983
  97.2 28.5 %collective-permute-start.10 = (bf16[256,2048]{1,0:T(8,128)(2,1)}, bf16[256,2048]{1,0:T(8,128)(2,1)S(1)}, u32[]{:S(2)}, u32[]{:S(2)}) collective-permute-start(bf16[256,2048]{1,0:T(8,128)(2,1)} %collective-permute-done.7.refs_10_.refs_7_), channel_id=1, source_target_pairs={{0,4},{4,0},{1,5},{5,1},{2,6},{6,2},{3,7},{7,3},{8,12},{12,8},{9,1... | collective-permute-start | bytes 3145736 | tf_op jit(solution)/shard_map/ppermute | solution.py:983
  98.9 53.1 %collective-permute-start.11 = (bf16[256,2048]{1,0:T(8,128)(2,1)}, bf16[256,2048]{1,0:T(8,128)(2,1)}, u32[]{:S(2)}, u32[]{:S(2)}) collective-permute-start(bf16[256,2048]{1,0:T(8,128)(2,1)} %get-tuple-element.127), channel_id=1, source_target_pairs={{0,2},{2,0},{1,3},{3,1},{4,6},{6,4},{5,7},{7,5},{8,10},{10,8},{9,1... | collective-permute-start | bytes 3145736 | tf_op jit(solution)/shard_map/ppermute | solution.py:983
  123.9 4.5 collective-permute-start.9
  123.9 55.7 %collective-permute-start.13 = (bf16[512,1024]{1,0:T(8,128)(2,1)}, bf16[512,1024]{1,0:T(8,128)(2,1)}, u32[]{:S(2)}, u32[]{:S(2)}) collective-permute-start(bf16[512,1024]{1,0:T(8,128)(2,1)} %get-tuple-element.130), channel_id=1, source_target_pairs={{0,2},{2,0},{1,3},{3,1},{4,6},{6,4},{5,7},{7,5},{8,10},{10,8},{9,1... | collective-permute-start | bytes 3145736 | tf_op jit(solution)/shard_map/ppermute | solution.py:983
  152.0 27.6 %collective-permute-start.12 = (bf16[256,2048]{1,0:T(8,128)(2,1)}, bf16[256,2048]{1,0:T(8,128)(2,1)}, u32[]{:S(2)}, u32[]{:S(2)}) collective-permute-start(bf16[256,2048]{1,0:T(8,128)(2,1)} %collective-permute-done.11.refs_7_), channel_id=1, source_target_pairs={{0,4},{4,0},{1,5},{5,1},{2,6},{6,2},{3,7},{7,3},{8,12},{12,8},{9,1... | collective-permute-start | bytes 3145736 | tf_op jit(solution)/shard_map/ppermute | solution.py:983
  163.2 40.0 %collective-permute-start.15 = (bf16[512,1024]{1,0:T(8,128)(2,1)}, bf16[512,1024]{1,0:T(8,128)(2,1)}, u32[]{:S(2)}, u32[]{:S(2)}) collective-permute-start(bf16[512,1024]{1,0:T(8,128)(2,1)} %get-tuple-element.132.refs_10_), channel_id=1, source_target_pairs={{0,4},{4,0},{1,5},{5,1},{2,6},{6,2},{3,7},{7,3},{8,12},{12,8},{9,1... | collective-permute-start | bytes 3145736 | tf_op jit(solution)/shard_map/ppermute | solution.py:983
  177.6 30.4 %collective-permute-start.14 = (bf16[256,2048]{1,0:T(8,128)(2,1)}, bf16[256,2048]{1,0:T(8,128)(2,1)}, u32[]{:S(2)}, u32[]{:S(2)}) collective-permute-start(bf16[256,2048]{1,0:T(8,128)(2,1)} %get-tuple-element.133.refs_11_), channel_id=1, source_target_pairs={{0,2},{2,0},{1,3},{3,1},{4,6},{6,4},{5,7},{7,5},{8,10},{10,8},{9,1... | collective-permute-start | bytes 3145736 | tf_op jit(solution)/shard_map/ppermute | solution.py:983
  179.3 81.9 %collective-permute-start.18 = (bf16[256,2048]{1,0:T(8,128)(2,1)}, bf16[256,2048]{1,0:T(8,128)(2,1)}, u32[]{:S(2)}, u32[]{:S(2)}) collective-permute-start(bf16[256,2048]{1,0:T(8,128)(2,1)} %get-tuple-element.142), channel_id=1, source_target_pairs={{0,2},{2,0},{1,3},{3,1},{4,6},{6,4},{5,7},{7,5},{8,10},{10,8},{9,1... | collective-permute-start | bytes 3145736 | tf_op jit(solution)/shard_map/ppermute | solution.py:983
  206.2 55.4 %collective-permute-start.17 = (bf16[256,1024]{1,0:T(8,128)(2,1)}, bf16[256,1024]{1,0:T(8,128)(2,1)}, u32[]{:S(2)}, u32[]{:S(2)}) collective-permute-start(bf16[256,1024]{1,0:T(8,128)(2,1)} %top_sum.4.refs_3_), channel_id=1, source_target_pairs={{0,2},{2,0},{1,3},{3,1},{4,6},{6,4},{5,7},{7,5},{8,10},{10,8},{9,1... | collective-permute-start | bytes 1572872 | tf_op jit(solution)/shard_map/ppermute | solution.py:983
  211.7 51.6 %collective-permute-start.19 = (bf16[256,2048]{1,0:T(8,128)(2,1)}, bf16[256,2048]{1,0:T(8,128)(2,1)}, u32[]{:S(2)}, u32[]{:S(2)}) collective-permute-start(bf16[256,2048]{1,0:T(8,128)(2,1)} %top_sum.5.refs_4_), channel_id=1, source_target_pairs={{0,4},{4,0},{1,5},{5,1},{2,6},{6,2},{3,7},{7,3},{8,12},{12,8},{9,1... | collective-permute-start | bytes 3145736 | tf_op jit(solution)/shard_map/ppermute | solution.py:983
  227.5 43.1 %collective-permute-start.16 = (bf16[1024,1024]{1,0:T(8,128)(2,1)}, bf16[1024,1024]{1,0:T(8,128)(2,1)}, u32[]{:S(2)}, u32[]{:S(2)}) collective-permute-start(bf16[1024,1024]{1,0:T(8,128)(2,1)} %feed_back_partner.1.refs_7_), channel_id=1, source_target_pairs={{0,1},{1,0},{2,3},{3,2},{4,5},{5,4},{6,7},{7,6},{8,9},{9,8},{10,11... | collective-permute-start | bytes 6291464 | tf_op jit(solution)/shard_map/ppermute | solution.py:983
  236.7 54.3 %collective-permute-start.21 = (bf16[512,1024]{1,0:T(8,128)(2,1)}, bf16[512,1024]{1,0:T(8,128)(2,1)}, u32[]{:S(2)}, u32[]{:S(2)}) collective-permute-start(bf16[512,1024]{1,0:T(8,128)(2,1)} %get-tuple-element.143.refs_10_), channel_id=1, source_target_pairs={{0,4},{4,0},{1,5},{5,1},{2,6},{6,2},{3,7},{7,3},{8,12},{12,8},{9,1... | collective-permute-start | bytes 3145736 | tf_op jit(solution)/shard_map/ppermute | solution.py:983
  261.2 33.2 %collective-permute-start.20 = (bf16[256,2048]{1,0:T(8,128)(2,1)}, bf16[256,2048]{1,0:T(8,128)(2,1)}, u32[]{:S(2)}, u32[]{:S(2)}) collective-permute-start(bf16[256,2048]{1,0:T(8,128)(2,1)} %get-tuple-element.144.refs_7_), channel_id=1, source_target_pairs={{0,2},{2,0},{1,3},{3,1},{4,6},{6,4},{5,7},{7,5},{8,10},{10,8},{9,1... | collective-permute-start | bytes 3145736 | tf_op jit(solution)/shard_map/ppermute | solution.py:983
  261.6 88.6 %collective-permute-start.23 = (bf16[256,2048]{1,0:T(8,128)(2,1)}, bf16[256,2048]{1,0:T(8,128)(2,1)}, u32[]{:S(2)}, u32[]{:S(2)}) collective-permute-start(bf16[256,2048]{1,0:T(8,128)(2,1)} %get-tuple-element.157), channel_id=1, source_target_pairs={{0,2},{2,0},{1,3},{3,1},{4,6},{6,4},{5,7},{7,5},{8,10},{10,8},{9,1... | collective-permute-start | bytes 3145736 | tf_op jit(solution)/shard_map/ppermute | solution.py:983
  269.9 79.0 %all-reduce.4.cloned.1.call-start = ((), (), s32[]{:S(2)}) async-start(), calls=%async_computation | async-start | bytes 3145728 | tf_op jit(solution)/shard_map/psum | solution.py:1102
  294.1 56.1 %collective-permute-start.22 = (bf16[256,1024]{1,0:T(8,128)(2,1)}, bf16[256,1024]{1,0:T(8,128)(2,1)}, u32[]{:S(2)}, u32[]{:S(2)}) collective-permute-start(bf16[256,1024]{1,0:T(8,128)(2,1)} %top_sum.6.refs_3_), channel_id=1, source_target_pairs={{0,2},{2,0},{1,3},{3,1},{4,6},{6,4},{5,7},{7,5},{8,10},{10,8},{9,1... | collective-permute-start | bytes 1572872 | tf_op jit(solution)/shard_map/ppermute | solution.py:983
  298.2 52.0 %collective-permute-start.24 = (bf16[256,2048]{1,0:T(8,128)(2,1)}, bf16[256,2048]{1,0:T(8,128)(2,1)}, u32[]{:S(2)}, u32[]{:S(2)}) collective-permute-start(bf16[256,2048]{1,0:T(8,128)(2,1)} %top_sum.7.refs_5_), channel_id=1, source_target_pairs={{0,4},{4,0},{1,5},{5,1},{2,6},{6,2},{3,7},{7,3},{8,12},{12,8},{9,1... | collective-permute-start | bytes 3145736 | tf_op jit(solution)/shard_map/ppermute | solution.py:983
  321.2 21.5 %collective-permute-start.25 = (bf16[512,2048]{1,0:T(8,128)(2,1)}, bf16[512,2048]{1,0:T(8,128)(2,1)}, u32[]{:S(2)}, u32[]{:S(2)}) collective-permute-start(bf16[512,2048]{1,0:T(8,128)(2,1)} %get-tuple-element.154.refs_9_), channel_id=1, source_target_pairs={{0,1},{1,0},{2,3},{3,2},{4,5},{5,4},{6,7},{7,6},{8,9},{9,8},{10,11... | collective-permute-start | bytes 6291464 | tf_op jit(solution)/shard_map/ppermute | solution.py:983
  321.2 21.4 %collective-permute-start.26 = (bf16[1024,128]{1,0:T(8,128)(2,1)}, bf16[1024,128]{1,0:T(8,128)(2,1)}, u32[]{:S(2)}, u32[]{:S(2)}) collective-permute-start(bf16[1024,128]{1,0:T(8,128)(2,1)} %get-tuple-element.159.refs_3_), channel_id=1, source_target_pairs={{0,1},{1,0},{2,3},{3,2},{4,5},{5,4},{6,7},{7,6},{8,9},{9,8},{10,11... | collective-permute-start | bytes 786440 | tf_op jit(solution)/shard_map/ppermute | solution.py:983
  347.5 30.5 %collective-permute-start.27 = (bf16[256,2176]{1,0:T(8,128)(2,1)}, bf16[256,2176]{1,0:T(8,128)(2,1)}, u32[]{:S(2)}, u32[]{:S(2)}) collective-permute-start(bf16[256,2176]{1,0:T(8,128)(2,1)} %get-tuple-element.160.refs_2_), channel_id=1, source_target_pairs={{0,2},{2,0},{1,3},{3,1},{4,6},{6,4},{5,7},{7,5},{8,10},{10,8},{9,1... | collective-permute-start | bytes 3342344 | tf_op jit(solution)/shard_map/ppermute | solution.py:983
  356.8 102.6 %all-reduce.6.cloned.1.call-start = ((), (), s32[]{:S(2)}) async-start(), calls=%async_computation.1 | async-start | bytes 3145728 | tf_op jit(solution)/shard_map/psum | solution.py:1126
  356.8 36.6 %collective-permute-start.29 = (bf16[256,3072]{1,0:T(8,128)(2,1)}, bf16[256,3072]{1,0:T(8,128)(2,1)}, u32[]{:S(2)}, u32[]{:S(2)}) collective-permute-start(bf16[256,3072]{1,0:T(8,128)(2,1)} %all-reduce.4.cloned.1.call-done.refs_1_), channel_id=1, source_target_pairs={{0,4},{4,0},{1,5},{5,1},{2,6},{6,2},{3,7},{7,3},{8,12},{12,8},{9,1... | collective-permute-start | bytes 4718600 | tf_op jit(solution)/shard_map/ppermute | solution.py:983
  389.4 8.2 %collective-permute-start.28 = (bf16[512,1536]{1,0:T(8,128)(2,1)}, bf16[512,1536]{1,0:T(8,128)(2,1)S(1)}, u32[]{:S(2)}, u32[]{:S(2)}) collective-permute-start(bf16[512,1536]{1,0:T(8,128)(2,1)} %get-tuple-element.166.refs_3_), channel_id=1, source_target_pairs={{0,1},{1,0},{2,3},{3,2},{4,5},{5,4},{6,7},{7,6},{8,9},{9,8},{10,11... | collective-permute-start | bytes 4718600 | tf_op jit(solution)/shard_map/ppermute | solution.py:983
  389.4 71.2 %collective-permute-start.32 = (bf16[128,2176]{1,0:T(8,128)(2,1)}, bf16[128,2176]{1,0:T(8,128)(2,1)}, u32[]{:S(2)}, u32[]{:S(2)}) collective-permute-start(bf16[128,2176]{1,0:T(8,128)(2,1)} %get-tuple-element.173), channel_id=1, source_target_pairs={{0,4},{4,0},{1,5},{5,1},{2,6},{6,2},{3,7},{7,3},{8,12},{12,8},{9,1... | collective-permute-start | bytes 1671176 | tf_op jit(solution)/shard_map/ppermute | solution.py:983
  397.6 126.9 %collective-permute-start.35 = (bf16[256,2048]{1,0:T(8,128)(2,1)}, bf16[256,2048]{1,0:T(8,128)(2,1)}, u32[]{:S(2)}, u32[]{:S(2)}) collective-permute-start(bf16[256,2048]{1,0:T(8,128)(2,1)} %get-tuple-element.175), channel_id=1, source_target_pairs={{0,1},{1,0},{2,3},{3,2},{4,5},{5,4},{6,7},{7,6},{8,9},{9,8},{10,11... | collective-permute-start | bytes 3145736 | tf_op jit(solution)/shard_map/ppermute | solution.py:983
  402.6 20.2 %collective-permute-start.30 = (bf16[256,1536]{1,0:T(8,128)(2,1)}, bf16[256,1536]{1,0:T(8,128)(2,1)S(1)}, u32[]{:S(2)}, u32[]{:S(2)}) collective-permute-start(bf16[256,1536]{1,0:T(8,128)(2,1)} %get-tuple-element.170.refs_7_), channel_id=1, source_target_pairs={{0,2},{2,0},{1,3},{3,1},{4,6},{6,4},{5,7},{7,5},{8,10},{10,8},{9,1... | collective-permute-start | bytes 2359304 | tf_op jit(solution)/shard_map/ppermute | solution.py:983
  435.4 32.2 %collective-permute-start.31 = (bf16[1024,1024]{1,0:T(8,128)(2,1)}, bf16[1024,1024]{1,0:T(8,128)(2,1)}, u32[]{:S(2)}, u32[]{:S(2)}) collective-permute-start(bf16[1024,1024]{1,0:T(8,128)(2,1)} %feed_out_partner.1.refs_2_), channel_id=1, source_target_pairs={{0,1},{1,0},{2,3},{3,2},{4,5},{5,4},{6,7},{7,6},{8,9},{9,8},{10,11... | collective-permute-start | bytes 6291464 | tf_op jit(solution)/shard_map/ppermute | solution.py:983
  435.4 25.2 %collective-permute-start.33 = (bf16[128,1536]{1,0:T(8,128)(2,1)}, bf16[128,1536]{1,0:T(8,128)(2,1)}, u32[]{:S(2)}, u32[]{:S(2)}) collective-permute-start(bf16[128,1536]{1,0:T(8,128)(2,1)} %get-tuple-element.174), channel_id=1, source_target_pairs={{0,4},{4,0},{1,5},{5,1},{2,6},{6,2},{3,7},{7,3},{8,12},{12,8},{9,1... | collective-permute-start | bytes 1179656 | tf_op jit(solution)/shard_map/ppermute | solution.py:983
  463.9 2.1 copy-start.1
  465.3 51.7 %all-reduce.8.cloned.1.call-start = ((), (), s32[]{:S(2)}) async-start(), calls=%async_computation.2 | async-start | bytes 1900544 | tf_op jit(solution)/shard_map/psum | solution.py:1149
  466.0 35.1 %collective-permute-start.36 = (bf16[256,3072]{1,0:T(8,128)(2,1)S(1)}, bf16[256,3072]{1,0:T(8,128)(2,1)S(1)}, u32[]{:S(2)}, u32[]{:S(2)}) collective-permute-start(bf16[256,3072]{1,0:T(8,128)(2,1)S(1)} %copy-done.1), channel_id=1, source_target_pairs={{0,4},{4,0},{1,5},{5,1},{2,6},{6,2},{3,7},{7,3},{8,12},{12,8},{9,1... | collective-permute-start | bytes 4718600 | tf_op jit(solution)/shard_map/ppermute | solution.py:983
  477.5 40.9 %copy-start.11 = (bf16[256]{0:T(256)(128)(2,1)S(1)}, bf16[256]{0:T(256)(128)(2,1)}, u32[]{:S(2)}) copy-start(bf16[256]{0:T(256)(128)(2,1)} %param.16) | copy-start | bytes 1540
  477.5 40.9 %copy-start.12 = (bf16[256]{0:T(256)(128)(2,1)S(1)}, bf16[256]{0:T(256)(128)(2,1)}, u32[]{:S(2)}) copy-start(bf16[256]{0:T(256)(128)(2,1)} %param.23) | copy-start | bytes 1540
  506.2 18.2 %collective-permute-start.37 = (bf16[256,2048]{1,0:T(8,128)(2,1)}, bf16[256,2048]{1,0:T(8,128)(2,1)S(1)}, u32[]{:S(2)}, u32[]{:S(2)}) collective-permute-start(bf16[256,2048]{1,0:T(8,128)(2,1)} %get-tuple-element.178), channel_id=1, source_target_pairs={{0,1},{1,0},{2,3},{3,2},{4,5},{5,4},{6,7},{7,6},{8,9},{9,8},{10,11... | collective-permute-start | bytes 3145736 | tf_op jit(solution)/shard_map/ppermute | solution.py:983
  516.9 23.2 %collective-permute-start.34 = (bf16[128,3712]{1,0:T(8,128)(2,1)}, bf16[128,3712]{1,0:T(8,128)(2,1)S(1)}, u32[]{:S(2)}, u32[]{:S(2)}) collective-permute-start(bf16[128,3712]{1,0:T(8,128)(2,1)} %all-reduce.8.cloned.1.call-done.refs_2_), channel_id=1, source_target_pairs={{0,4},{4,0},{1,5},{5,1},{2,6},{6,2},{3,7},{7,3},{8,12},{12,8},{9,1... | collective-permute-start | bytes 2850824 | tf_op jit(solution)/shard_map/ppermute | solution.py:983
  534.0 14.8 %copy-start.8 = (f32[256,1]{1,0:T(8,128)S(1)}, f32[256,1]{1,0:T(8,128)}, u32[]{:S(2)}) copy-start(f32[256,1]{1,0:T(8,128)} %get-tuple-element.187) | copy-start | bytes 3076
  (6 other events, 6.1 us)
Sparse Core Ops, SparseCore 0:
  273.1 69.4 all-reduce.3
  389.5 69.7 all-reduce.5
  469.0 47.8 all-reduce.7
